TPU v7x, 512 devices: a whole 4x4x16 slice. The times are simulated.
512 devices in a mesh: blk: 64 (over x, z_lo, core), tp: 8 (over z_hi, y).
Axes of the slice: x: 4, y: 4, z: 16 (z_hi: 2, z_lo: 8; z = z_hi * 8 + z_lo), core: 2. Of those that a mesh axis runs over, the one named last changes fastest.
Arguments:
- weights: float32 [64, 1024, 1024], P('blk', None, 'tp'), may hold values from -6 to 6
- copies: bfloat16 [64, 1024, 1024], P('blk', None, 'tp'), may hold values from -60 to 60
- copies_mixed: bfloat16 [64, 1024, 1024], P('blk', None, 'tp'), may hold values from -64 to 64
- tracker: bfloat16 [64, 1024, 1024], P('blk', None, 'tp'), may hold values from -6 to 6
- tracker_copy: bfloat16 [64, 1024, 1024], P('blk', None, 'tp'), may hold values from -6 to 6
- tracker_mixed: bfloat16 [64, 1024, 1024], P('blk', None, 'tp'), may hold values from -6 to 6
- grad_prev: bfloat16 [64, 1024, 1024], P('blk', None, 'tp'), may hold values from -3 to 3
- tokens: bfloat16 [64, 1024, 1024], P('blk', 'tp'), may hold values from -12 to 12
- image_ids: int32 [64, 1024], P('blk'), may hold values from 0 to 5, never falling along the last dimension, each value on 1 to 197 neighbouring positions
- key_weight: bfloat16 [1024, 1024], P(None, 'tp'), may hold values from -0.1875 to 0.1875
- value_weight: bfloat16 [1024, 1024], P(None, 'tp'), may hold values from -0.1875 to 0.1875
- out_grad: bfloat16 [64, 1024, 1024], P('blk', None, 'tp'), may hold values from -48 to 48
- row_picks: int32 [64, 2, 64], replicated, may hold values from 0 to 1023, as said below
Outputs:
- weights_new: float32 [64, 1024, 1024], P('blk', None, 'tp')
- copies_new: bfloat16 [64, 1024, 1024], P('blk', None, 'tp')
- mixed_new: bfloat16 [64, 1024, 1024], P('blk', None, 'tp')
- tracker_new: bfloat16 [64, 1024, 1024], P('blk', None, 'tp')
- tracker_copy_new: bfloat16 [64, 1024, 1024], P('blk', None, 'tp')
- tracker_mixed_new: bfloat16 [64, 1024, 1024], P('blk', None, 'tp')
- grad_new: bfloat16 [64, 1024, 1024], P('blk', None, 'tp')
- consensus: float32 [], replicated
Inputs may be any that keep to these rules, and one draw needn't show every extreme that they name: `image_ids`: never falling along a replica's tokens; an image holds 1 to 197 tokens. `row_picks`: each row lists 64 different rows; the same picks serve every head shard of a replica.
All inputs are finite; a program needn't handle non-finite values.
Results may differ from a plain program's by a relative error of at most 0.0095.
The roundings to bfloat16 on the way count: a program that leaves them out, or rounds other values in their place, can miss the bound.
Values may be sent and summed in bfloat16 or wider, within the bound.
No kernel may reach another device: no remote copies, remote signals or barrier semaphores. Data moves between devices by JAX's collectives and lax.ppermute only.
A program may use at most 64 MiB of HBM per device.

v0:
```python
import jax
import jax.numpy as jnp
from jax import lax
from jax.sharding import Mesh
from jax.sharding import PartitionSpec as P

HD = 64
BLK = ("blk_0", "blk_1", "blk_2")
BLK_TP = ("blk_0", "blk_1", "blk_2", "tp_0", "tp_1")
TP = ("tp_0", "tp_1")


mixing_rate = 0.2
step_rate = 0.5


def over_axes(value, axes):
    for axis in axes:
        value = lax.psum(value, axis)
    return value


def extended(value, sides, width):
    for axis, dim in sides:
        size, length = (lax.axis_size(axis), value.shape[dim])
        up = [(i, (i + 1) % size) for i in range(size)]
        down = [(j, i) for i, j in up]
        last = lax.slice_in_dim(value, length - width, length, axis=dim)
        leading = lax.slice_in_dim(value, 0, width, axis=dim)
        before = lax.ppermute(last, axis, up)
        after = lax.ppermute(leading, axis, down)
        value = jnp.concatenate([before, value, after], axis=dim)
    return value


def contract(left, right, left_dim, right_dim):
    return lax.dot_general(
        left, right, (((left_dim,), (right_dim,)), ((), ())), preferred_element_type=jnp.float32
    )


def pick_matrix(picks, total_rows):
    columns = lax.broadcasted_iota(jnp.int32, (picks.shape[0], total_rows), 1)
    return (picks[:, None] == columns).astype(jnp.float32)


def select_rows(picks, field):
    return jnp.dot(pick_matrix(picks, field.shape[0]), field, precision=lax.Precision.HIGHEST)


def place_rows(picks, values, total_rows):
    matrix = pick_matrix(picks, total_rows)
    return lax.dot_general(
        matrix, values, (((0,), (0,)), ((), ())), precision=lax.Precision.HIGHEST
    )


def neighbour_picks(row_picks, stream):
    replica_count = lax.axis_size(BLK)
    replica_rank = lax.axis_index(BLK)
    lower_picks = lax.dynamic_index_in_dim(
        row_picks, (replica_rank - 1 + replica_count) % replica_count, 0, keepdims=False
    )[stream]
    own_picks = lax.dynamic_index_in_dim(row_picks, replica_rank, 0, keepdims=False)[stream]
    upper_picks = lax.dynamic_index_in_dim(
        row_picks, (replica_rank + 1) % replica_count, 0, keepdims=False
    )[stream]
    return jnp.concatenate([lower_picks, own_picks, upper_picks], axis=0)


def mix_stream(received, row_picks, stream, total_rows):
    picks = neighbour_picks(row_picks, stream)
    values = received.reshape(received.shape[0] * received.shape[1], received.shape[2])
    return place_rows(picks, values, total_rows) / 3.0


def consensus_of(mixed_new, copies_new):
    gap_value = mixed_new.astype(jnp.float32) - copies_new.astype(jnp.float32)
    local_sum = jnp.sum(gap_value * gap_value)
    total_sum = over_axes(local_sum, BLK_TP)
    count = lax.axis_size(BLK) * copies_new.shape[0] * copies_new.shape[0]
    return total_sum / float(count)


def head_grad(query_head, key_head, value_head, out_head, same_image):
    scores = contract(query_head, key_head, 1, 1) * HD ** (-0.5)
    scores = jnp.where(same_image, scores, -1e30)
    row_max = jnp.max(scores, axis=-1, keepdims=True)
    exponent = jnp.exp(scores - row_max)
    attention = exponent / jnp.sum(exponent, axis=-1, keepdims=True)
    out_proj = contract(out_head, value_head, 1, 1)
    centred = out_proj - jnp.sum(attention * out_proj, axis=-1, keepdims=True)
    score_grad = (attention * centred * HD ** (-0.5)).astype(jnp.bfloat16)
    return jnp.dot(score_grad, key_head, preferred_element_type=jnp.float32).astype(jnp.bfloat16)


def attention_grad(projected, image_row, out_rows):
    width = out_rows.shape[1]
    queries = projected[:, :width]
    keyed = projected[:, width : 2 * width]
    valued = projected[:, 2 * width :]
    same_image = image_row[:, None] == image_row[None, :]
    pieces_list = []
    for head_index in range(width // HD):
        low_col = head_index * HD
        pieces_list.append(
            head_grad(
                queries[:, low_col : low_col + HD],
                keyed[:, low_col : low_col + HD],
                valued[:, low_col : low_col + HD],
                out_rows[:, low_col : low_col + HD],
                same_image,
            )
        )
    return jnp.concatenate(pieces_list, axis=1)


def local_gradient(weights_new, tokens, image_ids, key_weight, value_weight, out_grad):
    model_width = weights_new.shape[0]
    query_weight = (weights_new * model_width ** (-0.5)).astype(jnp.bfloat16)
    joined = jnp.concatenate([query_weight, key_weight, value_weight], axis=1)
    gathered = lax.all_gather(tokens, TP, axis=1, tiled=True)
    projected = jnp.dot(gathered[0], joined, preferred_element_type=jnp.float32).astype(
        jnp.bfloat16
    )[None][0]
    query_grad = attention_grad(projected, image_ids[0], out_grad[0])
    total = contract(gathered[0], query_grad, 0, 0)
    return (total * model_width ** (-0.5)).astype(jnp.bfloat16)


def per_device(
    weights,
    copies,
    copies_mixed,
    tracker,
    tracker_copy,
    tracker_mixed,
    grad_prev,
    tokens,
    image_ids,
    key_weight,
    value_weight,
    out_grad,
    row_picks,
):
    model_width = weights.shape[1]
    replica_rank = lax.axis_index(BLK)
    own_picks = lax.dynamic_index_in_dim(row_picks, replica_rank, 0, keepdims=False)
    copy_value = copies[0].astype(jnp.float32)
    mixed_value = copies_mixed[0].astype(jnp.float32)
    weights_new = (
        weights[0]
        + mixing_rate * (mixed_value - copy_value)
        - step_rate * tracker[0].astype(jnp.float32)
    )
    param_values = select_rows(own_picks[0], weights_new - copy_value)
    copies_new = (copy_value + place_rows(own_picks[0], param_values, model_width)).astype(
        jnp.bfloat16
    )
    param_received = extended(param_values[None].astype(jnp.bfloat16), ((BLK, 0),), 1).astype(
        jnp.float32
    )
    mixed_new = (mixed_value + mix_stream(param_received, row_picks, 0, model_width)).astype(
        jnp.bfloat16
    )
    consensus = consensus_of(mixed_new, copies_new)
    grad_new = local_gradient(weights_new, tokens, image_ids, key_weight, value_weight, out_grad)
    tracker_copy_value = tracker_copy[0].astype(jnp.float32)
    tracker_mixed_value = tracker_mixed[0].astype(jnp.float32)
    tracker_new = (
        tracker[0].astype(jnp.float32)
        + mixing_rate * (tracker_mixed_value - tracker_copy_value)
        + grad_new.astype(jnp.float32)
        - grad_prev[0].astype(jnp.float32)
    ).astype(jnp.bfloat16)
    tracker_values = select_rows(own_picks[1], tracker_new.astype(jnp.float32) - tracker_copy_value)
    tracker_copy_new = (
        tracker_copy_value + place_rows(own_picks[1], tracker_values, model_width)
    ).astype(jnp.bfloat16)
    tracker_received = extended(tracker_values[None], ((BLK, 0),), 1)
    tracker_mixed_new = (
        tracker_mixed_value + mix_stream(tracker_received, row_picks, 1, model_width)
    ).astype(jnp.bfloat16)
    return (
        weights_new[None],
        copies_new[None],
        mixed_new[None],
        tracker_new[None],
        tracker_copy_new[None],
        tracker_mixed_new[None],
        grad_new[None],
        consensus,
    )


def solution(mesh):
    finer = Mesh(mesh.devices.reshape(4, 8, 2, 2, 4), ("blk_0", "blk_1", "blk_2", "tp_0", "tp_1"))
    in_specs = (
        P(BLK, None, TP),
        P(BLK, None, TP),
        P(BLK, None, TP),
        P(BLK, None, TP),
        P(BLK, None, TP),
        P(BLK, None, TP),
        P(BLK, None, TP),
        P(BLK, TP, None),
        P(BLK, None),
        P(None, TP),
        P(None, TP),
        P(BLK, None, TP),
        P(),
    )
    out_specs = (
        P(BLK, None, TP),
        P(BLK, None, TP),
        P(BLK, None, TP),
        P(BLK, None, TP),
        P(BLK, None, TP),
        P(BLK, None, TP),
        P(BLK, None, TP),
        P(),
    )
    return jax.shard_map(
        per_device, mesh=finer, in_specs=in_specs, out_specs=out_specs, check_vma=False
    )
```

profile of v0, /device:TPU:8, one launch (start us, length us, event | category | flops | bytes accessed | tf_op | source)
XLA Modules:
  0.0 177.8 jit_solution(13009544344436294952)
XLA Ops:
  7.2 0.0 copy-start
  7.2 0.0 copy-start.3
  7.2 0.0 copy-start.4
  7.2 0.0 copy-start.1
  7.2 0.0 all-gather.2.cloned.1.call-start
  7.3 0.7 all-gather.2.cloned.1.call-update
  8.0 0.7 constant_dynamic-slice_fusion.1
  8.7 1.8 fusion.64
  10.5 1.9 %collective-permute-start = (bf16[1,64,128]{2,1,0:T(8,128)(2,1)S(1)}, bf16[1,64,128]{2,1,0:T(8,128)(2,1)S(1)}, u32[]{:S(2)}, u32[]{:S(2)}) collective-permute-start(bf16[1,64,128]{2,1,0:T(8,128)(2,1)S(1)} %convert_bitcast_fusion.3), channel_id=1, source_target_pairs={{0,8},{8,16},{16,24},{24,32},{32,40},{40,48},{48,56},{56,64},{64,7... | collective-permute-start | bytes 49160 | tf_op jit(solution)/shard_map/ppermute | solution.py:30
  12.4 14.8 %collective-permute-start.1 = (bf16[1,64,128]{2,1,0:T(8,128)(2,1)S(1)}, bf16[1,64,128]{2,1,0:T(8,128)(2,1)S(1)}, u32[]{:S(2)}, u32[]{:S(2)}) collective-permute-start(bf16[1,64,128]{2,1,0:T(8,128)(2,1)S(1)} %convert_bitcast_fusion.3), channel_id=1, source_target_pairs={{8,0},{16,8},{24,16},{32,24},{40,32},{48,40},{56,48},{64,56},{72,6... | collective-permute-start | bytes 49160 | tf_op jit(solution)/shard_map/ppermute | solution.py:31
  27.3 0.1 pad_add_fusion
  27.3 0.0 collective-permute-done
  27.3 1.3 collective-permute-done.1
  28.7 1.5 fusion.38
  30.2 0.0 copy-start.13
  30.2 3.0 %multiply_reduce_fusion = (f32[]{:T(128)}, bf16[1024,128]{1,0:T(8,128)(2,1)}) fusion(bf16[1024,128]{1,0:T(8,128)(2,1)S(1)} %fusion.38, f32[64,128]{1,0:T(8,128)S(1)} %fusion.64, s32[64]{0:T(128)S(1)} %get-tuple-element.22, bf16[1,1024,128]{2,1,0:T(8,128)(2,1)} %param.14), kind=kOutput, calls=%fused_computation.80 | convolution fusion | flops 101777408 | bytes 819460 | tf_op jit(solution)/shard_map/dot_general | solution.py:53
  33.2 9.2 %psum.35 = f32[]{:T(128)} all-reduce(f32[]{:T(128)} %get-tuple-element.27), channel_id=1, replica_groups=mesh['blk_0'=4,'blk_1'=8,'blk_2'=2,'tp_0'=2,'tp_1'=4] {'blk_0'}, use_global_device_ids=true, to_apply=%region_7.8 | all-reduce | flops 1 | bytes 8 | tf_op jit(solution)/shard_map/psum | solution.py:19
  42.4 27.7 %psum.36 = f32[]{:T(128)} all-reduce(f32[]{:T(128)} %psum.35), channel_id=1, replica_groups=mesh['blk_0'=4,'blk_1'=8,'blk_2'=2,'tp_0'=2,'tp_1'=4] {'blk_1'}, use_global_device_ids=true, to_apply=%region_8.9 | all-reduce | flops 1 | bytes 8 | tf_op jit(solution)/shard_map/psum | solution.py:19
  70.1 2.3 %fusion.68 = f32[1,1024,128]{2,1,0:T(8,128)} fusion(f32[1,1024,128]{2,1,0:T(8,128)} %param.13, bf16[1,1024,128]{2,1,0:T(8,128)(2,1)} %param.14, bf16[1,1024,128]{2,1,0:T(8,128)(2,1)} %param.15, bf16[1,1024,128]{2,1,0:T(8,128)(2,1)} %param.16), kind=kLoop, calls=%fused_computation.74 | loop fusion | flops 1048576 | bytes 1835008 | tf_op jit(solution)/shard_map/sub | solution.py:152
  72.4 5.8 %psum.37 = f32[]{:T(128)} all-reduce(f32[]{:T(128)} %psum.36), channel_id=1, replica_groups=mesh['blk_0'=4,'blk_1'=8,'blk_2'=2,'tp_0'=2,'tp_1'=4] {'blk_2'}, use_global_device_ids=true, to_apply=%region_9.10 | all-reduce | flops 1 | bytes 8 | tf_op jit(solution)/shard_map/psum | solution.py:19
  78.2 0.2 multiply_convert_fusion
  78.4 25.9 %psum.38 = f32[]{:T(128)} all-reduce(f32[]{:T(128)} %psum.37), channel_id=1, replica_groups=mesh['blk_0'=4,'blk_1'=8,'blk_2'=2,'tp_0'=2,'tp_1'=4] {'tp_0'}, use_global_device_ids=true, to_apply=%region_10.11 | all-reduce | flops 1 | bytes 8 | tf_op jit(solution)/shard_map/psum | solution.py:19
  104.3 0.1 pad_add_fusion.1
  104.4 9.3 %psum.39 = f32[]{:T(128)} all-reduce(f32[]{:T(128)} %psum.38), channel_id=1, replica_groups=mesh['blk_0'=4,'blk_1'=8,'blk_2'=2,'tp_0'=2,'tp_1'=4] {'tp_1'}, use_global_device_ids=true, to_apply=%region_11.12 | all-reduce | flops 1 | bytes 8 | tf_op jit(solution)/shard_map/psum | solution.py:19
  114.3 0.0 copy-start.7
  114.3 21.1 %all-gather.2.cloned.1.call-done = bf16[1,1024,1024]{2,1,0:T(8,128)(2,1)} async-done(((bf16[1,128,1024]{2,1,0:T(8,128)(2,1)}), bf16[1,1024,1024]{2,1,0:T(8,128)(2,1)}) %all-gather.2.cloned.1.call-update) | async-done | bytes 2097168 | tf_op jit(solution)/shard_map/all_gather | solution.py:122
  135.4 0.0 copy-done.11
  135.4 2.6 %fusion.29 = bf16[1024,384]{0,1:T(8,128)(2,1)S(1)} fusion(bf16[1,1024,1024]{2,1,0:T(8,128)(2,1)} %all-gather.2.cloned.1.call-done, bf16[1024,128]{1,0:T(8,128)(2,1)S(1)} %copy-done.11, bf16[1024,128]{1,0:T(8,128)(2,1)S(1)} %copy-done.12, bf16[1024,128]{1,0:T(8,128)(2,1)S(1)} %multiply_convert_fusion), kind=kOutput, calls=%fused_computation.33 | convolution fusion | flops 808058880 | bytes 3670016 | tf_op jit(solution)/shard_map/dot_general | solution.py:123
  138.0 0.0 copy-start.10
  138.0 0.8 fusion.86
  138.8 0.8 fusion.77
  139.6 0.0 copy-done.10
  139.6 1.3 fusion.12
  140.8 2.4 %fusion.9 = (f32[1024]{0:T(1024)S(1)}, f32[1024]{0:T(1024)S(1)}) fusion(f32[1024,1024]{0,1:T(8,128)S(1)} %get-tuple-element.23, f32[1024]{0:T(1024)S(1)} %get-tuple-element.12, s32[1024]{0:T(1024)S(1)} %bitcast.167, f32[1024]{0:T(1024)S(1)} %get-tuple-element.13, f32[1024,1024]{0,1:T(8,128)S(1)} %fusion.86), kind=kLoop, calls=%fused_computation.17 | loop fusion | flops 9435136 | bytes 8409088 | tf_op jit(solution)/shard_map/reduce_sum | solution.py:90
  143.3 2.7 %fusion.4 = (f32[1024]{0:T(1024)S(1)}, f32[1024]{0:T(1024)S(1)}, f32[1024,1024]{1,0:T(8,128)S(1)}) fusion(f32[1024]{0:T(1024)S(1)} %get-tuple-element.10, f32[1024]{0:T(1024)S(1)} %get-tuple-element.12, f32[1024,1024]{0,1:T(8,128)S(1)} %get-tuple-element.23, s32[1024]{0:T(1024)S(1)} %bitcast.168, f32[1024,1024]{1,0:T(8,128)S(1)} %fusion.77, ...), kind=kOutput, calls=%fused_computation.10 | convolution fusion | flops 147847168 | bytes 17203200 | tf_op jit(solution)/shard_map/dot_general | solution.py:37
  146.0 1.9 %fusion.41 = bf16[1024,64]{1,0:T(8,128)(2,1)S(1)} fusion(f32[1024,1024]{1,0:T(8,128)S(1)} %fusion.77, f32[1024]{0:T(1024)S(1)} %get-tuple-element.9, bf16[1024,384]{0,1:T(8,128)(2,1)S(1)} %fusion.29, f32[1024,1024]{0,1:T(8,128)S(1)} %fusion.86, f32[1024]{0:T(1024)S(1)} %get-tuple-element.11, f32[1024]{0:T(1024)S(1)} %get-tuple-element.13, ...), kind=kOutput, calls=%fused_computation.45 | convolution fusion | flops 143720448 | bytes 8671232 | tf_op jit(solution)/shard_map/dot_general | solution.py:94
  147.9 0.0 copy-start.2
  148.0 0.0 copy-start.8
  148.0 0.0 copy-start.9
  148.0 1.9 %fusion.44 = bf16[1024,64]{1,0:T(8,128)(2,1)S(1)} fusion(f32[1024,1024]{1,0:T(8,128)S(1)} %get-tuple-element.24, f32[1024]{0:T(1024)S(1)} %get-tuple-element.8, bf16[1024,384]{0,1:T(8,128)(2,1)S(1)} %fusion.29, f32[1024,1024]{0,1:T(8,128)S(1)} %get-tuple-element.23, f32[1024]{0:T(1024)S(1)} %get-tuple-element.10, f32[1024]{0:T(1024)S(1)} %get-tuple-element.12, ...), kind=kOutput, calls=%fused_computation.46 | convolution fusion | flops 143720448 | bytes 8671232 | tf_op jit(solution)/shard_map/dot_general | solution.py:94
  150.0 1.8 %fusion.71 = (bf16[1024,128]{1,0:T(8,128)(2,1)S(1)}, bf16[128,1024]{0,1:T(8,128)(2,1)}) fusion(bf16[1,1024,128]{2,1,0:T(8,128)(2,1)S(1)} %copy-done.1, bf16[1,1024,128]{2,1,0:T(8,128)(2,1)S(1)} %copy-done.8, bf16[1,1024,128]{2,1,0:T(8,128)(2,1)S(1)} %copy-done.9, bf16[1,1024,128]{2,1,0:T(8,128)(2,1)S(1)} %copy-done.2, ...), kind=kOutput, calls=%fused_computation.77 | convolution fusion | flops 270663680 | bytes 3932160 | tf_op jit(solution)/shard_map/dot_general | solution.py:37
  151.8 0.4 fusion.73
  152.1 1.9 %collective-permute-start.2 = (f32[1,64,128]{2,1,0:T(8,128)S(1)}, f32[1,64,128]{2,1,0:T(8,128)S(1)}, u32[]{:S(2)}, u32[]{:S(2)}) collective-permute-start(f32[1,64,128]{2,1,0:T(8,128)S(1)} %bitcast.158), channel_id=1, source_target_pairs={{0,8},{8,16},{16,24},{24,32},{32,40},{40,48},{48,56},{56,64},{64,7... | collective-permute-start | bytes 98312 | tf_op jit(solution)/shard_map/ppermute | solution.py:30
  154.1 12.4 %collective-permute-start.3 = (f32[1,64,128]{2,1,0:T(8,128)S(1)}, f32[1,64,128]{2,1,0:T(8,128)S(1)}, u32[]{:S(2)}, u32[]{:S(2)}) collective-permute-start(f32[1,64,128]{2,1,0:T(8,128)S(1)} %bitcast.159), channel_id=1, source_target_pairs={{8,0},{16,8},{24,16},{32,24},{40,32},{48,40},{56,48},{64,56},{72,6... | collective-permute-start | bytes 98312 | tf_op jit(solution)/shard_map/ppermute | solution.py:31
  166.4 1.4 fusion.50
  167.8 0.0 collective-permute-done.2
  167.8 0.2 collective-permute-done.3
  168.0 1.8 %fusion.51 = bf16[1,1024,128]{2,1,0:T(8,128)(2,1)} fusion(f32[192,128]{1,0:T(8,128)S(1)} %bitcast.164, s32[192]{0:T(256)S(1)} %pad_add_fusion.1, bf16[1,1024,128]{2,1,0:T(8,128)(2,1)S(1)} %copy-done.9), kind=kOutput, calls=%fused_computation.49 | convolution fusion | flops 302710784 | bytes 623360 | tf_op jit(solution)/shard_map/dot_general | solution.py:53
  (21 shorter events, 0.1 us)
Async XLA Ops:
  7.2 71.0 %copy-start = (f32[1,1024,128]{2,1,0:T(8,128)S(1)}, f32[1,1024,128]{2,1,0:T(8,128)}, u32[]{:S(2)}) copy-start(f32[1,1024,128]{2,1,0:T(8,128)} %param.13) | copy-start | bytes 1572868
  7.2 71.0 %copy-start.3 = (bf16[1,1024,128]{2,1,0:T(8,128)(2,1)S(1)}, bf16[1,1024,128]{2,1,0:T(8,128)(2,1)}, u32[]{:S(2)}) copy-start(bf16[1,1024,128]{2,1,0:T(8,128)(2,1)} %param.14) | copy-start | bytes 786436
  7.2 71.0 %copy-start.4 = (bf16[1,1024,128]{2,1,0:T(8,128)(2,1)S(1)}, bf16[1,1024,128]{2,1,0:T(8,128)(2,1)}, u32[]{:S(2)}) copy-start(bf16[1,1024,128]{2,1,0:T(8,128)(2,1)} %param.15) | copy-start | bytes 786436
  7.2 71.0 %copy-start.1 = (bf16[1,1024,128]{2,1,0:T(8,128)(2,1)S(1)}, bf16[1,1024,128]{2,1,0:T(8,128)(2,1)}, u32[]{:S(2)}) copy-start(bf16[1,1024,128]{2,1,0:T(8,128)(2,1)} %param.16) | copy-start | bytes 786436
  7.2 128.1 %copy-start.12 = (bf16[1024,128]{1,0:T(8,128)(2,1)S(1)}, bf16[1024,128]{1,0:T(8,128)(2,1)}, u32[]{:S(2)}) copy-start(bf16[1024,128]{1,0:T(8,128)(2,1)} %param.22) | copy-start | bytes 786436
  7.2 128.1 %copy-start.11 = (bf16[1024,128]{1,0:T(8,128)(2,1)S(1)}, bf16[1024,128]{1,0:T(8,128)(2,1)}, u32[]{:S(2)}) copy-start(bf16[1024,128]{1,0:T(8,128)(2,1)} %param.23) | copy-start | bytes 786436
  7.2 128.1 %all-gather.2.cloned.1.call-start = ((), (), s32[]{:S(2)}) async-start(), calls=%async_computation | async-start | bytes 2359296 | tf_op jit(solution)/shard_map/all_gather | solution.py:122
  10.5 16.8 %collective-permute-start = (bf16[1,64,128]{2,1,0:T(8,128)(2,1)S(1)}, bf16[1,64,128]{2,1,0:T(8,128)(2,1)S(1)}, u32[]{:S(2)}, u32[]{:S(2)}) collective-permute-start(bf16[1,64,128]{2,1,0:T(8,128)(2,1)S(1)} %convert_bitcast_fusion.3), channel_id=1, source_target_pairs={{0,8},{8,16},{16,24},{24,32},{32,40},{40,48},{48,56},{56,64},{64,7... | collective-permute-start | bytes 49160 | tf_op jit(solution)/shard_map/ppermute | solution.py:30
  12.4 16.2 %collective-permute-start.1 = (bf16[1,64,128]{2,1,0:T(8,128)(2,1)S(1)}, bf16[1,64,128]{2,1,0:T(8,128)(2,1)S(1)}, u32[]{:S(2)}, u32[]{:S(2)}) collective-permute-start(bf16[1,64,128]{2,1,0:T(8,128)(2,1)S(1)} %convert_bitcast_fusion.3), channel_id=1, source_target_pairs={{8,0},{16,8},{24,16},{32,24},{40,32},{48,40},{56,48},{64,56},{72,6... | collective-permute-start | bytes 49160 | tf_op jit(solution)/shard_map/ppermute | solution.py:31
  30.2 107.8 %copy-start.13 = (bf16[1024,128]{1,0:T(8,128)(2,1)}, bf16[1024,128]{1,0:T(8,128)(2,1)S(1)}, u32[]{:S(2)}) copy-start(bf16[1024,128]{1,0:T(8,128)(2,1)S(1)} %fusion.38) | copy-start | bytes 786436
  114.3 24.5 %copy-start.7 = (bf16[1,1024,128]{2,1,0:T(8,128)(2,1)S(1)}, bf16[1,1024,128]{2,1,0:T(8,128)(2,1)}, u32[]{:S(2)}) copy-start(bf16[1,1024,128]{2,1,0:T(8,128)(2,1)} %param.24) | copy-start | bytes 786436
  138.0 1.6 copy-start.10
  147.9 2.0 %copy-start.2 = (bf16[1,1024,128]{2,1,0:T(8,128)(2,1)S(1)}, bf16[1,1024,128]{2,1,0:T(8,128)(2,1)}, u32[]{:S(2)}) copy-start(bf16[1,1024,128]{2,1,0:T(8,128)(2,1)} %param.17) | copy-start | bytes 786436
  148.0 2.0 %copy-start.5 = (bf16[1,1024,1024]{2,1,0:T(8,128)(2,1)S(1)}, bf16[1,1024,1024]{2,1,0:T(8,128)(2,1)}, u32[]{:S(2)}) copy-start(bf16[1,1024,1024]{2,1,0:T(8,128)(2,1)} %all-gather.2.cloned.1.call-done) | copy-start | bytes 6291460
  148.0 2.0 %copy-start.8 = (bf16[1,1024,128]{2,1,0:T(8,128)(2,1)S(1)}, bf16[1,1024,128]{2,1,0:T(8,128)(2,1)}, u32[]{:S(2)}) copy-start(bf16[1,1024,128]{2,1,0:T(8,128)(2,1)} %param.19) | copy-start | bytes 786436
  148.0 2.0 %copy-start.9 = (bf16[1,1024,128]{2,1,0:T(8,128)(2,1)S(1)}, bf16[1,1024,128]{2,1,0:T(8,128)(2,1)}, u32[]{:S(2)}) copy-start(bf16[1,1024,128]{2,1,0:T(8,128)(2,1)} %param.18) | copy-start | bytes 786436
  151.8 18.1 %copy-start.6 = (bf16[1024,128]{1,0:T(8,128)(2,1)}, bf16[1024,128]{1,0:T(8,128)(2,1)S(1)}, u32[]{:S(2)}) copy-start(bf16[1024,128]{1,0:T(8,128)(2,1)S(1)} %get-tuple-element.25) | copy-start | bytes 786436
  152.1 15.7 %collective-permute-start.2 = (f32[1,64,128]{2,1,0:T(8,128)S(1)}, f32[1,64,128]{2,1,0:T(8,128)S(1)}, u32[]{:S(2)}, u32[]{:S(2)}) collective-permute-start(f32[1,64,128]{2,1,0:T(8,128)S(1)} %bitcast.158), channel_id=1, source_target_pairs={{0,8},{8,16},{16,24},{24,32},{32,40},{40,48},{48,56},{56,64},{64,7... | collective-permute-start | bytes 98312 | tf_op jit(solution)/shard_map/ppermute | solution.py:30
  154.1 13.9 %collective-permute-start.3 = (f32[1,64,128]{2,1,0:T(8,128)S(1)}, f32[1,64,128]{2,1,0:T(8,128)S(1)}, u32[]{:S(2)}, u32[]{:S(2)}) collective-permute-start(f32[1,64,128]{2,1,0:T(8,128)S(1)} %bitcast.159), channel_id=1, source_target_pairs={{8,0},{16,8},{24,16},{32,24},{40,32},{48,40},{56,48},{64,56},{72,6... | collective-permute-start | bytes 98312 | tf_op jit(solution)/shard_map/ppermute | solution.py:31
Sparse Core Ops, SparseCore 0:
  11.3 124.0 all-gather.1
where the time goes:
time: 178 us
  blocking collectives  77.9 us (44%)
  starting transfers between devices  31 us (17%)
  matrix products  23.6 us (13%)
  waiting for transfers between devices  23.3 us (13%)
  between operations  16.1 us (9%)
  other arithmetic  5.04 us (3%)
    psum x5, blocking collectives, over_axes(): value = lax.psum(value, axis)  77.9 us
    ppermute x2, starting transfers between devices, extended(): after = lax.ppermute(leading, axis, down)  27.1 us
    all_gather x1, waiting for transfers between devices, local_gradient(): gathered = lax.all_gather(tokens, TP, axis=1, tiled=True)  21.1 us
    dot_general x4, matrix products, place_rows(): lax.dot_general(matrix, values, (((0,), (0,)), ((), ())), precision=lax.P...  7.71 us
    dot_general x5, matrix products, contract(): lax.dot_general(left, right, (((left_dim,), (right_dim,)), ((), ())), pre...  7.34 us
    ppermute x2, starting transfers between devices, extended(): before = lax.ppermute(last, axis, up)  3.84 us
    dot_general x2, matrix products, head_grad(): jnp.dot(score_grad, key_head, preferred_element_type=jnp.float32)  3.83 us
  transfers between devices with their start and end apart: 5, of which 3 were waited for; matrix products, arithmetic and copies ran while one was open for 6% of the time, Pallas kernels for 0%

commit v1 on v0

--- a/solution.py
+++ b/solution.py
@@ -6,7 +6,6 @@
 
 HD = 64
 BLK = ("blk_0", "blk_1", "blk_2")
-BLK_TP = ("blk_0", "blk_1", "blk_2", "tp_0", "tp_1")
 TP = ("tp_0", "tp_1")
 
 
@@ -14,23 +13,31 @@
 step_rate = 0.5
 
 
-def over_axes(value, axes):
-    for axis in axes:
-        value = lax.psum(value, axis)
-    return value
-
-
-def extended(value, sides, width):
-    for axis, dim in sides:
-        size, length = (lax.axis_size(axis), value.shape[dim])
-        up = [(i, (i + 1) % size) for i in range(size)]
-        down = [(j, i) for i, j in up]
-        last = lax.slice_in_dim(value, length - width, length, axis=dim)
-        leading = lax.slice_in_dim(value, 0, width, axis=dim)
-        before = lax.ppermute(last, axis, up)
-        after = lax.ppermute(leading, axis, down)
-        value = jnp.concatenate([before, value, after], axis=dim)
-    return value
+def swaps(value):
+    count = lax.axis_size(BLK)
+    near = [(r, r ^ 1) for r in range(count)]
+    far = [(r, (r + 1) % count if r % 2 else (r - 1) % count) for r in range(count)]
+    return lax.ppermute(value, BLK, near), lax.ppermute(value, BLK, far)
+
+
+def spread_sum(value, axes):
+    count = lax.axis_size(axes)
+    rows = jnp.broadcast_to(value, (count, value.shape[1]))
+    received = lax.all_to_all(rows, axes, 0, 0, tiled=True)
+    return jnp.sum(received, axis=0, keepdims=True)
+
+
+def spread_tokens(value):
+    count = lax.axis_size("tp_1")
+    blocks = jnp.broadcast_to(value, (count,) + value.shape[1:])
+    return lax.all_to_all(blocks, "tp_1", 0, 0, tiled=True).reshape(-1, value.shape[2])
+
+
+def join_halves(own_half, other_half):
+    low = lax.axis_index("tp_0") == 0
+    first = jnp.where(low, own_half, other_half)
+    second = jnp.where(low, other_half, own_half)
+    return jnp.concatenate([first, second], axis=0)
 
 
 def contract(left, right, left_dim, right_dim):
@@ -57,29 +64,31 @@
 
 def neighbour_picks(row_picks, stream):
     replica_count = lax.axis_size(BLK)
-    replica_rank = lax.axis_index(BLK)
-    lower_picks = lax.dynamic_index_in_dim(
-        row_picks, (replica_rank - 1 + replica_count) % replica_count, 0, keepdims=False
-    )[stream]
-    own_picks = lax.dynamic_index_in_dim(row_picks, replica_rank, 0, keepdims=False)[stream]
-    upper_picks = lax.dynamic_index_in_dim(
-        row_picks, (replica_rank + 1) % replica_count, 0, keepdims=False
-    )[stream]
-    return jnp.concatenate([lower_picks, own_picks, upper_picks], axis=0)
+    rank = lax.axis_index(BLK)
+    near = rank + 1 - 2 * (rank % 2)
+    far = (rank - 1 + 2 * (rank % 2) + replica_count) % replica_count
+    return jnp.concatenate(
+        [
+            lax.dynamic_index_in_dim(row_picks, place, 0, keepdims=False)[stream]
+            for place in (rank, near, far)
+        ],
+        axis=0,
+    )
 
 
 def mix_stream(received, row_picks, stream, total_rows):
     picks = neighbour_picks(row_picks, stream)
-    values = received.reshape(received.shape[0] * received.shape[1], received.shape[2])
-    return place_rows(picks, values, total_rows) / 3.0
-
-
-def consensus_of(mixed_new, copies_new):
+    return place_rows(picks, received, total_rows) / 3.0
+
+
+def gap_rows(mixed_new, copies_new):
     gap_value = mixed_new.astype(jnp.float32) - copies_new.astype(jnp.float32)
-    local_sum = jnp.sum(gap_value * gap_value)
-    total_sum = over_axes(local_sum, BLK_TP)
-    count = lax.axis_size(BLK) * copies_new.shape[0] * copies_new.shape[0]
-    return total_sum / float(count)
+    return jnp.sum(gap_value * gap_value, axis=0, keepdims=True)
+
+
+def consensus_of(partial_sums, width):
+    total_sum = jnp.sum(spread_sum(partial_sums, ("blk_1", "tp_0")))
+    return total_sum / float(lax.axis_size(BLK) * width * width)
 
 
 def head_grad(query_head, key_head, value_head, out_head, same_image):
@@ -115,16 +124,15 @@
     return jnp.concatenate(pieces_list, axis=1)
 
 
-def local_gradient(weights_new, tokens, image_ids, key_weight, value_weight, out_grad):
+def local_gradient(weights_new, gathered, image_ids, key_weight, value_weight, out_grad):
     model_width = weights_new.shape[0]
     query_weight = (weights_new * model_width ** (-0.5)).astype(jnp.bfloat16)
     joined = jnp.concatenate([query_weight, key_weight, value_weight], axis=1)
-    gathered = lax.all_gather(tokens, TP, axis=1, tiled=True)
-    projected = jnp.dot(gathered[0], joined, preferred_element_type=jnp.float32).astype(
+    projected = jnp.dot(gathered, joined, preferred_element_type=jnp.float32).astype(
         jnp.bfloat16
     )[None][0]
     query_grad = attention_grad(projected, image_ids[0], out_grad[0])
-    total = contract(gathered[0], query_grad, 0, 0)
+    total = contract(gathered, query_grad, 0, 0)
     return (total * model_width ** (-0.5)).astype(jnp.bfloat16)
 
 
@@ -145,6 +153,8 @@
 ):
     model_width = weights.shape[1]
     replica_rank = lax.axis_index(BLK)
+    other = lax.ppermute(tokens, "tp_0", [(0, 1), (1, 0)])
+    own_half = spread_tokens(tokens)
     own_picks = lax.dynamic_index_in_dim(row_picks, replica_rank, 0, keepdims=False)
     copy_value = copies[0].astype(jnp.float32)
     mixed_value = copies_mixed[0].astype(jnp.float32)
@@ -157,14 +167,17 @@
     copies_new = (copy_value + place_rows(own_picks[0], param_values, model_width)).astype(
         jnp.bfloat16
     )
-    param_received = extended(param_values[None].astype(jnp.bfloat16), ((BLK, 0),), 1).astype(
-        jnp.float32
-    )
+    param_sent = param_values.astype(jnp.bfloat16)
+    own_half, param_sent = lax.optimization_barrier((own_half, param_sent))
+    param_received = jnp.concatenate((param_sent,) + swaps(param_sent), axis=0).astype(jnp.float32)
     mixed_new = (mixed_value + mix_stream(param_received, row_picks, 0, model_width)).astype(
         jnp.bfloat16
     )
-    consensus = consensus_of(mixed_new, copies_new)
-    grad_new = local_gradient(weights_new, tokens, image_ids, key_weight, value_weight, out_grad)
+    partial_sums = spread_sum(gap_rows(mixed_new, copies_new), ("blk_0", "blk_2", "tp_1"))
+    other, partial_sums = lax.optimization_barrier((other, partial_sums))
+    other_half = spread_tokens(other)
+    gathered = join_halves(own_half, other_half)
+    grad_new = local_gradient(weights_new, gathered, image_ids, key_weight, value_weight, out_grad)
     tracker_copy_value = tracker_copy[0].astype(jnp.float32)
     tracker_mixed_value = tracker_mixed[0].astype(jnp.float32)
     tracker_new = (
@@ -177,7 +190,9 @@
     tracker_copy_new = (
         tracker_copy_value + place_rows(own_picks[1], tracker_values, model_width)
     ).astype(jnp.bfloat16)
-    tracker_received = extended(tracker_values[None], ((BLK, 0),), 1)
+    tracker_values, partial_sums = lax.optimization_barrier((tracker_values, partial_sums))
+    consensus = consensus_of(partial_sums, model_width)
+    tracker_received = jnp.concatenate((tracker_values,) + swaps(tracker_values), axis=0)
     tracker_mixed_new = (
         tracker_mixed_value + mix_stream(tracker_received, row_picks, 1, model_width)
     ).astype(jnp.bfloat16)

time: 178 us -> 134 us (0.75)
  the two profiles are of different devices: /device:TPU:8 before, /device:TPU:1 now
where the time goes in v1:
time: 134 us; the launch traced here: 132 us
  starting transfers between devices  45.6 us (34%)
  waiting for transfers between devices  36.2 us (27%)
  blocking collectives  19.3 us (14%)
  matrix products  18.8 us (14%)
  other arithmetic  5.22 us (4%)
  local copies, waits for them, and re-layouts  4.74 us (4%)
  between operations  2.7 us (2%)
    all_to_all x2, waiting for transfers between devices, spread_tokens(): lax.all_to_all(blocks, 'tp_1', 0, 0, tiled=True).reshape(-1, value.shape[2])  24 us
    all_to_all x1, blocking collectives, spread_sum(): received = lax.all_to_all(rows, axes, 0, 0, tiled=True)  19.3 us
    ppermute x1, starting transfers between devices, per_device(): other = lax.ppermute(tokens, 'tp_0', [(0, 1), (1, 0)])  16.4 us
    ppermute x4, starting transfers between devices, swaps(): return (lax.ppermute(value, BLK, near), lax.ppermute(value, BLK, far))  11.9 us
    all_to_all x1, waiting for transfers between devices, spread_sum(): received = lax.all_to_all(rows, axes, 0, 0, tiled=True)  9.81 us
    all_to_all x1, starting transfers between devices, spread_sum(): received = lax.all_to_all(rows, axes, 0, 0, tiled=True)  9.39 us
    all_to_all x2, starting transfers between devices, spread_tokens(): lax.all_to_all(blocks, 'tp_1', 0, 0, tiled=True).reshape(-1, value.shape[2])  7.83 us
    dot_general x5, matrix products, contract(): lax.dot_general(left, right, (((left_dim,), (right_dim,)), ((), ())), pre...  7.04 us
  transfers between devices with their start and end apart: 8, of which 4 were waited for; matrix products, arithmetic and copies ran while one was open for 8% of the time, Pallas kernels for 0%

profile of v1, /device:TPU:1, one launch (start us, length us, event | category | flops | bytes accessed | tf_op | source)
XLA Modules:
  0.0 132.5 jit_solution(10665472039647047125)
XLA Ops:
  0.6 0.0 copy-start.1
  0.6 0.0 copy-start.2
  0.7 16.4 %collective-permute-start.2 = (bf16[1,128,1024]{2,1,0:T(8,128)(2,1)}, bf16[1,128,1024]{2,1,0:T(8,128)(2,1)S(1)}, u32[]{:S(2)}, u32[]{:S(2)}) collective-permute-start(bf16[1,128,1024]{2,1,0:T(8,128)(2,1)} %param.20), channel_id=1, source_target_pairs={{0,4},{4,0},{1,5},{5,1},{2,6},{6,2},{3,7},{7,3},{8,12},{12,8},{9,1... | collective-permute-start | bytes 786440 | tf_op jit(solution)/shard_map/ppermute | solution.py:156
  17.1 2.1 %broadcast_in_dim.63 = bf16[4,128,1024]{2,1,0:T(8,128)(2,1)} broadcast(bf16[128,1024]{1,0:T(8,128)(2,1)} %bitcast.149), dimensions={1,2} | broadcast | bytes 1310720 | tf_op jit(solution)/shard_map/broadcast_in_dim | solution.py:32
  19.1 4.3 %all-to-all-start = ((bf16[4,128,1024]{2,1,0:T(8,128)(2,1)}), bf16[4,128,1024]{2,1,0:T(8,128)(2,1)S(1)}, u32[]{:S(2)}, u32[]{:S(2)}) async-start(bf16[4,128,1024]{2,1,0:T(8,128)(2,1)} %broadcast_in_dim.63), calls=%async_computation | async-start | bytes 2097152 | tf_op jit(solution)/shard_map/all_to_all | solution.py:33
  23.4 0.7 constant_dynamic-slice_fusion.1
  24.2 1.8 %fusion.103 = (bf16[64,128]{1,0:T(8,128)(2,1)S(1)}, f32[64,128]{1,0:T(8,128)S(1)}) fusion(bf16[1,1024,128]{2,1,0:T(8,128)(2,1)} %param.14, bf16[1,1024,128]{2,1,0:T(8,128)(2,1)} %param.16, bf16[1,1024,128]{2,1,0:T(8,128)(2,1)} %param.15, f32[1,1024,128]{2,1,0:T(8,128)} %param.13, s32[64]{0:T(128)S(1)} %get-tuple-element.36), kind=kOutput, calls=%fused_computation.133 | convolution fusion | flops 101916672 | bytes 1360128 | tf_op jit(solution)/shard_map/dot_general | solution.py:55
  25.9 11.4 %all-to-all-done = bf16[4,128,1024]{2,1,0:T(8,128)(2,1)S(1)} async-done(((bf16[4,128,1024]{2,1,0:T(8,128)(2,1)}), bf16[4,128,1024]{2,1,0:T(8,128)(2,1)S(1)}, u32[]{:S(2)}, u32[]{:S(2)}) %all-to-all-start) | async-done | bytes 1048608 | tf_op jit(solution)/shard_map/all_to_all | solution.py:33
  37.3 4.1 %collective-permute-start = (bf16[64,128]{1,0:T(8,128)(2,1)S(1)}, bf16[64,128]{1,0:T(8,128)(2,1)S(1)}, u32[]{:S(2)}, u32[]{:S(2)}) collective-permute-start(bf16[64,128]{1,0:T(8,128)(2,1)S(1)} %get-tuple-element.14), channel_id=1, source_target_pairs={{0,8},{8,0},{16,24},{24,16},{32,40},{40,32},{48,56},{56,48},{64,72... | collective-permute-start | bytes 49160 | tf_op jit(solution)/shard_map/ppermute | solution.py:20
  41.4 2.5 %collective-permute-start.1 = (bf16[64,128]{1,0:T(8,128)(2,1)S(1)}, bf16[64,128]{1,0:T(8,128)(2,1)S(1)}, u32[]{:S(2)}, u32[]{:S(2)}) collective-permute-start(bf16[64,128]{1,0:T(8,128)(2,1)S(1)} %get-tuple-element.14), channel_id=1, source_target_pairs={{0,504},{8,16},{16,8},{24,32},{32,24},{40,48},{48,40},{56,64},{64,... | collective-permute-start | bytes 49160 | tf_op jit(solution)/shard_map/ppermute | solution.py:20
  44.0 0.1 pad_add_fusion
  44.0 0.0 collective-permute-done
  44.0 2.4 %collective-permute-done.1 = bf16[64,128]{1,0:T(8,128)(2,1)S(1)} collective-permute-done((bf16[64,128]{1,0:T(8,128)(2,1)S(1)}, bf16[64,128]{1,0:T(8,128)(2,1)S(1)}, u32[]{:S(2)}, u32[]{:S(2)}) %collective-permute-start.1) | collective-permute-done | bytes 16416 | tf_op jit(solution)/shard_map/ppermute | solution.py:20
  46.5 0.6 fusion.23
  47.0 0.0 copy-start.13
  47.1 1.4 %multiply_reduce_fusion = (f32[128]{0:T(128)S(1)}, bf16[1024,128]{1,0:T(8,128)(2,1)}) fusion(bf16[1024,128]{1,0:T(8,128)(2,1)S(1)} %fusion.23, f32[64,128]{1,0:T(8,128)S(1)} %get-tuple-element.38, s32[64]{0:T(128)S(1)} %get-tuple-element.36, bf16[1,1024,128]{2,1,0:T(8,128)(2,1)S(1)} %copy-done.1), kind=kOutput, calls=%fused_computation.77 | convolution fusion | flops 101777280 | bytes 819968 | tf_op jit(solution)/shard_map/dot_general | solution.py:60
  48.5 19.3 %all_to_all.22 = f32[32,1,128]{2,1,0:T(1,128)S(1)} all-to-all(f32[32,1,128]{2,1,0:T(1,128)S(1)} %broadcast_in_dim.65), channel_id=1, replica_groups=mesh['blk_0'=4,'blk_1'=8,'blk_2'=2,'tp_0'=2,'tp_1'=4] {'blk_0','blk_2','..., dimensions={0} | all-to-all | bytes 32768 | tf_op jit(solution)/shard_map/all_to_all | solution.py:26
  67.8 0.0 collective-permute-done.2
  67.8 1.1 broadcast_in_dim.68
  68.9 3.5 %all-to-all-start.2 = ((bf16[4,128,1024]{2,1,0:T(8,128)(2,1)}), bf16[4,128,1024]{2,1,0:T(8,128)(2,1)S(1)}, u32[]{:S(2)}, u32[]{:S(2)}) async-start(bf16[4,128,1024]{2,1,0:T(8,128)(2,1)} %broadcast_in_dim.68), calls=%async_computation.2 | async-start | bytes 2097152 | tf_op jit(solution)/shard_map/all_to_all | solution.py:33
  72.4 0.1 pad_add_fusion.1
  72.5 0.9 multiply_convert_fusion
  73.4 0.9 fusion.51
  74.3 12.6 %all-to-all-done.2 = bf16[4,128,1024]{2,1,0:T(8,128)(2,1)S(1)} async-done(((bf16[4,128,1024]{2,1,0:T(8,128)(2,1)}), bf16[4,128,1024]{2,1,0:T(8,128)(2,1)S(1)}, u32[]{:S(2)}, u32[]{:S(2)}) %all-to-all-start.2) | async-done | bytes 1048608 | tf_op jit(solution)/shard_map/all_to_all | solution.py:33
  86.9 0.2 bitcast_select_fusion.1
  87.1 1.0 convolution_convert_fusion
  88.2 0.0 copy-start.5
  88.2 0.0 copy-start.8
  88.2 0.8 fusion.69
  89.0 0.2 copy-done.5
  89.1 0.8 fusion.60
  89.9 1.3 fusion.12
  91.2 2.4 %fusion.9 = (f32[1024]{0:T(1024)S(1)}, f32[1024]{0:T(1024)S(1)}) fusion(f32[1024,1024]{0,1:T(8,128)S(1)} %get-tuple-element.41, f32[1024]{0:T(1024)S(1)} %get-tuple-element.24, s32[1024]{0:T(1024)S(1)} %bitcast.157, f32[1024]{0:T(1024)S(1)} %get-tuple-element.25, f32[1024,1024]{0,1:T(8,128)S(1)} %fusion.69), kind=kLoop, calls=%fused_computation.17 | loop fusion | flops 9435136 | bytes 8409088 | tf_op jit(solution)/shard_map/reduce_sum | solution.py:99
  93.6 2.7 %fusion.4 = (f32[1024]{0:T(1024)S(1)}, f32[1024]{0:T(1024)S(1)}, f32[1024,1024]{1,0:T(8,128)S(1)}) fusion(f32[1024]{0:T(1024)S(1)} %get-tuple-element.22, f32[1024]{0:T(1024)S(1)} %get-tuple-element.24, f32[1024,1024]{0,1:T(8,128)S(1)} %get-tuple-element.41, s32[1024]{0:T(1024)S(1)} %bitcast.158, f32[1024,1024]{1,0:T(8,128)S(1)} %fusion.60, ...), kind=kOutput, calls=%fused_computation.10 | convolution fusion | flops 147847168 | bytes 17203200 | tf_op jit(solution)/shard_map/dot_general | solution.py:44
  96.4 1.7 %fusion.29 = bf16[1024,64]{0,1:T(8,128)(2,1)S(1)} fusion(f32[1024,1024]{1,0:T(8,128)S(1)} %fusion.60, f32[1024]{0:T(1024)S(1)} %get-tuple-element.21, bf16[1024,384]{0,1:T(8,128)(2,1)S(1)} %convolution_convert_fusion, f32[1024,1024]{0,1:T(8,128)S(1)} %fusion.69, f32[1024]{0:T(1024)S(1)} %get-tuple-element.23, f32[1024]{0:T(1024)S(1)} %get-tuple-element.25, ...), kind=kOutput, calls=%fused_computation.41 | convolution fusion | flops 143720448 | bytes 8671232 | tf_op jit(solution)/shard_map/dot_general | solution.py:103
  98.1 0.0 copy-start.11
  98.1 0.0 copy-start.12
  98.1 1.7 %fusion.32 = bf16[1024,64]{0,1:T(8,128)(2,1)S(1)} fusion(f32[1024,1024]{1,0:T(8,128)S(1)} %get-tuple-element.42, f32[1024]{0:T(1024)S(1)} %get-tuple-element.20, bf16[1024,384]{0,1:T(8,128)(2,1)S(1)} %convolution_convert_fusion, f32[1024,1024]{0,1:T(8,128)S(1)} %get-tuple-element.41, f32[1024]{0:T(1024)S(1)} %get-tuple-element.22, ...), kind=kOutput, calls=%fused_computation.42 | convolution fusion | flops 143720448 | bytes 8671232 | tf_op jit(solution)/shard_map/dot_general | solution.py:103
  99.9 1.5 %fusion.54 = (bf16[1024,128]{1,0:T(8,128)(2,1)S(1)}, bf16[1024,128]{1,0:T(8,128)(2,1)}) fusion(bf16[1,1024,128]{2,1,0:T(8,128)(2,1)S(1)} %copy-done.3, bf16[1,1024,128]{2,1,0:T(8,128)(2,1)S(1)} %copy-done.11, bf16[1,1024,128]{2,1,0:T(8,128)(2,1)S(1)} %copy-done.12, bf16[1,1024,128]{2,1,0:T(8,128)(2,1)S(1)} %copy-done.4, bf16[1024,64]{0,1:T(8,128)(2,1)S(1)} %fusion.29, ...), kind=kOutput, calls=%fused_computation.72 | convolution fusion | flops 274857984 | bytes 3932160 | tf_op jit(solution)/shard_map/dot_general | solution.py:44
  101.4 0.4 fusion.56
  101.7 3.4 %collective-permute-start.3 = (f32[64,128]{1,0:T(8,128)S(1)}, f32[64,128]{1,0:T(8,128)S(1)}, u32[]{:S(2)}, u32[]{:S(2)}) collective-permute-start(f32[64,128]{1,0:T(8,128)S(1)} %fusion.56), channel_id=1, source_target_pairs={{0,8},{8,0},{16,24},{24,16},{32,40},{40,32},{48,56},{56,48},{64,72... | collective-permute-start | bytes 98312 | tf_op jit(solution)/shard_map/ppermute | solution.py:20
  105.2 1.9 %collective-permute-start.4 = (f32[64,128]{1,0:T(8,128)S(1)}, f32[64,128]{1,0:T(8,128)S(1)}, u32[]{:S(2)}, u32[]{:S(2)}) collective-permute-start(f32[64,128]{1,0:T(8,128)S(1)} %fusion.56), channel_id=1, source_target_pairs={{0,504},{8,16},{16,8},{24,32},{32,24},{40,48},{48,40},{56,64},{64,... | collective-permute-start | bytes 98312 | tf_op jit(solution)/shard_map/ppermute | solution.py:20
  107.1 0.6 broadcast_in_dim.74
  107.7 9.4 %all-to-all-start.3 = ((f32[16,1,128]{2,1,0:T(1,128)}), f32[16,1,128]{2,1,0:T(1,128)S(1)}, u32[]{:S(2)}, u32[]{:S(2)}) async-start(f32[16,1,128]{2,1,0:T(1,128)} %broadcast_in_dim.74), calls=%async_computation.3 | async-start | bytes 16384 | tf_op jit(solution)/shard_map/all_to_all | solution.py:26
  117.1 1.4 %fusion.27 = bf16[1,1024,128]{2,1,0:T(8,128)(2,1)} fusion(f32[64,128]{1,0:T(8,128)S(1)} %fusion.56, bf16[1,1024,128]{2,1,0:T(8,128)(2,1)S(1)} %copy-done.4, s32[64]{0:T(128)S(1)} %get-tuple-element.35), kind=kOutput, calls=%fused_computation.39 | convolution fusion | flops 101122048 | bytes 557312 | tf_op jit(solution)/shard_map/dot_general | solution.py:60
  118.5 9.8 %all-to-all-done.3 = f32[16,1,128]{2,1,0:T(1,128)S(1)} async-done(((f32[16,1,128]{2,1,0:T(1,128)}), f32[16,1,128]{2,1,0:T(1,128)S(1)}, u32[]{:S(2)}, u32[]{:S(2)}) %all-to-all-start.3) | async-done | bytes 8224 | tf_op jit(solution)/shard_map/all_to_all | solution.py:26
  128.3 0.6 reduce_sum.73
  129.6 1.8 %fusion.28 = bf16[1,1024,128]{2,1,0:T(8,128)(2,1)} fusion(s32[192]{0:T(256)S(1)} %pad_add_fusion.1, bf16[1,1024,128]{2,1,0:T(8,128)(2,1)S(1)} %copy-done.12, f32[64,128]{1,0:T(8,128)S(1)} %collective-permute-done.4, f32[64,128]{1,0:T(8,128)S(1)} %collective-permute-done.3, f32[64,128]{1,0:T(8,128)S(1)} %fusion.56), kind=kOutput, calls=%fused_computation.40 | convolution fusion | flops 302759936 | bytes 623360 | tf_op jit(solution)/shard_map/dot_general | solution.py:60
  (26 shorter events, 0.1 us)
Async XLA Ops:
  0.6 46.4 %copy-start.1 = (bf16[1,1024,128]{2,1,0:T(8,128)(2,1)S(1)}, bf16[1,1024,128]{2,1,0:T(8,128)(2,1)}, u32[]{:S(2)}) copy-start(bf16[1,1024,128]{2,1,0:T(8,128)(2,1)} %param.14) | copy-start | bytes 786436
  0.6 45.8 %copy-start.2 = (bf16[1,1024,128]{2,1,0:T(8,128)(2,1)S(1)}, bf16[1,1024,128]{2,1,0:T(8,128)(2,1)}, u32[]{:S(2)}) copy-start(bf16[1,1024,128]{2,1,0:T(8,128)(2,1)} %param.15) | copy-start | bytes 786436
  0.7 67.1 %collective-permute-start.2 = (bf16[1,128,1024]{2,1,0:T(8,128)(2,1)}, bf16[1,128,1024]{2,1,0:T(8,128)(2,1)S(1)}, u32[]{:S(2)}, u32[]{:S(2)}) collective-permute-start(bf16[1,128,1024]{2,1,0:T(8,128)(2,1)} %param.20), channel_id=1, source_target_pairs={{0,4},{4,0},{1,5},{5,1},{2,6},{6,2},{3,7},{7,3},{8,12},{12,8},{9,1... | collective-permute-start | bytes 786440 | tf_op jit(solution)/shard_map/ppermute | solution.py:156
  19.1 53.4 %copy-start = (f32[1,1024,128]{2,1,0:T(8,128)S(1)}, f32[1,1024,128]{2,1,0:T(8,128)}, u32[]{:S(2)}) copy-start(f32[1,1024,128]{2,1,0:T(8,128)} %param.13) | copy-start | bytes 1572868
  19.1 53.4 %copy-start.3 = (bf16[1,1024,128]{2,1,0:T(8,128)(2,1)S(1)}, bf16[1,1024,128]{2,1,0:T(8,128)(2,1)}, u32[]{:S(2)}) copy-start(bf16[1,1024,128]{2,1,0:T(8,128)(2,1)} %param.16) | copy-start | bytes 786436
  19.1 18.2 %all-to-all-start = ((bf16[4,128,1024]{2,1,0:T(8,128)(2,1)}), bf16[4,128,1024]{2,1,0:T(8,128)(2,1)S(1)}, u32[]{:S(2)}, u32[]{:S(2)}) async-start(bf16[4,128,1024]{2,1,0:T(8,128)(2,1)} %broadcast_in_dim.63), calls=%async_computation | async-start | bytes 2097152 | tf_op jit(solution)/shard_map/all_to_all | solution.py:33
  37.3 6.7 %collective-permute-start = (bf16[64,128]{1,0:T(8,128)(2,1)S(1)}, bf16[64,128]{1,0:T(8,128)(2,1)S(1)}, u32[]{:S(2)}, u32[]{:S(2)}) collective-permute-start(bf16[64,128]{1,0:T(8,128)(2,1)S(1)} %get-tuple-element.14), channel_id=1, source_target_pairs={{0,8},{8,0},{16,24},{24,16},{32,40},{40,32},{48,56},{56,48},{64,72... | collective-permute-start | bytes 49160 | tf_op jit(solution)/shard_map/ppermute | solution.py:20
  41.4 5.1 %collective-permute-start.1 = (bf16[64,128]{1,0:T(8,128)(2,1)S(1)}, bf16[64,128]{1,0:T(8,128)(2,1)S(1)}, u32[]{:S(2)}, u32[]{:S(2)}) collective-permute-start(bf16[64,128]{1,0:T(8,128)(2,1)S(1)} %get-tuple-element.14), channel_id=1, source_target_pairs={{0,504},{8,16},{16,8},{24,32},{32,24},{40,48},{48,40},{56,64},{64,... | collective-permute-start | bytes 49160 | tf_op jit(solution)/shard_map/ppermute | solution.py:20
  47.0 21.8 %copy-start.13 = (bf16[1024,128]{1,0:T(8,128)(2,1)}, bf16[1024,128]{1,0:T(8,128)(2,1)S(1)}, u32[]{:S(2)}) copy-start(bf16[1024,128]{1,0:T(8,128)(2,1)S(1)} %fusion.23) | copy-start | bytes 786436
  68.9 18.0 %all-to-all-start.2 = ((bf16[4,128,1024]{2,1,0:T(8,128)(2,1)}), bf16[4,128,1024]{2,1,0:T(8,128)(2,1)S(1)}, u32[]{:S(2)}, u32[]{:S(2)}) async-start(bf16[4,128,1024]{2,1,0:T(8,128)(2,1)} %broadcast_in_dim.68), calls=%async_computation.2 | async-start | bytes 2097152 | tf_op jit(solution)/shard_map/all_to_all | solution.py:33
  74.3 12.8 %copy-start.7 = (bf16[1024,128]{1,0:T(8,128)(2,1)S(1)}, bf16[1024,128]{1,0:T(8,128)(2,1)}, u32[]{:S(2)}) copy-start(bf16[1024,128]{1,0:T(8,128)(2,1)} %multiply_convert_fusion) | copy-start | bytes 786436
  74.3 12.8 %copy-start.9 = (bf16[1024,128]{1,0:T(8,128)(2,1)S(1)}, bf16[1024,128]{1,0:T(8,128)(2,1)}, u32[]{:S(2)}) copy-start(bf16[1024,128]{1,0:T(8,128)(2,1)} %param.23) | copy-start | bytes 786436
  74.3 12.8 %copy-start.10 = (bf16[1024,128]{1,0:T(8,128)(2,1)S(1)}, bf16[1024,128]{1,0:T(8,128)(2,1)}, u32[]{:S(2)}) copy-start(bf16[1024,128]{1,0:T(8,128)(2,1)} %param.22) | copy-start | bytes 786436
  88.2 1.0 copy-start.5
  88.2 1.7 %copy-start.8 = (s32[1,1024]{1,0:T(1,128)S(1)}, s32[1,1024]{1,0:T(1,128)}, u32[]{:S(2)}) copy-start(s32[1,1024]{1,0:T(1,128)} %param.21) | copy-start | bytes 12292
  98.1 1.7 %copy-start.4 = (bf16[1,1024,128]{2,1,0:T(8,128)(2,1)S(1)}, bf16[1,1024,128]{2,1,0:T(8,128)(2,1)}, u32[]{:S(2)}) copy-start(bf16[1,1024,128]{2,1,0:T(8,128)(2,1)} %param.17) | copy-start | bytes 786436
  98.1 1.7 %copy-start.11 = (bf16[1,1024,128]{2,1,0:T(8,128)(2,1)S(1)}, bf16[1,1024,128]{2,1,0:T(8,128)(2,1)}, u32[]{:S(2)}) copy-start(bf16[1,1024,128]{2,1,0:T(8,128)(2,1)} %param.19) | copy-start | bytes 786436
  98.1 1.7 %copy-start.12 = (bf16[1,1024,128]{2,1,0:T(8,128)(2,1)S(1)}, bf16[1,1024,128]{2,1,0:T(8,128)(2,1)}, u32[]{:S(2)}) copy-start(bf16[1,1024,128]{2,1,0:T(8,128)(2,1)} %param.18) | copy-start | bytes 786436
  101.4 30.0 %copy-start.6 = (bf16[1024,128]{1,0:T(8,128)(2,1)}, bf16[1024,128]{1,0:T(8,128)(2,1)S(1)}, u32[]{:S(2)}) copy-start(bf16[1024,128]{1,0:T(8,128)(2,1)S(1)} %get-tuple-element.43) | copy-start | bytes 786436
  101.7 27.8 %collective-permute-start.3 = (f32[64,128]{1,0:T(8,128)S(1)}, f32[64,128]{1,0:T(8,128)S(1)}, u32[]{:S(2)}, u32[]{:S(2)}) collective-permute-start(f32[64,128]{1,0:T(8,128)S(1)} %fusion.56), channel_id=1, source_target_pairs={{0,8},{8,0},{16,24},{24,16},{32,40},{40,32},{48,56},{56,48},{64,72... | collective-permute-start | bytes 98312 | tf_op jit(solution)/shard_map/ppermute | solution.py:20
  105.2 24.4 %collective-permute-start.4 = (f32[64,128]{1,0:T(8,128)S(1)}, f32[64,128]{1,0:T(8,128)S(1)}, u32[]{:S(2)}, u32[]{:S(2)}) collective-permute-start(f32[64,128]{1,0:T(8,128)S(1)} %fusion.56), channel_id=1, source_target_pairs={{0,504},{8,16},{16,8},{24,32},{32,24},{40,48},{48,40},{56,64},{64,... | collective-permute-start | bytes 98312 | tf_op jit(solution)/shard_map/ppermute | solution.py:20
  107.7 20.6 %all-to-all-start.3 = ((f32[16,1,128]{2,1,0:T(1,128)}), f32[16,1,128]{2,1,0:T(1,128)S(1)}, u32[]{:S(2)}, u32[]{:S(2)}) async-start(f32[16,1,128]{2,1,0:T(1,128)} %broadcast_in_dim.74), calls=%async_computation.3 | async-start | bytes 16384 | tf_op jit(solution)/shard_map/all_to_all | solution.py:26

commit v2 on v1

v2 whole, which is shorter than its diff:
```python
import jax
import jax.numpy as jnp
from jax import lax
from jax.experimental import pallas as pl
from jax.experimental.pallas import tpu as pltpu
from jax.sharding import Mesh
from jax.sharding import PartitionSpec as P

HD = 64
IMAGES = 6
WINDOW = 256
BLK = ("blk_0", "blk_1", "blk_2")
TP = ("tp_0", "tp_1")


mixing_rate = 0.2
step_rate = 0.5


def swaps(value):
    count = lax.axis_size(BLK)
    near = [(r, r ^ 1) for r in range(count)]
    far = [(r, (r + 1) % count if r % 2 else (r - 1) % count) for r in range(count)]
    return lax.ppermute(value, BLK, near), lax.ppermute(value, BLK, far)


def spread_sum(value, axes):
    count = lax.axis_size(axes)
    rows = jnp.broadcast_to(value, (count, value.shape[1]))
    received = lax.all_to_all(rows, axes, 0, 0, tiled=True)
    return jnp.sum(received, axis=0, keepdims=True)


def spread_tokens(value):
    count = lax.axis_size("tp_1")
    blocks = jnp.broadcast_to(value, (count,) + value.shape)
    return lax.all_to_all(blocks, "tp_1", 0, 0, tiled=True).reshape(-1, value.shape[1])


def pass_tokens(value):
    count = lax.axis_size("tp_1")
    blocks = [value]
    for shift in range(1, count):
        pairs = [(i, (i + shift) % count) for i in range(count)]
        blocks.append(lax.ppermute(value, "tp_1", pairs))
    return blocks


def pick_matrix(picks, total_rows):
    columns = lax.broadcasted_iota(jnp.int32, (picks.shape[0], total_rows), 1)
    return (picks[:, None] == columns).astype(jnp.float32)


def select_rows(picks, field):
    return jnp.dot(pick_matrix(picks, field.shape[0]), field, precision=lax.Precision.HIGHEST)


def place_rows(picks, values, total_rows):
    matrix = pick_matrix(picks, total_rows)
    return lax.dot_general(
        matrix, values, (((0,), (0,)), ((), ())), precision=lax.Precision.HIGHEST
    )


def neighbour_picks(row_picks):
    count = lax.axis_size(BLK)
    rank = lax.axis_index(BLK)
    near = rank + 1 - 2 * (rank % 2)
    far = (rank - 1 + 2 * (rank % 2) + count) % count
    return [
        lax.dynamic_index_in_dim(row_picks, place, 0, keepdims=False) for place in (rank, near, far)
    ]


def mix_stream(received, picks, total_rows):
    return place_rows(jnp.concatenate(picks), received, total_rows) / 3.0


def gap_rows(mixed_new, copies_new):
    gap_value = mixed_new.astype(jnp.float32) - copies_new.astype(jnp.float32)
    return jnp.sum(gap_value * gap_value, axis=0, keepdims=True)


def consensus_of(partial_sums, width):
    total_sum = jnp.sum(spread_sum(partial_sums, ("blk_1", "tp_0")))
    return total_sum / float(lax.axis_size(BLK) * width * width)


def image_starts(ids):
    marks = lax.broadcasted_iota(jnp.int32, (8, ids.shape[0]), 0)
    return jnp.sum((ids[None, :] < marks).astype(jnp.int32), axis=1)


def gradient_kernel(
    spots,
    starts,
    picks,
    own,
    other_0,
    other_1,
    other_2,
    other_3,
    query_weight,
    key_weight,
    value_weight,
    out_grad,
    tracker,
    tracker_copy,
    tracker_mixed,
    grad_prev,
    grad_new,
    tracker_new,
    tracker_copy_new,
    update,
    kept,
    joined,
    tokens,
    projected,
    total,
    change,
):
    width = query_weight.shape[1]
    rows = tokens.shape[0]
    joined[:, :width] = query_weight[...]
    joined[:, width : 2 * width] = key_weight[...]
    joined[:, 2 * width :] = value_weight[...]

    def project(block, place):
        size = block.shape[0]
        tokens[pl.ds(place, size), :] = block
        result = jnp.dot(block, joined[...], preferred_element_type=jnp.float32)
        projected[pl.ds(place, size), :] = result.astype(jnp.bfloat16)

    for part in range(own.shape[0] // WINDOW):
        place = pl.multiple_of(spots[0] + part * WINDOW, WINDOW)
        project(own[part * WINDOW : (part + 1) * WINDOW, :], place)
    for index, block in enumerate((other_0, other_1, other_2, other_3)):
        project(block[...], pl.multiple_of(spots[1 + index], 128))
    total[...] = jnp.zeros_like(total)

    lane = lax.broadcasted_iota(jnp.int32, (1, width), 1)
    first_head = (lane < HD).astype(jnp.float32).astype(jnp.bfloat16)
    second_head = (lane >= HD).astype(jnp.float32).astype(jnp.bfloat16)
    scale = HD ** (-0.5)

    @pl.loop(0, IMAGES)
    def _(image):
        start = starts[image]
        end = starts[image + 1]
        base = pl.multiple_of(jnp.minimum((start // 16) * 16, rows - WINDOW), 16)
        window = pl.ds(base, WINDOW)
        query = projected[window, :width] * scale
        keyed = projected[window, width : 2 * width]
        valued = projected[window, 2 * width :]
        given = out_grad[window, :]
        queries = jnp.concatenate([query * first_head, query * second_head], axis=0)
        givens = jnp.concatenate([given * first_head, given * second_head], axis=0)
        over_columns = (((1,), (1,)), ((), ()))
        over_rows = (((0,), (0,)), ((), ()))
        scores = lax.dot_general(keyed, queries, over_columns, preferred_element_type=jnp.float32)
        out_proj = lax.dot_general(valued, givens, over_columns, preferred_element_type=jnp.float32)
        row = lax.broadcasted_iota(jnp.int32, scores.shape, 0) + base
        scores = jnp.where((row >= start) & (row < end), scores, -1e30)
        exponent = jnp.exp(scores - jnp.max(scores, axis=0, keepdims=True))
        inverse = 1.0 / jnp.sum(exponent, axis=0, keepdims=True)
        centre = jnp.sum(exponent * out_proj, axis=0, keepdims=True) * inverse
        score_grad = ((exponent * (inverse * scale)) * (out_proj - centre)).astype(jnp.bfloat16)
        both = lax.dot_general(keyed, score_grad, over_rows, preferred_element_type=jnp.float32)
        query_grad = jnp.concatenate([both[:HD, :WINDOW], both[HD:, WINDOW:]], axis=0)
        column = lax.broadcasted_iota(jnp.int32, query_grad.shape, 1) + base
        query_grad = jnp.where((column >= start) & (column < end), query_grad, 0.0)
        total[...] += jnp.dot(
            query_grad.astype(jnp.bfloat16), tokens[window, :], preferred_element_type=jnp.float32
        )

    gradient = (total[...].T * rows ** (-0.5)).astype(jnp.bfloat16)
    grad_new[...] = gradient
    copy_value = tracker_copy[...].astype(jnp.float32)
    fresh = (
        tracker[...].astype(jnp.float32)
        + mixing_rate * (tracker_mixed[...].astype(jnp.float32) - copy_value)
        + gradient.astype(jnp.float32)
        - grad_prev[...].astype(jnp.float32)
    ).astype(jnp.bfloat16)
    tracker_new[...] = fresh
    change[...] = fresh.astype(jnp.float32) - copy_value
    update[...] = jnp.zeros_like(update)
    for index in range(picks.shape[0]):
        place = picks[index]
        row = change[pl.ds(place, 1), :]
        kept[pl.ds(index, 1), :] = row
        update[pl.ds(place, 1), :] = row
    tracker_copy_new[...] = (copy_value + update[...]).astype(jnp.bfloat16)


def gradient_step(spots, starts, picks, *arrays):
    rows, width = arrays[8].shape
    depth = arrays[0].shape[1]
    scalars = [pl.BlockSpec(memory_space=pltpu.SMEM)] * 3
    whole = pl.BlockSpec(memory_space=pltpu.VMEM)
    narrow = jax.ShapeDtypeStruct((rows, width), jnp.bfloat16)
    return pl.pallas_call(
        gradient_kernel,
        out_shape=(
            narrow,
            narrow,
            narrow,
            jax.ShapeDtypeStruct((rows, width), jnp.float32),
            jax.ShapeDtypeStruct((picks.shape[0], width), jnp.float32),
        ),
        in_specs=scalars + [whole] * len(arrays),
        out_specs=(whole,) * 5,
        scratch_shapes=[
            pltpu.VMEM((depth, 3 * width), jnp.bfloat16),
            pltpu.VMEM((rows, depth), jnp.bfloat16),
            pltpu.VMEM((rows, 3 * width), jnp.bfloat16),
            pltpu.VMEM((width, depth), jnp.float32),
            pltpu.VMEM((rows, width), jnp.float32),
        ],
        compiler_params=pltpu.CompilerParams(vmem_limit_bytes=28 * 2**20),
        cost_estimate=pl.CostEstimate(
            flops=2 * 10**9, bytes_accessed=8 * 10**6, transcendentals=8 * 10**5
        ),
    )(spots, starts, picks, *arrays)


def mix_kernel(near_picks, far_picks, near, far, update, mixed, mixed_new, total):
    total[...] = update[...]
    for picks, values in ((near_picks, near), (far_picks, far)):
        for low in range(0, picks.shape[0], 8):
            places = [pl.ds(picks[low + step], 1) for step in range(8)]
            sums = [
                total[place, :] + values[low + step : low + step + 1, :]
                for step, place in enumerate(places)
            ]
            for place, row in zip(places, sums):
                total[place, :] = row
    mixed_new[...] = (mixed[...].astype(jnp.float32) + total[...] / 3.0).astype(jnp.bfloat16)


def mix_step(near_picks, far_picks, *arrays):
    scalars = [pl.BlockSpec(memory_space=pltpu.SMEM)] * 2
    whole = pl.BlockSpec(memory_space=pltpu.VMEM)
    rows, width = arrays[3].shape
    return pl.pallas_call(
        mix_kernel,
        out_shape=jax.ShapeDtypeStruct((rows, width), jnp.bfloat16),
        in_specs=scalars + [whole] * len(arrays),
        out_specs=whole,
        scratch_shapes=[pltpu.VMEM((rows, width), jnp.float32)],
        compiler_params=pltpu.CompilerParams(vmem_limit_bytes=8 * 2**20),
        cost_estimate=pl.CostEstimate(flops=10**6, bytes_accessed=10**6, transcendentals=0),
    )(near_picks, far_picks, *arrays)


def per_device(
    weights,
    copies,
    copies_mixed,
    tracker,
    tracker_copy,
    tracker_mixed,
    grad_prev,
    tokens,
    image_ids,
    key_weight,
    value_weight,
    out_grad,
    row_picks,
):
    model_width = weights.shape[1]
    high = lax.axis_index("tp_0")
    place = lax.axis_index("tp_1")
    height = tokens.shape[1]
    half = height * lax.axis_size("tp_1")
    other = lax.ppermute(tokens[0], "tp_0", [(0, 1), (1, 0)])
    own_half = spread_tokens(tokens[0])
    picks = neighbour_picks(row_picks)
    own_picks = picks[0]
    copy_value = copies[0].astype(jnp.float32)
    mixed_value = copies_mixed[0].astype(jnp.float32)
    weights_new = (
        weights[0]
        + mixing_rate * (mixed_value - copy_value)
        - step_rate * tracker[0].astype(jnp.float32)
    )
    param_values = select_rows(own_picks[0], weights_new - copy_value)
    copies_new = (copy_value + place_rows(own_picks[0], param_values, model_width)).astype(
        jnp.bfloat16
    )
    param_sent = param_values.astype(jnp.bfloat16)
    param_received = jnp.concatenate((param_sent,) + swaps(param_sent), axis=0).astype(jnp.float32)
    mixed_new = (mixed_value + mix_stream(param_received, [own[0] for own in picks], model_width)).astype(
        jnp.bfloat16
    )
    partial_sums = gap_rows(mixed_new, copies_new)
    own_half, other, partial_sums = lax.optimization_barrier((own_half, other, partial_sums))
    blocks = pass_tokens(other)
    partial_sums = spread_sum(partial_sums, ("blk_0", "blk_2", "tp_1"))
    consensus = consensus_of(partial_sums, model_width)
    spots = [high * half] + [
        (1 - high) * half + ((place - shift) % len(blocks)) * height for shift in range(len(blocks))
    ]
    query_weight = (weights_new * model_width ** (-0.5)).astype(jnp.bfloat16)
    grad_new, tracker_new, tracker_copy_new, update, tracker_values = gradient_step(
        jnp.stack(spots).astype(jnp.int32),
        image_starts(image_ids[0]),
        own_picks[1],
        own_half,
        *blocks,
        query_weight,
        key_weight,
        value_weight,
        out_grad[0],
        tracker[0],
        tracker_copy[0],
        tracker_mixed[0],
        grad_prev[0],
    )
    near, far = swaps(tracker_values)
    tracker_mixed_new = mix_step(picks[1][1], picks[2][1], near, far, update, tracker_mixed[0])
    return (
        weights_new[None],
        copies_new[None],
        mixed_new[None],
        tracker_new[None],
        tracker_copy_new[None],
        tracker_mixed_new[None],
        grad_new[None],
        consensus,
    )


def solution(mesh):
    finer = Mesh(mesh.devices.reshape(4, 8, 2, 2, 4), ("blk_0", "blk_1", "blk_2", "tp_0", "tp_1"))
    in_specs = (
        P(BLK, None, TP),
        P(BLK, None, TP),
        P(BLK, None, TP),
        P(BLK, None, TP),
        P(BLK, None, TP),
        P(BLK, None, TP),
        P(BLK, None, TP),
        P(BLK, TP, None),
        P(BLK, None),
        P(None, TP),
        P(None, TP),
        P(BLK, None, TP),
        P(),
    )
    out_specs = (
        P(BLK, None, TP),
        P(BLK, None, TP),
        P(BLK, None, TP),
        P(BLK, None, TP),
        P(BLK, None, TP),
        P(BLK, None, TP),
        P(BLK, None, TP),
        P(),
    )
    return jax.shard_map(
        per_device, mesh=finer, in_specs=in_specs, out_specs=out_specs, check_vma=False
    )
```

time: 134 us -> 115 us (0.86)
  the two profiles are of different devices: /device:TPU:1 before, /device:TPU:8 now
where the time goes in v2:
time: 115 us
  starting transfers between devices  74.6 us (65%)
  waiting for transfers between devices  13.4 us (12%)
  Pallas kernels  9.97 us (9%)
  local copies, waits for them, and re-layouts  7.1 us (6%)
  matrix products  3.75 us (3%)
  other arithmetic  3.15 us (3%)
  between operations  2.78 us (2%)
    ppermute x4, starting transfers between devices, swaps(): return (lax.ppermute(value, BLK, near), lax.ppermute(value, BLK, far))  30.4 us
    all_to_all x2, starting transfers between devices, spread_sum(): received = lax.all_to_all(rows, axes, 0, 0, tiled=True)  20.5 us
    ppermute x3, starting transfers between devices, pass_tokens(): blocks.append(lax.ppermute(value, 'tp_1', pairs))  10.4 us
    pallas_call x1, Pallas kernels, gradient_step(): pl.pallas_call(gradient_kernel, out_shape=(narrow, narrow, narrow, jax.Sh...  8.43 us
    ppermute x1, starting transfers between devices, per_device(): other = lax.ppermute(tokens[0], 'tp_0', [(0, 1), (1, 0)])  8.22 us
    all_to_all x1, waiting for transfers between devices, spread_tokens(): lax.all_to_all(blocks, 'tp_1', 0, 0, tiled=True).reshape(-1, value.shape[1])  6.46 us
    all_to_all x2, waiting for transfers between devices, spread_sum(): received = lax.all_to_all(rows, axes, 0, 0, tiled=True)  5.76 us
    all_to_all x1, starting transfers between devices, spread_tokens(): lax.all_to_all(blocks, 'tp_1', 0, 0, tiled=True).reshape(-1, value.shape[1])  5.04 us
  transfers between devices with their start and end apart: 11, of which 4 were waited for; matrix products, arithmetic and copies ran while one was open for 7% of the time, Pallas kernels for 7%

profile of v2, /device:TPU:8, one launch (start us, length us, event | category | flops | bytes accessed | tf_op | source)
XLA Modules:
  0.0 114.7 jit_solution(11682296236600677690)
XLA Ops:
  0.7 0.7 constant_dynamic-slice_fusion.1
  1.4 1.8 %fusion.26 = (bf16[64,128]{1,0:T(8,128)(2,1)S(1)}, f32[64,128]{1,0:T(8,128)S(1)}) fusion(bf16[1,1024,128]{2,1,0:T(8,128)(2,1)} %param.14, bf16[1,1024,128]{2,1,0:T(8,128)(2,1)} %param.15, f32[1,1024,128]{2,1,0:T(8,128)} %param.13, bf16[1,1024,128]{2,1,0:T(8,128)(2,1)} %param.16, s32[64]{0:T(128)S(1)} %get-tuple-element.32), kind=kOutput, calls=%fused_computation.45 | convolution fusion | flops 101916672 | bytes 1360128 | tf_op jit(solution)/shard_map/dot_general | solution.py:55
  3.2 1.9 %collective-permute-start = (bf16[64,128]{1,0:T(8,128)(2,1)S(1)}, bf16[64,128]{1,0:T(8,128)(2,1)S(1)}, u32[]{:S(2)}, u32[]{:S(2)}) collective-permute-start(bf16[64,128]{1,0:T(8,128)(2,1)S(1)} %get-tuple-element.33), channel_id=1, source_target_pairs={{0,8},{8,0},{16,24},{24,16},{32,40},{40,32},{48,56},{56,48},{64,72... | collective-permute-start | bytes 49160 | tf_op jit(solution)/shard_map/ppermute | solution.py:24
  5.1 15.5 %collective-permute-start.1 = (bf16[64,128]{1,0:T(8,128)(2,1)S(1)}, bf16[64,128]{1,0:T(8,128)(2,1)S(1)}, u32[]{:S(2)}, u32[]{:S(2)}) collective-permute-start(bf16[64,128]{1,0:T(8,128)(2,1)S(1)} %get-tuple-element.33), channel_id=1, source_target_pairs={{0,504},{8,16},{16,8},{24,32},{32,24},{40,48},{48,40},{56,64},{64,... | collective-permute-start | bytes 49160 | tf_op jit(solution)/shard_map/ppermute | solution.py:24
  20.6 8.2 %collective-permute-start.2 = (bf16[128,1024]{1,0:T(8,128)(2,1)S(1)}, bf16[128,1024]{1,0:T(8,128)(2,1)S(1)}, u32[]{:S(2)}, u32[]{:S(2)}) collective-permute-start(bf16[128,1024]{1,0:T(8,128)(2,1)S(1)} %bitcast.100), channel_id=1, source_target_pairs={{0,4},{4,0},{1,5},{5,1},{2,6},{6,2},{3,7},{7,3},{8,12},{12,8},{9,1... | collective-permute-start | bytes 786440 | tf_op jit(solution)/shard_map/ppermute | solution.py:276
  28.8 1.1 broadcast_in_dim.40
  30.0 5.0 %all-to-all-start = ((bf16[4,128,1024]{2,1,0:T(8,128)(2,1)}), bf16[4,128,1024]{2,1,0:T(8,128)(2,1)S(1)}, u32[]{:S(2)}, u32[]{:S(2)}) async-start(bf16[4,128,1024]{2,1,0:T(8,128)(2,1)} %broadcast_in_dim.40), calls=%async_computation | async-start | bytes 2097152 | tf_op jit(solution)/shard_map/all_to_all | solution.py:37
  35.0 0.1 pad_add_fusion
  35.1 0.0 collective-permute-done
  35.1 0.0 collective-permute-done.1
  35.1 0.6 fusion.1
  35.7 0.0 copy-start.18
  35.7 0.3 copy-done.12
  36.0 1.4 %multiply_reduce_fusion = (f32[128]{0:T(128)S(1)}, bf16[1024,128]{1,0:T(8,128)(2,1)}) fusion(bf16[1024,128]{1,0:T(8,128)(2,1)S(1)} %fusion.1, f32[64,128]{1,0:T(8,128)S(1)} %get-tuple-element.34, s32[64]{0:T(128)S(1)} %get-tuple-element.32, bf16[1,1024,128]{2,1,0:T(8,128)(2,1)S(1)} %copy-done.12), kind=kOutput, calls=%fused_computation.19 | convolution fusion | flops 101777280 | bytes 819968 | tf_op jit(solution)/shard_map/dot_general | solution.py:60
  37.4 0.0 copy-done.18
  37.4 0.6 collective-permute-done.2.other_0
  38.0 6.5 %all-to-all-done = bf16[4,128,1024]{2,1,0:T(8,128)(2,1)S(1)} async-done(((bf16[4,128,1024]{2,1,0:T(8,128)(2,1)}), bf16[4,128,1024]{2,1,0:T(8,128)(2,1)S(1)}, u32[]{:S(2)}, u32[]{:S(2)}) %all-to-all-start) | async-done | bytes 1048608 | tf_op jit(solution)/shard_map/all_to_all | solution.py:37
  44.5 0.0 copy-start.5
  44.5 2.4 %collective-permute-start.3 = (bf16[128,1024]{1,0:T(8,128)(2,1)S(1)}, bf16[128,1024]{1,0:T(8,128)(2,1)S(1)}, u32[]{:S(2)}, u32[]{:S(2)}) collective-permute-start(bf16[128,1024]{1,0:T(8,128)(2,1)S(1)} %collective-permute-done.2.other_0), channel_id=1, source_target_pairs={{0,1},{1,2},{2,3},{3,0},{4,5},{5,6},{6,7},{7,4},{8,9},{9,10},{10,1... | collective-permute-start | bytes 786440 | tf_op jit(solution)/shard_map/ppermute | solution.py:45
  46.9 6.1 %collective-permute-start.4 = (bf16[128,1024]{1,0:T(8,128)(2,1)S(1)}, bf16[128,1024]{1,0:T(8,128)(2,1)}, u32[]{:S(2)}, u32[]{:S(2)}) collective-permute-start(bf16[128,1024]{1,0:T(8,128)(2,1)S(1)} %collective-permute-done.2.other_0), channel_id=1, source_target_pairs={{0,2},{1,3},{2,0},{3,1},{4,6},{5,7},{6,4},{7,5},{8,10},{9,11},{10,... | collective-permute-start | bytes 786440 | tf_op jit(solution)/shard_map/ppermute | solution.py:45
  53.0 1.9 %collective-permute-start.5 = (bf16[128,1024]{1,0:T(8,128)(2,1)S(1)}, bf16[128,1024]{1,0:T(8,128)(2,1)}, u32[]{:S(2)}, u32[]{:S(2)}) collective-permute-start(bf16[128,1024]{1,0:T(8,128)(2,1)S(1)} %collective-permute-done.2.other_0), channel_id=1, source_target_pairs={{0,3},{1,0},{2,1},{3,2},{4,7},{5,4},{6,5},{7,6},{8,11},{9,8},{10,9... | collective-permute-start | bytes 786440 | tf_op jit(solution)/shard_map/ppermute | solution.py:45
  54.9 0.0 copy-start.17
  54.9 1.4 %multiply_convert_fusion.query_weight = bf16[1024,128]{1,0:T(8,128)(2,1)S(1)} fusion(bf16[1,1024,128]{2,1,0:T(8,128)(2,1)} %param.14, bf16[1,1024,128]{2,1,0:T(8,128)(2,1)} %param.15, f32[1,1024,128]{2,1,0:T(8,128)} %param.13, bf16[1,1024,128]{2,1,0:T(8,128)(2,1)S(1)} %copy-done), kind=kLoop, calls=%fused_computation.18 | loop fusion | flops 1310720 | bytes 1572864 | tf_op jit(solution)/shard_map/convert_element_type | solution.py:304
  56.3 0.6 broadcast_in_dim.46
  56.9 6.1 %all-to-all-start.1 = ((f32[32,1,128]{2,1,0:T(1,128)}), f32[32,1,128]{2,1,0:T(1,128)S(1)}, u32[]{:S(2)}, u32[]{:S(2)}) async-start(f32[32,1,128]{2,1,0:T(1,128)} %broadcast_in_dim.46), calls=%async_computation.1 | async-start | bytes 32768 | tf_op jit(solution)/shard_map/all_to_all | solution.py:30
  63.1 0.1 convert_reduce_fusion.starts
  63.3 0.1 stack.23.spots
  63.4 5.8 %all-to-all-done.1 = f32[32,1,128]{2,1,0:T(1,128)S(1)} async-done(((f32[32,1,128]{2,1,0:T(1,128)}), f32[32,1,128]{2,1,0:T(1,128)S(1)}, u32[]{:S(2)}, u32[]{:S(2)}) %all-to-all-start.1) | async-done | bytes 16416 | tf_op jit(solution)/shard_map/all_to_all | solution.py:30
  69.1 0.6 broadcast_in_dim.47
  69.7 14.4 %all-to-all-start.2 = ((f32[16,1,128]{2,1,0:T(1,128)}), f32[16,1,128]{2,1,0:T(1,128)S(1)}, u32[]{:S(2)}, u32[]{:S(2)}) async-start(f32[16,1,128]{2,1,0:T(1,128)} %broadcast_in_dim.47), calls=%async_computation.2 | async-start | bytes 16384 | tf_op jit(solution)/shard_map/all_to_all | solution.py:30
  84.1 0.0 collective-permute-done.3.other_1
  84.1 0.0 copy-start.9
  84.1 0.7 copy-done.9
  84.8 0.0 collective-permute-done.4.other_2
  84.8 0.0 collective-permute-done.5.other_3
  84.9 0.0 copy-start.6
  84.9 0.9 copy-done.6
  85.8 0.9 copy-done.8
  86.8 0.9 copy-done.10
  87.8 8.4 %shard_map.188 = (bf16[1024,128]{1,0:T(8,128)(2,1)}, bf16[1024,128]{1,0:T(8,128)(2,1)}, bf16[1024,128]{1,0:T(8,128)(2,1)}, f32[1024,128]{1,0:T(8,128)S(1)}, f32[64,128]{1,0:T(8,128)S(1)}) custom-call(s32[5]{0:T(128)S(1)} %stack.23.spots, s32[8]{0:T(128)S(1)} %convert_reduce_fusion.starts, s32[64]{0:T(128)S(1)} %get-tuple-element.31.picks, ...), custom_call_target="tpu_custom_call" | custom-call | flops 2000000000 | bytes 8000000 | tf_op jit(solution)/shard_map/pallas_call | solution.py:202
  96.2 1.9 %collective-permute-start.6 = (f32[64,128]{1,0:T(8,128)S(1)}, f32[64,128]{1,0:T(8,128)S(1)}, u32[]{:S(2)}, u32[]{:S(2)}) collective-permute-start(f32[64,128]{1,0:T(8,128)S(1)} %get-tuple-element.20), channel_id=1, source_target_pairs={{0,8},{8,0},{16,24},{24,16},{32,40},{40,32},{48,56},{56,48},{64,72... | collective-permute-start | bytes 98312 | tf_op jit(solution)/shard_map/ppermute | solution.py:24
  98.1 11.1 %collective-permute-start.7 = (f32[64,128]{1,0:T(8,128)S(1)}, f32[64,128]{1,0:T(8,128)S(1)}, u32[]{:S(2)}, u32[]{:S(2)}) collective-permute-start(f32[64,128]{1,0:T(8,128)S(1)} %get-tuple-element.20), channel_id=1, source_target_pairs={{0,504},{8,16},{16,8},{24,32},{32,24},{40,48},{48,40},{56,64},{64,... | collective-permute-start | bytes 98312 | tf_op jit(solution)/shard_map/ppermute | solution.py:24
  109.3 0.9 fusion.12
  110.2 0.0 all-to-all-done.2
  110.2 0.6 reduce_sum.43
  111.5 0.0 collective-permute-done.6.near
  111.5 0.6 collective-permute-done.7.far
  112.0 1.5 %shard_map.189 = bf16[1024,128]{1,0:T(8,128)(2,1)} custom-call(s32[64]{0:T(128)S(1)} %get-tuple-element.38.near_picks, s32[64]{0:T(128)S(1)} %get-tuple-element.27.far_picks, f32[64,128]{1,0:T(8,128)S(1)} %collective-permute-done.6.near, f32[64,128]{1,0:T(8,128)S(1)} %collective-permute-done.7.far, f32[1024,128]{1,0:T(8,128)S(1)} %get-tuple-element.21.update, ...), custom_call_target="tpu_custom_call" | custom-call | flops 1000000 | bytes 1000000 | tf_op jit(solution)/shard_map/pallas_call | solution.py:245
  (30 shorter events, 0.1 us)
Async XLA Ops:
  1.4 19.2 %copy-start.16 = (bf16[1,128,1024]{2,1,0:T(8,128)(2,1)S(1)}, bf16[1,128,1024]{2,1,0:T(8,128)(2,1)}, u32[]{:S(2)}) copy-start(bf16[1,128,1024]{2,1,0:T(8,128)(2,1)} %param.20) | copy-start | bytes 786436
  3.2 31.9 %collective-permute-start = (bf16[64,128]{1,0:T(8,128)(2,1)S(1)}, bf16[64,128]{1,0:T(8,128)(2,1)S(1)}, u32[]{:S(2)}, u32[]{:S(2)}) collective-permute-start(bf16[64,128]{1,0:T(8,128)(2,1)S(1)} %get-tuple-element.33), channel_id=1, source_target_pairs={{0,8},{8,0},{16,24},{24,16},{32,40},{40,32},{48,56},{56,48},{64,72... | collective-permute-start | bytes 49160 | tf_op jit(solution)/shard_map/ppermute | solution.py:24
  5.1 30.0 %collective-permute-start.1 = (bf16[64,128]{1,0:T(8,128)(2,1)S(1)}, bf16[64,128]{1,0:T(8,128)(2,1)S(1)}, u32[]{:S(2)}, u32[]{:S(2)}) collective-permute-start(bf16[64,128]{1,0:T(8,128)(2,1)S(1)} %get-tuple-element.33), channel_id=1, source_target_pairs={{0,504},{8,16},{16,8},{24,32},{32,24},{40,48},{48,40},{56,64},{64,... | collective-permute-start | bytes 49160 | tf_op jit(solution)/shard_map/ppermute | solution.py:24
  20.6 17.4 %collective-permute-start.2 = (bf16[128,1024]{1,0:T(8,128)(2,1)S(1)}, bf16[128,1024]{1,0:T(8,128)(2,1)S(1)}, u32[]{:S(2)}, u32[]{:S(2)}) collective-permute-start(bf16[128,1024]{1,0:T(8,128)(2,1)S(1)} %bitcast.100), channel_id=1, source_target_pairs={{0,4},{4,0},{1,5},{5,1},{2,6},{6,2},{3,7},{7,3},{8,12},{12,8},{9,1... | collective-permute-start | bytes 786440 | tf_op jit(solution)/shard_map/ppermute | solution.py:276
  30.0 5.1 %copy-start.14 = (bf16[1,1024,128]{2,1,0:T(8,128)(2,1)S(1)}, bf16[1,1024,128]{2,1,0:T(8,128)(2,1)}, u32[]{:S(2)}) copy-start(bf16[1,1024,128]{2,1,0:T(8,128)(2,1)} %param.15) | copy-start | bytes 786436
  30.0 14.5 %all-to-all-start = ((bf16[4,128,1024]{2,1,0:T(8,128)(2,1)}), bf16[4,128,1024]{2,1,0:T(8,128)(2,1)S(1)}, u32[]{:S(2)}, u32[]{:S(2)}) async-start(bf16[4,128,1024]{2,1,0:T(8,128)(2,1)} %broadcast_in_dim.40), calls=%async_computation | async-start | bytes 2097152 | tf_op jit(solution)/shard_map/all_to_all | solution.py:37
  35.1 0.9 copy-start.12
  35.7 1.7 %copy-start.18 = (bf16[1024,128]{1,0:T(8,128)(2,1)}, bf16[1024,128]{1,0:T(8,128)(2,1)S(1)}, u32[]{:S(2)}) copy-start(bf16[1024,128]{1,0:T(8,128)(2,1)S(1)} %fusion.1) | copy-start | bytes 786436
  36.0 18.9 %copy-start = (bf16[1,1024,128]{2,1,0:T(8,128)(2,1)S(1)}, bf16[1,1024,128]{2,1,0:T(8,128)(2,1)}, u32[]{:S(2)}) copy-start(bf16[1,1024,128]{2,1,0:T(8,128)(2,1)} %param.16) | copy-start | bytes 786436
  38.0 18.3 %copy-start.7 = (bf16[128,1024]{1,0:T(8,128)(2,1)}, bf16[128,1024]{1,0:T(8,128)(2,1)S(1)}, u32[]{:S(2)}) copy-start(bf16[128,1024]{1,0:T(8,128)(2,1)S(1)} %collective-permute-done.2.other_0) | copy-start | bytes 786436
  44.4 40.4 %copy-start.1 = (bf16[1,1024,128]{2,1,0:T(8,128)(2,1)S(1)}, bf16[1,1024,128]{2,1,0:T(8,128)(2,1)}, u32[]{:S(2)}) copy-start(bf16[1,1024,128]{2,1,0:T(8,128)(2,1)} %param.18) | copy-start | bytes 786436
  44.5 40.4 %copy-start.2 = (bf16[1024,128]{1,0:T(8,128)(2,1)S(1)}, bf16[1024,128]{1,0:T(8,128)(2,1)}, u32[]{:S(2)}) copy-start(bf16[1024,128]{1,0:T(8,128)(2,1)} %key_weight.1) | copy-start | bytes 786436
  44.5 40.4 %copy-start.3 = (bf16[1024,128]{1,0:T(8,128)(2,1)S(1)}, bf16[1024,128]{1,0:T(8,128)(2,1)}, u32[]{:S(2)}) copy-start(bf16[1024,128]{1,0:T(8,128)(2,1)} %value_weight.1) | copy-start | bytes 786436
  44.5 40.4 %copy-start.4 = (bf16[1,1024,128]{2,1,0:T(8,128)(2,1)S(1)}, bf16[1,1024,128]{2,1,0:T(8,128)(2,1)}, u32[]{:S(2)}) copy-start(bf16[1,1024,128]{2,1,0:T(8,128)(2,1)} %param.24) | copy-start | bytes 786436
  44.5 40.4 %copy-start.5 = (bf16[1,1024,128]{2,1,0:T(8,128)(2,1)S(1)}, bf16[1,1024,128]{2,1,0:T(8,128)(2,1)}, u32[]{:S(2)}) copy-start(bf16[1,1024,128]{2,1,0:T(8,128)(2,1)} %param.17) | copy-start | bytes 786436
  44.5 39.7 %collective-permute-start.3 = (bf16[128,1024]{1,0:T(8,128)(2,1)S(1)}, bf16[128,1024]{1,0:T(8,128)(2,1)S(1)}, u32[]{:S(2)}, u32[]{:S(2)}) collective-permute-start(bf16[128,1024]{1,0:T(8,128)(2,1)S(1)} %collective-permute-done.2.other_0), channel_id=1, source_target_pairs={{0,1},{1,2},{2,3},{3,0},{4,5},{5,6},{6,7},{7,4},{8,9},{9,10},{10,1... | collective-permute-start | bytes 786440 | tf_op jit(solution)/shard_map/ppermute | solution.py:45
  46.9 38.0 %collective-permute-start.4 = (bf16[128,1024]{1,0:T(8,128)(2,1)S(1)}, bf16[128,1024]{1,0:T(8,128)(2,1)}, u32[]{:S(2)}, u32[]{:S(2)}) collective-permute-start(bf16[128,1024]{1,0:T(8,128)(2,1)S(1)} %collective-permute-done.2.other_0), channel_id=1, source_target_pairs={{0,2},{1,3},{2,0},{3,1},{4,6},{5,7},{6,4},{7,5},{8,10},{9,11},{10,... | collective-permute-start | bytes 786440 | tf_op jit(solution)/shard_map/ppermute | solution.py:45
  53.0 31.9 %collective-permute-start.5 = (bf16[128,1024]{1,0:T(8,128)(2,1)S(1)}, bf16[128,1024]{1,0:T(8,128)(2,1)}, u32[]{:S(2)}, u32[]{:S(2)}) collective-permute-start(bf16[128,1024]{1,0:T(8,128)(2,1)S(1)} %collective-permute-done.2.other_0), channel_id=1, source_target_pairs={{0,3},{1,0},{2,1},{3,2},{4,7},{5,4},{6,5},{7,6},{8,11},{9,8},{10,9... | collective-permute-start | bytes 786440 | tf_op jit(solution)/shard_map/ppermute | solution.py:45
  54.9 8.2 %copy-start.17 = (s32[1,1024]{1,0:T(1,128)S(1)}, s32[1,1024]{1,0:T(1,128)}, u32[]{:S(2)}) copy-start(s32[1,1024]{1,0:T(1,128)} %param.21) | copy-start | bytes 12292
  56.9 12.2 %all-to-all-start.1 = ((f32[32,1,128]{2,1,0:T(1,128)}), f32[32,1,128]{2,1,0:T(1,128)S(1)}, u32[]{:S(2)}, u32[]{:S(2)}) async-start(f32[32,1,128]{2,1,0:T(1,128)} %broadcast_in_dim.46), calls=%async_computation.1 | async-start | bytes 32768 | tf_op jit(solution)/shard_map/all_to_all | solution.py:30
  69.7 40.5 %all-to-all-start.2 = ((f32[16,1,128]{2,1,0:T(1,128)}), f32[16,1,128]{2,1,0:T(1,128)S(1)}, u32[]{:S(2)}, u32[]{:S(2)}) async-start(f32[16,1,128]{2,1,0:T(1,128)} %broadcast_in_dim.47), calls=%async_computation.2 | async-start | bytes 16384 | tf_op jit(solution)/shard_map/all_to_all | solution.py:30
  84.1 0.7 copy-start.9
  84.9 1.0 copy-start.6
  85.8 0.9 copy-start.8
  86.8 0.9 copy-start.10
  87.7 21.5 %copy-start.11 = (f32[1,1024,128]{2,1,0:T(8,128)S(1)}, f32[1,1024,128]{2,1,0:T(8,128)}, u32[]{:S(2)}) copy-start(f32[1,1024,128]{2,1,0:T(8,128)} %param.13) | copy-start | bytes 1572868
  87.8 21.5 %copy-start.13 = (bf16[1,1024,128]{2,1,0:T(8,128)(2,1)S(1)}, bf16[1,1024,128]{2,1,0:T(8,128)(2,1)}, u32[]{:S(2)}) copy-start(bf16[1,1024,128]{2,1,0:T(8,128)(2,1)} %param.14) | copy-start | bytes 786436
  87.8 21.5 %copy-start.15 = (bf16[1,1024,128]{2,1,0:T(8,128)(2,1)S(1)}, bf16[1,1024,128]{2,1,0:T(8,128)(2,1)}, u32[]{:S(2)}) copy-start(bf16[1,1024,128]{2,1,0:T(8,128)(2,1)} %param.15) | copy-start | bytes 786436
  96.2 15.3 %collective-permute-start.6 = (f32[64,128]{1,0:T(8,128)S(1)}, f32[64,128]{1,0:T(8,128)S(1)}, u32[]{:S(2)}, u32[]{:S(2)}) collective-permute-start(f32[64,128]{1,0:T(8,128)S(1)} %get-tuple-element.20), channel_id=1, source_target_pairs={{0,8},{8,0},{16,24},{24,16},{32,40},{40,32},{48,56},{56,48},{64,72... | collective-permute-start | bytes 98312 | tf_op jit(solution)/shard_map/ppermute | solution.py:24
  98.1 13.9 %collective-permute-start.7 = (f32[64,128]{1,0:T(8,128)S(1)}, f32[64,128]{1,0:T(8,128)S(1)}, u32[]{:S(2)}, u32[]{:S(2)}) collective-permute-start(f32[64,128]{1,0:T(8,128)S(1)} %get-tuple-element.20), channel_id=1, source_target_pairs={{0,504},{8,16},{16,8},{24,32},{32,24},{40,48},{48,40},{56,64},{64,... | collective-permute-start | bytes 98312 | tf_op jit(solution)/shard_map/ppermute | solution.py:24

commit v3 on v2

--- a/solution.py
+++ b/solution.py
@@ -21,14 +21,18 @@
     count = lax.axis_size(BLK)
     near = [(r, r ^ 1) for r in range(count)]
     far = [(r, (r + 1) % count if r % 2 else (r - 1) % count) for r in range(count)]
-    return lax.ppermute(value, BLK, near), lax.ppermute(value, BLK, far)
-
-
-def spread_sum(value, axes):
+    from_far = lax.ppermute(value, BLK, far)
+    return lax.ppermute(value, BLK, near), from_far
+
+
+def spread_rows(value, axes):
     count = lax.axis_size(axes)
     rows = jnp.broadcast_to(value, (count, value.shape[1]))
-    received = lax.all_to_all(rows, axes, 0, 0, tiled=True)
-    return jnp.sum(received, axis=0, keepdims=True)
+    return lax.all_to_all(rows, axes, 0, 0, tiled=True)
+
+
+def spread_sum(value, axes):
+    return jnp.sum(spread_rows(value, axes), axis=0, keepdims=True)
 
 
 def spread_tokens(value):
@@ -82,7 +86,7 @@
 
 
 def consensus_of(partial_sums, width):
-    total_sum = jnp.sum(spread_sum(partial_sums, ("blk_1", "tp_0")))
+    total_sum = jnp.sum(spread_sum(partial_sums, ("blk_0", "blk_2", "tp_1")))
     return total_sum / float(lax.axis_size(BLK) * width * width)
 
 
@@ -103,11 +107,11 @@
     query_weight,
     key_weight,
     value_weight,
-    out_grad,
-    tracker,
-    tracker_copy,
-    tracker_mixed,
-    grad_prev,
+    out_grad_in,
+    tracker_in,
+    tracker_copy_in,
+    tracker_mixed_in,
+    grad_prev_in,
     grad_new,
     tracker_new,
     tracker_copy_new,
@@ -118,24 +122,52 @@
     projected,
     total,
     change,
+    out_grad,
+    tracker,
+    tracker_copy,
+    tracker_mixed,
+    grad_prev,
+    sems,
 ):
     width = query_weight.shape[1]
     rows = tokens.shape[0]
-    joined[:, :width] = query_weight[...]
-    joined[:, width : 2 * width] = key_weight[...]
-    joined[:, 2 * width :] = value_weight[...]
-
-    def project(block, place):
-        size = block.shape[0]
-        tokens[pl.ds(place, size), :] = block
-        result = jnp.dot(block, joined[...], preferred_element_type=jnp.float32)
-        projected[pl.ds(place, size), :] = result.astype(jnp.bfloat16)
-
+    copies = []
+
+    def fetch(source, target):
+        copy = pltpu.make_async_copy(source, target, sems.at[len(copies)])
+        copy.start()
+        copies.append(copy)
+        return copy
+
+    ready = [
+        fetch(source, joined.at[:, index * width : (index + 1) * width])
+        for index, source in enumerate((query_weight, key_weight, value_weight))
+    ]
+    parts = []
     for part in range(own.shape[0] // WINDOW):
         place = pl.multiple_of(spots[0] + part * WINDOW, WINDOW)
-        project(own[part * WINDOW : (part + 1) * WINDOW, :], place)
-    for index, block in enumerate((other_0, other_1, other_2, other_3)):
-        project(block[...], pl.multiple_of(spots[1 + index], 128))
+        source = own.at[part * WINDOW : (part + 1) * WINDOW, :]
+        parts.append((place, WINDOW, fetch(source, tokens.at[pl.ds(place, WINDOW), :])))
+    for index, source in enumerate((other_0, other_1, other_2, other_3)):
+        size = source.shape[0]
+        place = pl.multiple_of(spots[1 + index], 128)
+        parts.append((place, size, fetch(source, tokens.at[pl.ds(place, size), :])))
+    given_copy = fetch(out_grad_in, out_grad)
+    late = [
+        fetch(tracker_in, tracker),
+        fetch(tracker_copy_in, tracker_copy),
+        fetch(tracker_mixed_in, tracker_mixed),
+        fetch(grad_prev_in, grad_prev),
+    ]
+    for copy in ready:
+        copy.wait()
+    for place, size, copy in parts:
+        copy.wait()
+        result = jnp.dot(
+            tokens[pl.ds(place, size), :], joined[...], preferred_element_type=jnp.float32
+        )
+        projected[pl.ds(place, size), :] = result.astype(jnp.bfloat16)
+    given_copy.wait()
     total[...] = jnp.zeros_like(total)
 
     lane = lax.broadcasted_iota(jnp.int32, (1, width), 1)
@@ -175,6 +207,8 @@
 
     gradient = (total[...].T * rows ** (-0.5)).astype(jnp.bfloat16)
     grad_new[...] = gradient
+    for copy in late:
+        copy.wait()
     copy_value = tracker_copy[...].astype(jnp.float32)
     fresh = (
         tracker[...].astype(jnp.float32)
@@ -208,7 +242,7 @@
             jax.ShapeDtypeStruct((rows, width), jnp.float32),
             jax.ShapeDtypeStruct((picks.shape[0], width), jnp.float32),
         ),
-        in_specs=scalars + [whole] * len(arrays),
+        in_specs=scalars + [pl.BlockSpec(memory_space=pltpu.HBM)] * len(arrays),
         out_specs=(whole,) * 5,
         scratch_shapes=[
             pltpu.VMEM((depth, 3 * width), jnp.bfloat16),
@@ -216,8 +250,10 @@
             pltpu.VMEM((rows, 3 * width), jnp.bfloat16),
             pltpu.VMEM((width, depth), jnp.float32),
             pltpu.VMEM((rows, width), jnp.float32),
-        ],
-        compiler_params=pltpu.CompilerParams(vmem_limit_bytes=28 * 2**20),
+        ]
+        + [pltpu.VMEM((rows, width), jnp.bfloat16)] * 5
+        + [pltpu.SemaphoreType.DMA((14,))],
+        compiler_params=pltpu.CompilerParams(vmem_limit_bytes=56 * 2**20),
         cost_estimate=pl.CostEstimate(
             flops=2 * 10**9, bytes_accessed=8 * 10**6, transcendentals=8 * 10**5
         ),
@@ -294,10 +330,10 @@
         jnp.bfloat16
     )
     partial_sums = gap_rows(mixed_new, copies_new)
-    own_half, other, partial_sums = lax.optimization_barrier((own_half, other, partial_sums))
+    own_half, other = lax.optimization_barrier((own_half, other))
     blocks = pass_tokens(other)
-    partial_sums = spread_sum(partial_sums, ("blk_0", "blk_2", "tp_1"))
-    consensus = consensus_of(partial_sums, model_width)
+    _, partial_sums = lax.optimization_barrier((other, partial_sums))
+    partial_sums = spread_rows(partial_sums, ("blk_1", "tp_0"))
     spots = [high * half] + [
         (1 - high) * half + ((place - shift) % len(blocks)) * height for shift in range(len(blocks))
     ]
@@ -317,7 +353,9 @@
         tracker_mixed[0],
         grad_prev[0],
     )
+    tracker_values, partial_sums = lax.optimization_barrier((tracker_values, partial_sums))
     near, far = swaps(tracker_values)
+    consensus = consensus_of(jnp.sum(partial_sums, axis=0, keepdims=True), model_width)
     tracker_mixed_new = mix_step(picks[1][1], picks[2][1], near, far, update, tracker_mixed[0])
     return (
         weights_new[None],

time: 115 us -> 109 us (0.948)
  the two profiles are of different devices: /device:TPU:8 before, /device:TPU:1 now
where the time goes in v3:
time: 109 us; the launch traced here: 108 us
  starting transfers between devices  71.4 us (66%)
  Pallas kernels  12.3 us (11%)
  waiting for transfers between devices  9.47 us (9%)
  local copies, waits for them, and re-layouts  6.77 us (6%)
  other arithmetic  3.15 us (3%)
  between operations  2.69 us (2%)
  matrix products  2.44 us (2%)
    all_to_all x2, starting transfers between devices, spread_rows(): return lax.all_to_all(rows, axes, 0, 0, tiled=True)  28.8 us
    ppermute x1, starting transfers between devices, per_device(): other = lax.ppermute(tokens[0], 'tp_0', [(0, 1), (1, 0)])  16.3 us
    pallas_call x1, Pallas kernels, gradient_step(): pl.pallas_call(gradient_kernel, out_shape=(narrow, narrow, narrow, jax.Sh...  10.7 us
    ppermute x2, starting transfers between devices, swaps(): return (lax.ppermute(value, BLK, near), from_far)  8.41 us
    ppermute x3, starting transfers between devices, pass_tokens(): blocks.append(lax.ppermute(value, 'tp_1', pairs))  8.4 us
    all_to_all x2, waiting for transfers between devices, spread_rows(): return lax.all_to_all(rows, axes, 0, 0, tiled=True)  5.97 us
    ppermute x2, starting transfers between devices, swaps(): from_far = lax.ppermute(value, BLK, far)  5.25 us
    all_to_all x1, starting transfers between devices, spread_tokens(): lax.all_to_all(blocks, 'tp_1', 0, 0, tiled=True).reshape(-1, value.shape[1])  4.33 us
  transfers between devices with their start and end apart: 11, of which 2 were waited for; matrix products, arithmetic and copies ran while one was open for 10% of the time, Pallas kernels for 10%

profile of v3, /device:TPU:1, one launch (start us, length us, event | category | flops | bytes accessed | tf_op | source)
XLA Modules:
  0.0 108.2 jit_solution(12282813573879696995)
XLA Ops:
  0.6 16.3 %collective-permute-start.2 = (bf16[128,1024]{1,0:T(8,128)(2,1)}, bf16[128,1024]{1,0:T(8,128)(2,1)S(1)}, u32[]{:S(2)}, u32[]{:S(2)}) collective-permute-start(bf16[128,1024]{1,0:T(8,128)(2,1)} %bitcast.97), channel_id=1, source_target_pairs={{0,4},{4,0},{1,5},{5,1},{2,6},{6,2},{3,7},{7,3},{8,12},{12,8},{9,1... | collective-permute-start | bytes 786440 | tf_op jit(solution)/shard_map/ppermute | solution.py:312
  16.9 2.1 %broadcast_in_dim.40 = bf16[4,128,1024]{2,1,0:T(8,128)(2,1)} broadcast(bf16[128,1024]{1,0:T(8,128)(2,1)} %bitcast.98), dimensions={1,2} | broadcast | bytes 1310720 | tf_op jit(solution)/shard_map/broadcast_in_dim | solution.py:40
  19.0 4.3 %all-to-all-start = ((bf16[4,128,1024]{2,1,0:T(8,128)(2,1)}), bf16[4,128,1024]{2,1,0:T(8,128)(2,1)S(1)}, u32[]{:S(2)}, u32[]{:S(2)}) async-start(bf16[4,128,1024]{2,1,0:T(8,128)(2,1)} %broadcast_in_dim.40), calls=%async_computation | async-start | bytes 2097152 | tf_op jit(solution)/shard_map/all_to_all | solution.py:41
  23.3 0.7 constant_dynamic-slice_fusion.1
  24.1 0.5 slice_bitcast_fusion.2
  24.6 0.0 copy-done.2
  24.6 0.5 fusion.26
  25.1 3.1 %collective-permute-start = (bf16[64,128]{1,0:T(8,128)(2,1)S(1)}, bf16[64,128]{1,0:T(8,128)(2,1)S(1)}, u32[]{:S(2)}, u32[]{:S(2)}) collective-permute-start(bf16[64,128]{1,0:T(8,128)(2,1)S(1)} %get-tuple-element.37), channel_id=1, source_target_pairs={{0,8},{8,0},{16,24},{24,16},{32,40},{40,32},{48,56},{56,48},{64,72... | collective-permute-start | bytes 49160 | tf_op jit(solution)/shard_map/ppermute | solution.py:25
  28.2 2.5 %collective-permute-start.1 = (bf16[64,128]{1,0:T(8,128)(2,1)S(1)}, bf16[64,128]{1,0:T(8,128)(2,1)S(1)}, u32[]{:S(2)}, u32[]{:S(2)}) collective-permute-start(bf16[64,128]{1,0:T(8,128)(2,1)S(1)} %get-tuple-element.37), channel_id=1, source_target_pairs={{0,504},{8,16},{16,8},{24,32},{32,24},{40,48},{48,40},{56,64},{64,... | collective-permute-start | bytes 49160 | tf_op jit(solution)/shard_map/ppermute | solution.py:24
  30.8 0.9 multiply_convert_fusion.query_weight
  31.7 0.7 copy-done.8
  32.3 0.6 convert_reduce_fusion.starts
  33.0 0.1 pad_add_fusion
  33.1 0.7 stack.23.spots
  33.7 0.0 collective-permute-done.2.other_0
  33.7 3.5 %all-to-all-done = bf16[4,128,1024]{2,1,0:T(8,128)(2,1)S(1)} async-done(((bf16[4,128,1024]{2,1,0:T(8,128)(2,1)}), bf16[4,128,1024]{2,1,0:T(8,128)(2,1)S(1)}, u32[]{:S(2)}, u32[]{:S(2)}) %all-to-all-start) | async-done | bytes 1048608 | tf_op jit(solution)/shard_map/all_to_all | solution.py:41
  37.2 2.2 %collective-permute-start.3 = (bf16[128,1024]{1,0:T(8,128)(2,1)S(1)}, bf16[128,1024]{1,0:T(8,128)(2,1)S(1)}, u32[]{:S(2)}, u32[]{:S(2)}) collective-permute-start(bf16[128,1024]{1,0:T(8,128)(2,1)S(1)} %collective-permute-done.2.other_0), channel_id=1, source_target_pairs={{0,1},{1,2},{2,3},{3,0},{4,5},{5,6},{6,7},{7,4},{8,9},{9,10},{10,1... | collective-permute-start | bytes 786440 | tf_op jit(solution)/shard_map/ppermute | solution.py:49
  39.4 3.7 %collective-permute-start.4 = (bf16[128,1024]{1,0:T(8,128)(2,1)S(1)}, bf16[128,1024]{1,0:T(8,128)(2,1)S(1)}, u32[]{:S(2)}, u32[]{:S(2)}) collective-permute-start(bf16[128,1024]{1,0:T(8,128)(2,1)S(1)} %collective-permute-done.2.other_0), channel_id=1, source_target_pairs={{0,2},{1,3},{2,0},{3,1},{4,6},{5,7},{6,4},{7,5},{8,10},{9,11},{10,... | collective-permute-start | bytes 786440 | tf_op jit(solution)/shard_map/ppermute | solution.py:49
  43.1 2.5 %collective-permute-start.5 = (bf16[128,1024]{1,0:T(8,128)(2,1)S(1)}, bf16[128,1024]{1,0:T(8,128)(2,1)S(1)}, u32[]{:S(2)}, u32[]{:S(2)}) collective-permute-start(bf16[128,1024]{1,0:T(8,128)(2,1)S(1)} %collective-permute-done.2.other_0), channel_id=1, source_target_pairs={{0,3},{1,0},{2,1},{3,2},{4,7},{5,4},{6,5},{7,6},{8,11},{9,8},{10,9... | collective-permute-start | bytes 786440 | tf_op jit(solution)/shard_map/ppermute | solution.py:49
  45.7 0.0 collective-permute-done
  45.7 0.0 collective-permute-done.1
  45.7 0.6 fusion.1
  46.3 0.0 copy-start.13
  46.3 1.4 %multiply_reduce_fusion = (f32[128]{0:T(128)S(1)}, bf16[1024,128]{1,0:T(8,128)(2,1)}) fusion(bf16[1024,128]{1,0:T(8,128)(2,1)S(1)} %fusion.1, f32[64,128]{1,0:T(8,128)S(1)} %get-tuple-element.38, s32[64]{0:T(128)S(1)} %get-tuple-element.36, bf16[1,1024,128]{2,1,0:T(8,128)(2,1)S(1)} %copy-done.3), kind=kOutput, calls=%fused_computation.18 | convolution fusion | flops 101777280 | bytes 819968 | tf_op jit(solution)/shard_map/dot_general | solution.py:64
  47.7 0.6 broadcast_in_dim.44
  48.3 16.0 %all-to-all-start.1 = ((f32[16,1,128]{2,1,0:T(1,128)}), f32[16,1,128]{2,1,0:T(1,128)S(1)}, u32[]{:S(2)}, u32[]{:S(2)}) async-start(f32[16,1,128]{2,1,0:T(1,128)} %broadcast_in_dim.44), calls=%async_computation.1 | async-start | bytes 16384 | tf_op jit(solution)/shard_map/all_to_all | solution.py:31
  64.2 0.0 collective-permute-done.3.other_1
  64.3 0.0 copy-start.10
  64.3 0.0 collective-permute-done.4.other_2
  64.3 0.0 collective-permute-done.5.other_3
  64.3 0.0 copy-start.12
  64.3 0.0 copy-done.7
  64.3 0.6 copy-done.10
  65.0 0.1 copy-done.11
  65.0 0.1 copy-done.12
  65.1 10.7 %shard_map.188 = (bf16[1024,128]{1,0:T(8,128)(2,1)}, bf16[1024,128]{1,0:T(8,128)(2,1)}, bf16[1024,128]{1,0:T(8,128)(2,1)}, f32[1024,128]{1,0:T(8,128)}, f32[64,128]{1,0:T(8,128)}) custom-call(s32[5]{0:T(128)} %stack.23.spots, s32[8]{0:T(128)} %convert_reduce_fusion.starts, s32[64]{0:T(128)} %get-tuple-element.35.picks, bf16[512,1024]{1,0:T(8,128)(2,1)} %bitcast.96, ...), custom_call_target="tpu_custom_call" | custom-call | flops 2000000000 | bytes 8000000 | tf_op jit(solution)/shard_map/pallas_call | solution.py:236
  75.9 0.0 all-to-all-done.1
  75.9 5.3 %collective-permute-start.6 = (f32[64,128]{1,0:T(8,128)}, f32[64,128]{1,0:T(8,128)S(1)}, u32[]{:S(2)}, u32[]{:S(2)}) collective-permute-start(f32[64,128]{1,0:T(8,128)} %get-tuple-element.24), channel_id=1, source_target_pairs={{0,8},{8,0},{16,24},{24,16},{32,40},{40,32},{48,56},{56,48},{64,72... | collective-permute-start | bytes 98312 | tf_op jit(solution)/shard_map/ppermute | solution.py:25
  81.2 2.7 %collective-permute-start.7 = (f32[64,128]{1,0:T(8,128)}, f32[64,128]{1,0:T(8,128)S(1)}, u32[]{:S(2)}, u32[]{:S(2)}) collective-permute-start(f32[64,128]{1,0:T(8,128)} %get-tuple-element.24), channel_id=1, source_target_pairs={{0,504},{8,16},{16,8},{24,32},{32,24},{40,48},{48,40},{56,64},{64,... | collective-permute-start | bytes 98312 | tf_op jit(solution)/shard_map/ppermute | solution.py:24
  83.9 0.6 broadcast_in_dim.47
  84.5 12.8 %all-to-all-start.2 = ((f32[32,1,128]{2,1,0:T(1,128)}), f32[32,1,128]{2,1,0:T(1,128)S(1)}, u32[]{:S(2)}, u32[]{:S(2)}) async-start(f32[32,1,128]{2,1,0:T(1,128)} %broadcast_in_dim.47), calls=%async_computation.2 | async-start | bytes 32768 | tf_op jit(solution)/shard_map/all_to_all | solution.py:31
  97.4 0.0 copy-start.1
  97.4 0.9 fusion.12
  98.3 6.0 %all-to-all-done.2 = f32[32,1,128]{2,1,0:T(1,128)S(1)} async-done(((f32[32,1,128]{2,1,0:T(1,128)}), f32[32,1,128]{2,1,0:T(1,128)S(1)}, u32[]{:S(2)}, u32[]{:S(2)}) %all-to-all-start.2) | async-done | bytes 16416 | tf_op jit(solution)/shard_map/all_to_all | solution.py:31
  104.3 0.6 reduce_sum.43
  105.5 0.0 collective-permute-done.6.near
  105.5 0.0 collective-permute-done.7.far
  105.6 1.5 %shard_map.189 = bf16[1024,128]{1,0:T(8,128)(2,1)} custom-call(s32[64]{0:T(128)S(1)} %get-tuple-element.42.near_picks, s32[64]{0:T(128)S(1)} %get-tuple-element.31.far_picks, f32[64,128]{1,0:T(8,128)S(1)} %collective-permute-done.6.near, f32[64,128]{1,0:T(8,128)S(1)} %collective-permute-done.7.far, f32[1024,128]{1,0:T(8,128)S(1)} %copy-done, ...), custom_call_target="tpu_custom_call" | custom-call | flops 1000000 | bytes 1000000 | tf_op jit(solution)/shard_map/pallas_call | solution.py:281
  (20 shorter events, 0.1 us)
Async XLA Ops:
  0.6 33.1 %collective-permute-start.2 = (bf16[128,1024]{1,0:T(8,128)(2,1)}, bf16[128,1024]{1,0:T(8,128)(2,1)S(1)}, u32[]{:S(2)}, u32[]{:S(2)}) collective-permute-start(bf16[128,1024]{1,0:T(8,128)(2,1)} %bitcast.97), channel_id=1, source_target_pairs={{0,4},{4,0},{1,5},{5,1},{2,6},{6,2},{3,7},{7,3},{8,12},{12,8},{9,1... | collective-permute-start | bytes 786440 | tf_op jit(solution)/shard_map/ppermute | solution.py:312
  19.0 5.6 %copy-start.2 = (f32[1,1024,128]{2,1,0:T(8,128)S(1)}, f32[1,1024,128]{2,1,0:T(8,128)}, u32[]{:S(2)}) copy-start(f32[1,1024,128]{2,1,0:T(8,128)} %param.13) | copy-start | bytes 1572868
  19.0 5.6 %copy-start.3 = (bf16[1,1024,128]{2,1,0:T(8,128)(2,1)S(1)}, bf16[1,1024,128]{2,1,0:T(8,128)(2,1)}, u32[]{:S(2)}) copy-start(bf16[1,1024,128]{2,1,0:T(8,128)(2,1)} %param.14) | copy-start | bytes 786436
  19.0 5.6 %copy-start.4 = (bf16[1,1024,128]{2,1,0:T(8,128)(2,1)S(1)}, bf16[1,1024,128]{2,1,0:T(8,128)(2,1)}, u32[]{:S(2)}) copy-start(bf16[1,1024,128]{2,1,0:T(8,128)(2,1)} %param.15) | copy-start | bytes 786436
  19.0 5.6 %copy-start.5 = (bf16[1,1024,128]{2,1,0:T(8,128)(2,1)S(1)}, bf16[1,1024,128]{2,1,0:T(8,128)(2,1)}, u32[]{:S(2)}) copy-start(bf16[1,1024,128]{2,1,0:T(8,128)(2,1)} %param.16) | copy-start | bytes 786436
  19.0 18.2 %all-to-all-start = ((bf16[4,128,1024]{2,1,0:T(8,128)(2,1)}), bf16[4,128,1024]{2,1,0:T(8,128)(2,1)S(1)}, u32[]{:S(2)}, u32[]{:S(2)}) async-start(bf16[4,128,1024]{2,1,0:T(8,128)(2,1)} %broadcast_in_dim.40), calls=%async_computation | async-start | bytes 2097152 | tf_op jit(solution)/shard_map/all_to_all | solution.py:41
  25.1 20.6 %collective-permute-start = (bf16[64,128]{1,0:T(8,128)(2,1)S(1)}, bf16[64,128]{1,0:T(8,128)(2,1)S(1)}, u32[]{:S(2)}, u32[]{:S(2)}) collective-permute-start(bf16[64,128]{1,0:T(8,128)(2,1)S(1)} %get-tuple-element.37), channel_id=1, source_target_pairs={{0,8},{8,0},{16,24},{24,16},{32,40},{40,32},{48,56},{56,48},{64,72... | collective-permute-start | bytes 49160 | tf_op jit(solution)/shard_map/ppermute | solution.py:25
  28.2 17.4 %collective-permute-start.1 = (bf16[64,128]{1,0:T(8,128)(2,1)S(1)}, bf16[64,128]{1,0:T(8,128)(2,1)S(1)}, u32[]{:S(2)}, u32[]{:S(2)}) collective-permute-start(bf16[64,128]{1,0:T(8,128)(2,1)S(1)} %get-tuple-element.37), channel_id=1, source_target_pairs={{0,504},{8,16},{16,8},{24,32},{32,24},{40,48},{48,40},{56,64},{64,... | collective-permute-start | bytes 49160 | tf_op jit(solution)/shard_map/ppermute | solution.py:24
  31.7 0.7 copy-start.8
  33.7 12.5 %copy-start.9 = (bf16[128,1024]{1,0:T(8,128)(2,1)}, bf16[128,1024]{1,0:T(8,128)(2,1)S(1)}, u32[]{:S(2)}) copy-start(bf16[128,1024]{1,0:T(8,128)(2,1)S(1)} %collective-permute-done.2.other_0) | copy-start | bytes 786436
  37.2 27.1 %copy-start.7 = (bf16[4,128,1024]{2,1,0:T(8,128)(2,1)}, bf16[4,128,1024]{2,1,0:T(8,128)(2,1)S(1)}, u32[]{:S(2)}) copy-start(bf16[4,128,1024]{2,1,0:T(8,128)(2,1)S(1)} %all-to-all-done) | copy-start | bytes 3145732
  37.2 27.0 %collective-permute-start.3 = (bf16[128,1024]{1,0:T(8,128)(2,1)S(1)}, bf16[128,1024]{1,0:T(8,128)(2,1)S(1)}, u32[]{:S(2)}, u32[]{:S(2)}) collective-permute-start(bf16[128,1024]{1,0:T(8,128)(2,1)S(1)} %collective-permute-done.2.other_0), channel_id=1, source_target_pairs={{0,1},{1,2},{2,3},{3,0},{4,5},{5,6},{6,7},{7,4},{8,9},{9,10},{10,1... | collective-permute-start | bytes 786440 | tf_op jit(solution)/shard_map/ppermute | solution.py:49
  39.4 24.9 %collective-permute-start.4 = (bf16[128,1024]{1,0:T(8,128)(2,1)S(1)}, bf16[128,1024]{1,0:T(8,128)(2,1)S(1)}, u32[]{:S(2)}, u32[]{:S(2)}) collective-permute-start(bf16[128,1024]{1,0:T(8,128)(2,1)S(1)} %collective-permute-done.2.other_0), channel_id=1, source_target_pairs={{0,2},{1,3},{2,0},{3,1},{4,6},{5,7},{6,4},{7,5},{8,10},{9,11},{10,... | collective-permute-start | bytes 786440 | tf_op jit(solution)/shard_map/ppermute | solution.py:49
  43.1 21.2 %collective-permute-start.5 = (bf16[128,1024]{1,0:T(8,128)(2,1)S(1)}, bf16[128,1024]{1,0:T(8,128)(2,1)S(1)}, u32[]{:S(2)}, u32[]{:S(2)}) collective-permute-start(bf16[128,1024]{1,0:T(8,128)(2,1)S(1)} %collective-permute-done.2.other_0), channel_id=1, source_target_pairs={{0,3},{1,0},{2,1},{3,2},{4,7},{5,4},{6,5},{7,6},{8,11},{9,8},{10,9... | collective-permute-start | bytes 786440 | tf_op jit(solution)/shard_map/ppermute | solution.py:49
  46.3 1.4 %copy-start.13 = (bf16[1024,128]{1,0:T(8,128)(2,1)}, bf16[1024,128]{1,0:T(8,128)(2,1)S(1)}, u32[]{:S(2)}) copy-start(bf16[1024,128]{1,0:T(8,128)(2,1)S(1)} %fusion.1) | copy-start | bytes 786436
  48.3 27.6 %all-to-all-start.1 = ((f32[16,1,128]{2,1,0:T(1,128)}), f32[16,1,128]{2,1,0:T(1,128)S(1)}, u32[]{:S(2)}, u32[]{:S(2)}) async-start(f32[16,1,128]{2,1,0:T(1,128)} %broadcast_in_dim.44), calls=%async_computation.1 | async-start | bytes 16384 | tf_op jit(solution)/shard_map/all_to_all | solution.py:31
  64.3 0.7 copy-start.10
  64.3 0.8 copy-start.11
  64.3 0.8 copy-start.12
  65.1 32.2 %copy-start.6 = (bf16[1,1024,128]{2,1,0:T(8,128)(2,1)S(1)}, bf16[1,1024,128]{2,1,0:T(8,128)(2,1)}, u32[]{:S(2)}) copy-start(bf16[1,1024,128]{2,1,0:T(8,128)(2,1)} %param.16) | copy-start | bytes 786436
  75.9 29.6 %collective-permute-start.6 = (f32[64,128]{1,0:T(8,128)}, f32[64,128]{1,0:T(8,128)S(1)}, u32[]{:S(2)}, u32[]{:S(2)}) collective-permute-start(f32[64,128]{1,0:T(8,128)} %get-tuple-element.24), channel_id=1, source_target_pairs={{0,8},{8,0},{16,24},{24,16},{32,40},{40,32},{48,56},{56,48},{64,72... | collective-permute-start | bytes 98312 | tf_op jit(solution)/shard_map/ppermute | solution.py:25
  81.2 24.4 %collective-permute-start.7 = (f32[64,128]{1,0:T(8,128)}, f32[64,128]{1,0:T(8,128)S(1)}, u32[]{:S(2)}, u32[]{:S(2)}) collective-permute-start(f32[64,128]{1,0:T(8,128)} %get-tuple-element.24), channel_id=1, source_target_pairs={{0,504},{8,16},{16,8},{24,32},{32,24},{40,48},{48,40},{56,64},{64,... | collective-permute-start | bytes 98312 | tf_op jit(solution)/shard_map/ppermute | solution.py:24
  84.5 19.7 %all-to-all-start.2 = ((f32[32,1,128]{2,1,0:T(1,128)}), f32[32,1,128]{2,1,0:T(1,128)S(1)}, u32[]{:S(2)}, u32[]{:S(2)}) async-start(f32[32,1,128]{2,1,0:T(1,128)} %broadcast_in_dim.47), calls=%async_computation.2 | async-start | bytes 32768 | tf_op jit(solution)/shard_map/all_to_all | solution.py:31
  97.3 8.2 %copy-start = (f32[1024,128]{1,0:T(8,128)S(1)}, f32[1024,128]{1,0:T(8,128)}, u32[]{:S(2)}) copy-start(f32[1024,128]{1,0:T(8,128)} %get-tuple-element.25.update) | copy-start | bytes 1572868
  97.4 8.2 %copy-start.1 = (bf16[1,1024,128]{2,1,0:T(8,128)(2,1)S(1)}, bf16[1,1024,128]{2,1,0:T(8,128)(2,1)}, u32[]{:S(2)}) copy-start(bf16[1,1024,128]{2,1,0:T(8,128)(2,1)} %param.18) | copy-start | bytes 786436

commit v4 on v3

--- a/solution.py
+++ b/solution.py
@@ -86,7 +86,7 @@
 
 
 def consensus_of(partial_sums, width):
-    total_sum = jnp.sum(spread_sum(partial_sums, ("blk_0", "blk_2", "tp_1")))
+    total_sum = jnp.sum(spread_sum(partial_sums, ("blk_1", "tp_0")))
     return total_sum / float(lax.axis_size(BLK) * width * width)
 
 
@@ -260,7 +260,7 @@
     )(spots, starts, picks, *arrays)
 
 
-def mix_kernel(near_picks, far_picks, near, far, update, mixed, mixed_new, total):
+def mix_kernel(far_picks, near_picks, far, near, update, mixed, mixed_new, total):
     total[...] = update[...]
     for picks, values in ((near_picks, near), (far_picks, far)):
         for low in range(0, picks.shape[0], 8):
@@ -274,7 +274,7 @@
     mixed_new[...] = (mixed[...].astype(jnp.float32) + total[...] / 3.0).astype(jnp.bfloat16)
 
 
-def mix_step(near_picks, far_picks, *arrays):
+def mix_step(far_picks, near_picks, *arrays):
     scalars = [pl.BlockSpec(memory_space=pltpu.SMEM)] * 2
     whole = pl.BlockSpec(memory_space=pltpu.VMEM)
     rows, width = arrays[3].shape
@@ -286,7 +286,7 @@
         scratch_shapes=[pltpu.VMEM((rows, width), jnp.float32)],
         compiler_params=pltpu.CompilerParams(vmem_limit_bytes=8 * 2**20),
         cost_estimate=pl.CostEstimate(flops=10**6, bytes_accessed=10**6, transcendentals=0),
-    )(near_picks, far_picks, *arrays)
+    )(far_picks, near_picks, *arrays)
 
 
 def per_device(
@@ -325,15 +325,18 @@
         jnp.bfloat16
     )
     param_sent = param_values.astype(jnp.bfloat16)
-    param_received = jnp.concatenate((param_sent,) + swaps(param_sent), axis=0).astype(jnp.float32)
-    mixed_new = (mixed_value + mix_stream(param_received, [own[0] for own in picks], model_width)).astype(
+    param_near, param_far = swaps(param_sent)
+    param_received = jnp.concatenate((param_sent, param_far, param_near), axis=0).astype(
+        jnp.float32
+    )
+    mixed_new = (mixed_value + mix_stream(param_received, [own_picks[0], picks[2][0], picks[1][0]], model_width)).astype(
         jnp.bfloat16
     )
     partial_sums = gap_rows(mixed_new, copies_new)
     own_half, other = lax.optimization_barrier((own_half, other))
     blocks = pass_tokens(other)
     _, partial_sums = lax.optimization_barrier((other, partial_sums))
-    partial_sums = spread_rows(partial_sums, ("blk_1", "tp_0"))
+    partial_sums = spread_rows(partial_sums, ("blk_0", "blk_2", "tp_1"))
     spots = [high * half] + [
         (1 - high) * half + ((place - shift) % len(blocks)) * height for shift in range(len(blocks))
     ]
@@ -356,7 +359,7 @@
     tracker_values, partial_sums = lax.optimization_barrier((tracker_values, partial_sums))
     near, far = swaps(tracker_values)
     consensus = consensus_of(jnp.sum(partial_sums, axis=0, keepdims=True), model_width)
-    tracker_mixed_new = mix_step(picks[1][1], picks[2][1], near, far, update, tracker_mixed[0])
+    tracker_mixed_new = mix_step(picks[2][1], picks[1][1], far, near, update, tracker_mixed[0])
     return (
         weights_new[None],
         copies_new[None],

time: 109 us -> 105 us (0.963)
  starting transfers between devices: 71.4 us -> 66.3 us
    all_to_all x2, starting transfers between devices: 28.8 us -> 15 us  [spread_rows(): return lax.all_to_all(rows, axes, 0, 0, tiled=True)]
    all_to_all x2, waiting for transfers between devices: 5.97 us -> 10.2 us  [spread_rows(): return lax.all_to_all(rows, axes, 0, 0, tiled=True)]
    ppermute x2, starting transfers between devices: 5.25 us -> 9.16 us  [swaps(): from_far = lax.ppermute(value, BLK, far)]
    all_to_all x1, waiting for transfers between devices: 3.48 us -> 0.01 us  [spread_tokens(): lax.all_to_all(blocks, 'tp_1', 0, 0, tiled=True).reshape(-1, value.shape[1])]
    ppermute x3, starting transfers between devices: 8.4 us -> 10.8 us  [pass_tokens(): blocks.append(lax.ppermute(value, 'tp_1', pairs))]
    ppermute x2, starting transfers between devices: 8.41 us -> 10.7 us  [swaps(): return (lax.ppermute(value, BLK, near), from_far)]
  transfers between devices with their start and end apart: 11 -> 11, of which waited for: 2 -> 1; matrix products, arithmetic and copies ran while one was open for 10% -> 10% of each run, Pallas kernels for 10% -> 10%
where the time goes in v4:
time: 105 us; the launch traced here: 104 us
  starting transfers between devices  66.3 us (63%)
  Pallas kernels  12.3 us (12%)
  waiting for transfers between devices  10.2 us (10%)
  local copies, waits for them, and re-layouts  6.77 us (6%)
  other arithmetic  3.15 us (3%)
  between operations  2.7 us (3%)
  matrix products  2.44 us (2%)
    ppermute x1, starting transfers between devices, per_device(): other = lax.ppermute(tokens[0], 'tp_0', [(0, 1), (1, 0)])  16.3 us
    all_to_all x2, starting transfers between devices, spread_rows(): return lax.all_to_all(rows, axes, 0, 0, tiled=True)  15 us
    ppermute x3, starting transfers between devices, pass_tokens(): blocks.append(lax.ppermute(value, 'tp_1', pairs))  10.8 us
    ppermute x2, starting transfers between devices, swaps(): return (lax.ppermute(value, BLK, near), from_far)  10.7 us
    pallas_call x1, Pallas kernels, gradient_step(): pl.pallas_call(gradient_kernel, out_shape=(narrow, narrow, narrow, jax.Sh...  10.7 us
    all_to_all x2, waiting for transfers between devices, spread_rows(): return lax.all_to_all(rows, axes, 0, 0, tiled=True)  10.2 us
    ppermute x2, starting transfers between devices, swaps(): from_far = lax.ppermute(value, BLK, far)  9.16 us
    all_to_all x1, starting transfers between devices, spread_tokens(): lax.all_to_all(blocks, 'tp_1', 0, 0, tiled=True).reshape(-1, value.shape[1])  4.33 us
  transfers between devices with their start and end apart: 11, of which 1 were waited for; matrix products, arithmetic and copies ran while one was open for 10% of the time, Pallas kernels for 10%

profile of v4, /device:TPU:1, one launch (start us, length us, event | category | flops | bytes accessed | tf_op | source)
XLA Modules:
  0.0 103.9 jit_solution(1995018813572599321)
XLA Ops:
  0.6 16.3 %collective-permute-start.2 = (bf16[128,1024]{1,0:T(8,128)(2,1)}, bf16[128,1024]{1,0:T(8,128)(2,1)S(1)}, u32[]{:S(2)}, u32[]{:S(2)}) collective-permute-start(bf16[128,1024]{1,0:T(8,128)(2,1)} %bitcast.97), channel_id=1, source_target_pairs={{0,4},{4,0},{1,5},{5,1},{2,6},{6,2},{3,7},{7,3},{8,12},{12,8},{9,1... | collective-permute-start | bytes 786440 | tf_op jit(solution)/shard_map/ppermute | solution.py:312
  16.9 2.1 %broadcast_in_dim.40 = bf16[4,128,1024]{2,1,0:T(8,128)(2,1)} broadcast(bf16[128,1024]{1,0:T(8,128)(2,1)} %bitcast.98), dimensions={1,2} | broadcast | bytes 1310720 | tf_op jit(solution)/shard_map/broadcast_in_dim | solution.py:40
  19.0 4.3 %all-to-all-start = ((bf16[4,128,1024]{2,1,0:T(8,128)(2,1)}), bf16[4,128,1024]{2,1,0:T(8,128)(2,1)S(1)}, u32[]{:S(2)}, u32[]{:S(2)}) async-start(bf16[4,128,1024]{2,1,0:T(8,128)(2,1)} %broadcast_in_dim.40), calls=%async_computation | async-start | bytes 2097152 | tf_op jit(solution)/shard_map/all_to_all | solution.py:41
  23.3 0.7 constant_dynamic-slice_fusion.1
  24.1 0.5 slice_bitcast_fusion.2
  24.6 0.0 copy-done.2
  24.6 0.5 fusion.26
  25.1 3.8 %collective-permute-start = (bf16[64,128]{1,0:T(8,128)(2,1)S(1)}, bf16[64,128]{1,0:T(8,128)(2,1)S(1)}, u32[]{:S(2)}, u32[]{:S(2)}) collective-permute-start(bf16[64,128]{1,0:T(8,128)(2,1)S(1)} %get-tuple-element.37), channel_id=1, source_target_pairs={{0,504},{8,16},{16,8},{24,32},{32,24},{40,48},{48,40},{56,64},{64,... | collective-permute-start | bytes 49160 | tf_op jit(solution)/shard_map/ppermute | solution.py:24
  28.9 6.1 %collective-permute-start.1 = (bf16[64,128]{1,0:T(8,128)(2,1)S(1)}, bf16[64,128]{1,0:T(8,128)(2,1)S(1)}, u32[]{:S(2)}, u32[]{:S(2)}) collective-permute-start(bf16[64,128]{1,0:T(8,128)(2,1)S(1)} %get-tuple-element.37), channel_id=1, source_target_pairs={{0,8},{8,0},{16,24},{24,16},{32,40},{40,32},{48,56},{56,48},{64,72... | collective-permute-start | bytes 49160 | tf_op jit(solution)/shard_map/ppermute | solution.py:25
  35.0 0.9 multiply_convert_fusion.query_weight
  35.9 0.7 copy-done.8
  36.5 0.6 convert_reduce_fusion.starts
  37.2 0.1 pad_add_fusion
  37.2 0.7 stack.23.spots
  37.9 0.0 collective-permute-done.2.other_0
  37.9 0.0 all-to-all-done
  37.9 3.4 %collective-permute-start.3 = (bf16[128,1024]{1,0:T(8,128)(2,1)S(1)}, bf16[128,1024]{1,0:T(8,128)(2,1)S(1)}, u32[]{:S(2)}, u32[]{:S(2)}) collective-permute-start(bf16[128,1024]{1,0:T(8,128)(2,1)S(1)} %collective-permute-done.2.other_0), channel_id=1, source_target_pairs={{0,1},{1,2},{2,3},{3,0},{4,5},{5,6},{6,7},{7,4},{8,9},{9,10},{10,1... | collective-permute-start | bytes 786440 | tf_op jit(solution)/shard_map/ppermute | solution.py:49
  41.3 4.3 %collective-permute-start.4 = (bf16[128,1024]{1,0:T(8,128)(2,1)S(1)}, bf16[128,1024]{1,0:T(8,128)(2,1)S(1)}, u32[]{:S(2)}, u32[]{:S(2)}) collective-permute-start(bf16[128,1024]{1,0:T(8,128)(2,1)S(1)} %collective-permute-done.2.other_0), channel_id=1, source_target_pairs={{0,2},{1,3},{2,0},{3,1},{4,6},{5,7},{6,4},{7,5},{8,10},{9,11},{10,... | collective-permute-start | bytes 786440 | tf_op jit(solution)/shard_map/ppermute | solution.py:49
  45.6 3.1 %collective-permute-start.5 = (bf16[128,1024]{1,0:T(8,128)(2,1)S(1)}, bf16[128,1024]{1,0:T(8,128)(2,1)S(1)}, u32[]{:S(2)}, u32[]{:S(2)}) collective-permute-start(bf16[128,1024]{1,0:T(8,128)(2,1)S(1)} %collective-permute-done.2.other_0), channel_id=1, source_target_pairs={{0,3},{1,0},{2,1},{3,2},{4,7},{5,4},{6,5},{7,6},{8,11},{9,8},{10,9... | collective-permute-start | bytes 786440 | tf_op jit(solution)/shard_map/ppermute | solution.py:49
  48.7 0.0 collective-permute-done
  48.7 0.0 collective-permute-done.1
  48.8 0.6 fusion.1
  49.4 0.0 copy-start.13
  49.4 1.4 %multiply_reduce_fusion = (f32[128]{0:T(128)S(1)}, bf16[1024,128]{1,0:T(8,128)(2,1)}) fusion(bf16[1024,128]{1,0:T(8,128)(2,1)S(1)} %fusion.1, f32[64,128]{1,0:T(8,128)S(1)} %get-tuple-element.38, s32[64]{0:T(128)S(1)} %get-tuple-element.36, bf16[1,1024,128]{2,1,0:T(8,128)(2,1)S(1)} %copy-done.3), kind=kOutput, calls=%fused_computation.18 | convolution fusion | flops 101777280 | bytes 819968 | tf_op jit(solution)/shard_map/dot_general | solution.py:64
  50.7 0.6 broadcast_in_dim.44
  51.4 6.4 %all-to-all-start.1 = ((f32[32,1,128]{2,1,0:T(1,128)}), f32[32,1,128]{2,1,0:T(1,128)S(1)}, u32[]{:S(2)}, u32[]{:S(2)}) async-start(f32[32,1,128]{2,1,0:T(1,128)} %broadcast_in_dim.44), calls=%async_computation.1 | async-start | bytes 32768 | tf_op jit(solution)/shard_map/all_to_all | solution.py:31
  57.8 0.0 collective-permute-done.3.other_1
  57.8 0.0 copy-start.10
  57.8 0.0 collective-permute-done.4.other_2
  57.8 0.0 collective-permute-done.5.other_3
  57.9 0.6 copy-done.10
  58.5 0.1 copy-done.11
  58.6 0.1 copy-done.12
  58.7 10.7 %shard_map.188 = (bf16[1024,128]{1,0:T(8,128)(2,1)}, bf16[1024,128]{1,0:T(8,128)(2,1)}, bf16[1024,128]{1,0:T(8,128)(2,1)}, f32[1024,128]{1,0:T(8,128)}, f32[64,128]{1,0:T(8,128)}) custom-call(s32[5]{0:T(128)} %stack.23.spots, s32[8]{0:T(128)} %convert_reduce_fusion.starts, s32[64]{0:T(128)} %get-tuple-element.35.picks, bf16[512,1024]{1,0:T(8,128)(2,1)} %bitcast.96, ...), custom_call_target="tpu_custom_call" | custom-call | flops 2000000000 | bytes 8000000 | tf_op jit(solution)/shard_map/pallas_call | solution.py:236
  69.4 0.0 all-to-all-done.1
  69.5 5.4 %collective-permute-start.6 = (f32[64,128]{1,0:T(8,128)}, f32[64,128]{1,0:T(8,128)S(1)}, u32[]{:S(2)}, u32[]{:S(2)}) collective-permute-start(f32[64,128]{1,0:T(8,128)} %get-tuple-element.24), channel_id=1, source_target_pairs={{0,504},{8,16},{16,8},{24,32},{32,24},{40,48},{48,40},{56,64},{64,... | collective-permute-start | bytes 98312 | tf_op jit(solution)/shard_map/ppermute | solution.py:24
  74.9 4.6 %collective-permute-start.7 = (f32[64,128]{1,0:T(8,128)}, f32[64,128]{1,0:T(8,128)S(1)}, u32[]{:S(2)}, u32[]{:S(2)}) collective-permute-start(f32[64,128]{1,0:T(8,128)} %get-tuple-element.24), channel_id=1, source_target_pairs={{0,8},{8,0},{16,24},{24,16},{32,40},{40,32},{48,56},{56,48},{64,72... | collective-permute-start | bytes 98312 | tf_op jit(solution)/shard_map/ppermute | solution.py:25
  79.5 0.6 broadcast_in_dim.47
  80.1 8.6 %all-to-all-start.2 = ((f32[16,1,128]{2,1,0:T(1,128)}), f32[16,1,128]{2,1,0:T(1,128)S(1)}, u32[]{:S(2)}, u32[]{:S(2)}) async-start(f32[16,1,128]{2,1,0:T(1,128)} %broadcast_in_dim.47), calls=%async_computation.2 | async-start | bytes 16384 | tf_op jit(solution)/shard_map/all_to_all | solution.py:31
  88.7 0.0 copy-done.6
  88.7 0.0 copy-start
  88.7 0.0 copy-start.1
  88.7 0.9 fusion.12
  89.7 10.2 %all-to-all-done.2 = f32[16,1,128]{2,1,0:T(1,128)S(1)} async-done(((f32[16,1,128]{2,1,0:T(1,128)}), f32[16,1,128]{2,1,0:T(1,128)S(1)}, u32[]{:S(2)}, u32[]{:S(2)}) %all-to-all-start.2) | async-done | bytes 8224 | tf_op jit(solution)/shard_map/all_to_all | solution.py:31
  99.9 0.6 reduce_sum.43
  101.1 0.0 collective-permute-done.6.far
  101.2 0.0 collective-permute-done.7.near
  101.2 1.5 %shard_map.189 = bf16[1024,128]{1,0:T(8,128)(2,1)} custom-call(s32[64]{0:T(128)S(1)} %get-tuple-element.42.far_picks, s32[64]{0:T(128)S(1)} %get-tuple-element.31.near_picks, f32[64,128]{1,0:T(8,128)S(1)} %collective-permute-done.6.far, f32[64,128]{1,0:T(8,128)S(1)} %collective-permute-done.7.near, f32[1024,128]{1,0:T(8,128)S(1)} %copy-done, ...), custom_call_target="tpu_custom_call" | custom-call | flops 1000000 | bytes 1000000 | tf_op jit(solution)/shard_map/pallas_call | solution.py:281
  (20 shorter events, 0.1 us)
Async XLA Ops:
  0.6 37.3 %collective-permute-start.2 = (bf16[128,1024]{1,0:T(8,128)(2,1)}, bf16[128,1024]{1,0:T(8,128)(2,1)S(1)}, u32[]{:S(2)}, u32[]{:S(2)}) collective-permute-start(bf16[128,1024]{1,0:T(8,128)(2,1)} %bitcast.97), channel_id=1, source_target_pairs={{0,4},{4,0},{1,5},{5,1},{2,6},{6,2},{3,7},{7,3},{8,12},{12,8},{9,1... | collective-permute-start | bytes 786440 | tf_op jit(solution)/shard_map/ppermute | solution.py:312
  19.0 5.6 %copy-start.2 = (f32[1,1024,128]{2,1,0:T(8,128)S(1)}, f32[1,1024,128]{2,1,0:T(8,128)}, u32[]{:S(2)}) copy-start(f32[1,1024,128]{2,1,0:T(8,128)} %param.13) | copy-start | bytes 1572868
  19.0 5.6 %copy-start.3 = (bf16[1,1024,128]{2,1,0:T(8,128)(2,1)S(1)}, bf16[1,1024,128]{2,1,0:T(8,128)(2,1)}, u32[]{:S(2)}) copy-start(bf16[1,1024,128]{2,1,0:T(8,128)(2,1)} %param.14) | copy-start | bytes 786436
  19.0 5.6 %copy-start.4 = (bf16[1,1024,128]{2,1,0:T(8,128)(2,1)S(1)}, bf16[1,1024,128]{2,1,0:T(8,128)(2,1)}, u32[]{:S(2)}) copy-start(bf16[1,1024,128]{2,1,0:T(8,128)(2,1)} %param.15) | copy-start | bytes 786436
  19.0 5.6 %copy-start.5 = (bf16[1,1024,128]{2,1,0:T(8,128)(2,1)S(1)}, bf16[1,1024,128]{2,1,0:T(8,128)(2,1)}, u32[]{:S(2)}) copy-start(bf16[1,1024,128]{2,1,0:T(8,128)(2,1)} %param.16) | copy-start | bytes 786436
  19.0 18.9 %all-to-all-start = ((bf16[4,128,1024]{2,1,0:T(8,128)(2,1)}), bf16[4,128,1024]{2,1,0:T(8,128)(2,1)S(1)}, u32[]{:S(2)}, u32[]{:S(2)}) async-start(bf16[4,128,1024]{2,1,0:T(8,128)(2,1)} %broadcast_in_dim.40), calls=%async_computation | async-start | bytes 2097152 | tf_op jit(solution)/shard_map/all_to_all | solution.py:41
  25.1 23.7 %collective-permute-start = (bf16[64,128]{1,0:T(8,128)(2,1)S(1)}, bf16[64,128]{1,0:T(8,128)(2,1)S(1)}, u32[]{:S(2)}, u32[]{:S(2)}) collective-permute-start(bf16[64,128]{1,0:T(8,128)(2,1)S(1)} %get-tuple-element.37), channel_id=1, source_target_pairs={{0,504},{8,16},{16,8},{24,32},{32,24},{40,48},{48,40},{56,64},{64,... | collective-permute-start | bytes 49160 | tf_op jit(solution)/shard_map/ppermute | solution.py:24
  28.9 19.9 %collective-permute-start.1 = (bf16[64,128]{1,0:T(8,128)(2,1)S(1)}, bf16[64,128]{1,0:T(8,128)(2,1)S(1)}, u32[]{:S(2)}, u32[]{:S(2)}) collective-permute-start(bf16[64,128]{1,0:T(8,128)(2,1)S(1)} %get-tuple-element.37), channel_id=1, source_target_pairs={{0,8},{8,0},{16,24},{24,16},{32,40},{40,32},{48,56},{56,48},{64,72... | collective-permute-start | bytes 49160 | tf_op jit(solution)/shard_map/ppermute | solution.py:25
  35.8 0.7 copy-start.8
  37.9 11.4 %copy-start.9 = (bf16[128,1024]{1,0:T(8,128)(2,1)}, bf16[128,1024]{1,0:T(8,128)(2,1)S(1)}, u32[]{:S(2)}) copy-start(bf16[128,1024]{1,0:T(8,128)(2,1)S(1)} %collective-permute-done.2.other_0) | copy-start | bytes 786436
  37.9 19.9 %copy-start.7 = (bf16[4,128,1024]{2,1,0:T(8,128)(2,1)}, bf16[4,128,1024]{2,1,0:T(8,128)(2,1)S(1)}, u32[]{:S(2)}) copy-start(bf16[4,128,1024]{2,1,0:T(8,128)(2,1)S(1)} %all-to-all-done) | copy-start | bytes 3145732
  37.9 19.9 %collective-permute-start.3 = (bf16[128,1024]{1,0:T(8,128)(2,1)S(1)}, bf16[128,1024]{1,0:T(8,128)(2,1)S(1)}, u32[]{:S(2)}, u32[]{:S(2)}) collective-permute-start(bf16[128,1024]{1,0:T(8,128)(2,1)S(1)} %collective-permute-done.2.other_0), channel_id=1, source_target_pairs={{0,1},{1,2},{2,3},{3,0},{4,5},{5,6},{6,7},{7,4},{8,9},{9,10},{10,1... | collective-permute-start | bytes 786440 | tf_op jit(solution)/shard_map/ppermute | solution.py:49
  41.3 16.5 %collective-permute-start.4 = (bf16[128,1024]{1,0:T(8,128)(2,1)S(1)}, bf16[128,1024]{1,0:T(8,128)(2,1)S(1)}, u32[]{:S(2)}, u32[]{:S(2)}) collective-permute-start(bf16[128,1024]{1,0:T(8,128)(2,1)S(1)} %collective-permute-done.2.other_0), channel_id=1, source_target_pairs={{0,2},{1,3},{2,0},{3,1},{4,6},{5,7},{6,4},{7,5},{8,10},{9,11},{10,... | collective-permute-start | bytes 786440 | tf_op jit(solution)/shard_map/ppermute | solution.py:49
  45.6 12.2 %collective-permute-start.5 = (bf16[128,1024]{1,0:T(8,128)(2,1)S(1)}, bf16[128,1024]{1,0:T(8,128)(2,1)S(1)}, u32[]{:S(2)}, u32[]{:S(2)}) collective-permute-start(bf16[128,1024]{1,0:T(8,128)(2,1)S(1)} %collective-permute-done.2.other_0), channel_id=1, source_target_pairs={{0,3},{1,0},{2,1},{3,2},{4,7},{5,4},{6,5},{7,6},{8,11},{9,8},{10,9... | collective-permute-start | bytes 786440 | tf_op jit(solution)/shard_map/ppermute | solution.py:49
  49.4 1.4 %copy-start.13 = (bf16[1024,128]{1,0:T(8,128)(2,1)}, bf16[1024,128]{1,0:T(8,128)(2,1)S(1)}, u32[]{:S(2)}) copy-start(bf16[1024,128]{1,0:T(8,128)(2,1)S(1)} %fusion.1) | copy-start | bytes 786436
  51.4 18.1 %all-to-all-start.1 = ((f32[32,1,128]{2,1,0:T(1,128)}), f32[32,1,128]{2,1,0:T(1,128)S(1)}, u32[]{:S(2)}, u32[]{:S(2)}) async-start(f32[32,1,128]{2,1,0:T(1,128)} %broadcast_in_dim.44), calls=%async_computation.1 | async-start | bytes 32768 | tf_op jit(solution)/shard_map/all_to_all | solution.py:31
  57.8 0.7 copy-start.10
  57.8 0.8 copy-start.11
  57.9 0.8 copy-start.12
  58.7 30.0 %copy-start.6 = (bf16[1,1024,128]{2,1,0:T(8,128)(2,1)S(1)}, bf16[1,1024,128]{2,1,0:T(8,128)(2,1)}, u32[]{:S(2)}) copy-start(bf16[1,1024,128]{2,1,0:T(8,128)(2,1)} %param.16) | copy-start | bytes 786436
  69.5 31.7 %collective-permute-start.6 = (f32[64,128]{1,0:T(8,128)}, f32[64,128]{1,0:T(8,128)S(1)}, u32[]{:S(2)}, u32[]{:S(2)}) collective-permute-start(f32[64,128]{1,0:T(8,128)} %get-tuple-element.24), channel_id=1, source_target_pairs={{0,504},{8,16},{16,8},{24,32},{32,24},{40,48},{48,40},{56,64},{64,... | collective-permute-start | bytes 98312 | tf_op jit(solution)/shard_map/ppermute | solution.py:24
  74.9 26.3 %collective-permute-start.7 = (f32[64,128]{1,0:T(8,128)}, f32[64,128]{1,0:T(8,128)S(1)}, u32[]{:S(2)}, u32[]{:S(2)}) collective-permute-start(f32[64,128]{1,0:T(8,128)} %get-tuple-element.24), channel_id=1, source_target_pairs={{0,8},{8,0},{16,24},{24,16},{32,40},{40,32},{48,56},{56,48},{64,72... | collective-permute-start | bytes 98312 | tf_op jit(solution)/shard_map/ppermute | solution.py:25
  80.1 19.8 %all-to-all-start.2 = ((f32[16,1,128]{2,1,0:T(1,128)}), f32[16,1,128]{2,1,0:T(1,128)S(1)}, u32[]{:S(2)}, u32[]{:S(2)}) async-start(f32[16,1,128]{2,1,0:T(1,128)} %broadcast_in_dim.47), calls=%async_computation.2 | async-start | bytes 16384 | tf_op jit(solution)/shard_map/all_to_all | solution.py:31
  88.7 12.4 %copy-start = (f32[1024,128]{1,0:T(8,128)S(1)}, f32[1024,128]{1,0:T(8,128)}, u32[]{:S(2)}) copy-start(f32[1024,128]{1,0:T(8,128)} %get-tuple-element.25.update) | copy-start | bytes 1572868
  88.7 12.4 %copy-start.1 = (bf16[1,1024,128]{2,1,0:T(8,128)(2,1)S(1)}, bf16[1,1024,128]{2,1,0:T(8,128)(2,1)}, u32[]{:S(2)}) copy-start(bf16[1,1024,128]{2,1,0:T(8,128)(2,1)} %param.18) | copy-start | bytes 786436

commit v5 on v4

--- a/solution.py
+++ b/solution.py
@@ -86,8 +86,7 @@
 
 
 def consensus_of(partial_sums, width):
-    total_sum = jnp.sum(spread_sum(partial_sums, ("blk_1", "tp_0")))
-    return total_sum / float(lax.axis_size(BLK) * width * width)
+    return jnp.sum(partial_sums) / float(lax.axis_size(BLK) * width * width)
 
 
 def image_starts(ids):
@@ -147,11 +146,11 @@
     for part in range(own.shape[0] // WINDOW):
         place = pl.multiple_of(spots[0] + part * WINDOW, WINDOW)
         source = own.at[part * WINDOW : (part + 1) * WINDOW, :]
-        parts.append((place, WINDOW, fetch(source, tokens.at[pl.ds(place, WINDOW), :])))
+        parts.append(fetch(source, tokens.at[pl.ds(place, WINDOW), :]))
     for index, source in enumerate((other_0, other_1, other_2, other_3)):
         size = source.shape[0]
         place = pl.multiple_of(spots[1 + index], 128)
-        parts.append((place, size, fetch(source, tokens.at[pl.ds(place, size), :])))
+        parts.append(fetch(source, tokens.at[pl.ds(place, size), :]))
     given_copy = fetch(out_grad_in, out_grad)
     late = [
         fetch(tracker_in, tracker),
@@ -161,12 +160,13 @@
     ]
     for copy in ready:
         copy.wait()
-    for place, size, copy in parts:
-        copy.wait()
-        result = jnp.dot(
-            tokens[pl.ds(place, size), :], joined[...], preferred_element_type=jnp.float32
-        )
-        projected[pl.ds(place, size), :] = result.astype(jnp.bfloat16)
+    half = own.shape[0]
+    for place, group in ((spots[0], parts[:-4]), (half - spots[0], parts[-4:])):
+        for copy in group:
+            copy.wait()
+        window = pl.ds(pl.multiple_of(place, half), half)
+        result = jnp.dot(tokens[window, :], joined[...], preferred_element_type=jnp.float32)
+        projected[window, :] = result.astype(jnp.bfloat16)
     given_copy.wait()
     total[...] = jnp.zeros_like(total)
 
@@ -175,7 +175,7 @@
     second_head = (lane >= HD).astype(jnp.float32).astype(jnp.bfloat16)
     scale = HD ** (-0.5)
 
-    @pl.loop(0, IMAGES)
+    @pl.loop(0, IMAGES, unroll=6)
     def _(image):
         start = starts[image]
         end = starts[image + 1]
@@ -242,7 +242,7 @@
             jax.ShapeDtypeStruct((rows, width), jnp.float32),
             jax.ShapeDtypeStruct((picks.shape[0], width), jnp.float32),
         ),
-        in_specs=scalars + [pl.BlockSpec(memory_space=pltpu.HBM)] * len(arrays),
+        in_specs=scalars + [pl.BlockSpec(memory_space=pl.ANY)] * len(arrays),
         out_specs=(whole,) * 5,
         scratch_shapes=[
             pltpu.VMEM((depth, 3 * width), jnp.bfloat16),
@@ -253,7 +253,7 @@
         ]
         + [pltpu.VMEM((rows, width), jnp.bfloat16)] * 5
         + [pltpu.SemaphoreType.DMA((14,))],
-        compiler_params=pltpu.CompilerParams(vmem_limit_bytes=56 * 2**20),
+        compiler_params=pltpu.CompilerParams(vmem_limit_bytes=52 * 2**20),
         cost_estimate=pl.CostEstimate(
             flops=2 * 10**9, bytes_accessed=8 * 10**6, transcendentals=8 * 10**5
         ),
@@ -333,10 +333,11 @@
         jnp.bfloat16
     )
     partial_sums = gap_rows(mixed_new, copies_new)
-    own_half, other = lax.optimization_barrier((own_half, other))
+    own_half, partial_sums = lax.optimization_barrier((own_half, partial_sums))
+    partial_sums = spread_sum(partial_sums, ("blk_0", "blk_2", "tp_1"))
+    other, partial_sums = lax.optimization_barrier((other, partial_sums))
     blocks = pass_tokens(other)
-    _, partial_sums = lax.optimization_barrier((other, partial_sums))
-    partial_sums = spread_rows(partial_sums, ("blk_0", "blk_2", "tp_1"))
+    partial_sums = spread_rows(partial_sums, ("blk_1", "tp_0"))
     spots = [high * half] + [
         (1 - high) * half + ((place - shift) % len(blocks)) * height for shift in range(len(blocks))
     ]
@@ -358,7 +359,7 @@
     )
     tracker_values, partial_sums = lax.optimization_barrier((tracker_values, partial_sums))
     near, far = swaps(tracker_values)
-    consensus = consensus_of(jnp.sum(partial_sums, axis=0, keepdims=True), model_width)
+    consensus = consensus_of(partial_sums, model_width)
     tracker_mixed_new = mix_step(picks[2][1], picks[1][1], far, near, update, tracker_mixed[0])
     return (
         weights_new[None],

time: 105 us -> 107 us (1.019)
  the two profiles are of different devices: /device:TPU:1 before, /device:TPU:8 now
where the time goes in v5:
time: 107 us; the launch traced here: 106 us
  starting transfers between devices  59 us (55%)
  waiting for transfers between devices  25.1 us (23%)
  Pallas kernels  10.5 us (10%)
  matrix products  3.75 us (4%)
  local copies, waits for them, and re-layouts  3.53 us (3%)
  between operations  2.73 us (3%)
  other arithmetic  1.93 us (2%)
    ppermute x2, starting transfers between devices, swaps(): from_far = lax.ppermute(value, BLK, far)  20.7 us
    all_to_all x1, waiting for transfers between devices, spread_tokens(): lax.all_to_all(blocks, 'tp_1', 0, 0, tiled=True).reshape(-1, value.shape[1])  11.8 us
    all_to_all x2, starting transfers between devices, spread_rows(): return lax.all_to_all(rows, axes, 0, 0, tiled=True)  11.2 us
    ppermute x3, starting transfers between devices, pass_tokens(): blocks.append(lax.ppermute(value, 'tp_1', pairs))  9.98 us
    pallas_call x1, Pallas kernels, gradient_step(): pl.pallas_call(gradient_kernel, out_shape=(narrow, narrow, narrow, jax.Sh...  8.95 us
    ppermute x1, starting transfers between devices, per_device(): other = lax.ppermute(tokens[0], 'tp_0', [(0, 1), (1, 0)])  8.22 us
    all_to_all x2, waiting for transfers between devices, spread_rows(): return lax.all_to_all(rows, axes, 0, 0, tiled=True)  7.04 us
    all_to_all x1, starting transfers between devices, spread_tokens(): lax.all_to_all(blocks, 'tp_1', 0, 0, tiled=True).reshape(-1, value.shape[1])  5.04 us
  transfers between devices with their start and end apart: 11, of which 5 were waited for; matrix products, arithmetic and copies ran while one was open for 6% of the time, Pallas kernels for 8%

profile of v5, /device:TPU:8, one launch (start us, length us, event | category | flops | bytes accessed | tf_op | source)
XLA Modules:
  0.0 106.5 jit_solution(2122385917469535145)
XLA Ops:
  0.7 0.7 constant_dynamic-slice_fusion.1
  1.4 1.8 %fusion.26 = (bf16[64,128]{1,0:T(8,128)(2,1)S(1)}, f32[64,128]{1,0:T(8,128)S(1)}) fusion(bf16[1,1024,128]{2,1,0:T(8,128)(2,1)} %param.14, bf16[1,1024,128]{2,1,0:T(8,128)(2,1)} %param.15, f32[1,1024,128]{2,1,0:T(8,128)} %param.13, bf16[1,1024,128]{2,1,0:T(8,128)(2,1)} %param.16, s32[64]{0:T(128)S(1)} %get-tuple-element.38), kind=kOutput, calls=%fused_computation.45 | convolution fusion | flops 101916672 | bytes 1360128 | tf_op jit(solution)/shard_map/dot_general | solution.py:59
  3.2 14.8 %collective-permute-start = (bf16[64,128]{1,0:T(8,128)(2,1)S(1)}, bf16[64,128]{1,0:T(8,128)(2,1)S(1)}, u32[]{:S(2)}, u32[]{:S(2)}) collective-permute-start(bf16[64,128]{1,0:T(8,128)(2,1)S(1)} %get-tuple-element.39), channel_id=1, source_target_pairs={{0,504},{8,16},{16,8},{24,32},{32,24},{40,48},{48,40},{56,64},{64,... | collective-permute-start | bytes 49160 | tf_op jit(solution)/shard_map/ppermute | solution.py:24
  18.0 1.9 %collective-permute-start.1 = (bf16[64,128]{1,0:T(8,128)(2,1)S(1)}, bf16[64,128]{1,0:T(8,128)(2,1)S(1)}, u32[]{:S(2)}, u32[]{:S(2)}) collective-permute-start(bf16[64,128]{1,0:T(8,128)(2,1)S(1)} %get-tuple-element.39), channel_id=1, source_target_pairs={{0,8},{8,0},{16,24},{24,16},{32,40},{40,32},{48,56},{56,48},{64,72... | collective-permute-start | bytes 49160 | tf_op jit(solution)/shard_map/ppermute | solution.py:25
  19.9 0.0 copy-done.9
  19.9 8.2 %collective-permute-start.2 = (bf16[128,1024]{1,0:T(8,128)(2,1)S(1)}, bf16[128,1024]{1,0:T(8,128)(2,1)S(1)}, u32[]{:S(2)}, u32[]{:S(2)}) collective-permute-start(bf16[128,1024]{1,0:T(8,128)(2,1)S(1)} %bitcast.98), channel_id=1, source_target_pairs={{0,4},{4,0},{1,5},{5,1},{2,6},{6,2},{3,7},{7,3},{8,12},{12,8},{9,1... | collective-permute-start | bytes 786440 | tf_op jit(solution)/shard_map/ppermute | solution.py:312
  28.2 1.1 %broadcast_in_dim.41 = bf16[4,128,1024]{2,1,0:T(8,128)(2,1)} broadcast(bf16[128,1024]{1,0:T(8,128)(2,1)S(1)} %bitcast.99), dimensions={1,2} | broadcast | bytes 1310720 | tf_op jit(solution)/shard_map/broadcast_in_dim | solution.py:40
  29.3 5.0 %all-to-all-start = ((bf16[4,128,1024]{2,1,0:T(8,128)(2,1)}), bf16[4,128,1024]{2,1,0:T(8,128)(2,1)}, u32[]{:S(2)}, u32[]{:S(2)}) async-start(bf16[4,128,1024]{2,1,0:T(8,128)(2,1)} %broadcast_in_dim.41), calls=%async_computation | async-start | bytes 2097152 | tf_op jit(solution)/shard_map/all_to_all | solution.py:41
  34.3 0.1 pad_add_fusion
  34.4 0.0 collective-permute-done
  34.4 0.0 collective-permute-done.1
  34.4 0.0 copy-done.6
  34.4 0.6 fusion.1
  35.0 0.0 copy-start.11
  35.0 0.3 copy-done.5
  35.4 1.4 %multiply_reduce_fusion = (f32[128]{0:T(128)S(1)}, bf16[1024,128]{1,0:T(8,128)(2,1)}) fusion(bf16[1024,128]{1,0:T(8,128)(2,1)S(1)} %fusion.1, f32[64,128]{1,0:T(8,128)S(1)} %get-tuple-element.40, s32[64]{0:T(128)S(1)} %get-tuple-element.38, bf16[1,1024,128]{2,1,0:T(8,128)(2,1)S(1)} %copy-done.5), kind=kOutput, calls=%fused_computation.19 | convolution fusion | flops 101777280 | bytes 819968 | tf_op jit(solution)/shard_map/dot_general | solution.py:64
  36.7 0.0 copy-done.11
  36.7 11.8 %all-to-all-done = bf16[4,128,1024]{2,1,0:T(8,128)(2,1)} async-done(((bf16[4,128,1024]{2,1,0:T(8,128)(2,1)}), bf16[4,128,1024]{2,1,0:T(8,128)(2,1)}, u32[]{:S(2)}, u32[]{:S(2)}) %all-to-all-start) | async-done | bytes 1048608 | tf_op jit(solution)/shard_map/all_to_all | solution.py:41
  48.5 0.6 broadcast_in_dim.43
  49.2 4.9 %all-to-all-start.1 = ((f32[32,1,128]{2,1,0:T(1,128)}), f32[32,1,128]{2,1,0:T(1,128)S(1)}, u32[]{:S(2)}, u32[]{:S(2)}) async-start(f32[32,1,128]{2,1,0:T(1,128)} %broadcast_in_dim.43), calls=%async_computation.1 | async-start | bytes 32768 | tf_op jit(solution)/shard_map/all_to_all | solution.py:31
  54.0 0.0 copy-done.10
  54.0 0.1 convert_reduce_fusion.starts
  54.2 0.1 stack.23.spots
  54.3 5.9 %all-to-all-done.1 = f32[32,1,128]{2,1,0:T(1,128)S(1)} async-done(((f32[32,1,128]{2,1,0:T(1,128)}), f32[32,1,128]{2,1,0:T(1,128)S(1)}, u32[]{:S(2)}, u32[]{:S(2)}) %all-to-all-start.1) | async-done | bytes 16416 | tf_op jit(solution)/shard_map/all_to_all | solution.py:31
  60.2 0.0 collective-permute-done.2.other_0
  60.2 0.0 copy-start.2
  60.2 0.0 copy-start.3
  60.2 2.6 %collective-permute-start.3 = (bf16[128,1024]{1,0:T(8,128)(2,1)S(1)}, bf16[128,1024]{1,0:T(8,128)(2,1)S(1)}, u32[]{:S(2)}, u32[]{:S(2)}) collective-permute-start(bf16[128,1024]{1,0:T(8,128)(2,1)S(1)} %collective-permute-done.2.other_0), channel_id=1, source_target_pairs={{0,1},{1,2},{2,3},{3,0},{4,5},{5,6},{6,7},{7,4},{8,9},{9,10},{10,1... | collective-permute-start | bytes 786440 | tf_op jit(solution)/shard_map/ppermute | solution.py:49
  62.9 4.8 %collective-permute-start.4 = (bf16[128,1024]{1,0:T(8,128)(2,1)S(1)}, bf16[128,1024]{1,0:T(8,128)(2,1)S(1)}, u32[]{:S(2)}, u32[]{:S(2)}) collective-permute-start(bf16[128,1024]{1,0:T(8,128)(2,1)S(1)} %collective-permute-done.2.other_0), channel_id=1, source_target_pairs={{0,2},{1,3},{2,0},{3,1},{4,6},{5,7},{6,4},{7,5},{8,10},{9,11},{10,... | collective-permute-start | bytes 786440 | tf_op jit(solution)/shard_map/ppermute | solution.py:49
  67.7 2.5 %collective-permute-start.5 = (bf16[128,1024]{1,0:T(8,128)(2,1)S(1)}, bf16[128,1024]{1,0:T(8,128)(2,1)S(1)}, u32[]{:S(2)}, u32[]{:S(2)}) collective-permute-start(bf16[128,1024]{1,0:T(8,128)(2,1)S(1)} %collective-permute-done.2.other_0), channel_id=1, source_target_pairs={{0,3},{1,0},{2,1},{3,2},{4,7},{5,4},{6,5},{7,6},{8,11},{9,8},{10,9... | collective-permute-start | bytes 786440 | tf_op jit(solution)/shard_map/ppermute | solution.py:49
  70.2 0.0 copy-done.4
  70.2 0.0 copy-done.7
  70.2 0.2 multiply_convert_fusion.query_weight
  70.4 0.6 broadcast_in_dim.47
  71.0 6.4 %all-to-all-start.2 = ((f32[16,1,128]{2,1,0:T(1,128)}), f32[16,1,128]{2,1,0:T(1,128)S(1)}, u32[]{:S(2)}, u32[]{:S(2)}) async-start(f32[16,1,128]{2,1,0:T(1,128)} %broadcast_in_dim.47), calls=%async_computation.2 | async-start | bytes 16384 | tf_op jit(solution)/shard_map/all_to_all | solution.py:31
  77.4 0.0 collective-permute-done.3.other_1
  77.4 0.0 collective-permute-done.4.other_2
  77.4 2.2 %collective-permute-done.5.other_3 = bf16[128,1024]{1,0:T(8,128)(2,1)S(1)} collective-permute-done((bf16[128,1024]{1,0:T(8,128)(2,1)S(1)}, bf16[128,1024]{1,0:T(8,128)(2,1)S(1)}, u32[]{:S(2)}, u32[]{:S(2)}) %collective-permute-start.5) | collective-permute-done | bytes 262176 | tf_op jit(solution)/shard_map/ppermute | solution.py:49
  79.6 0.0 copy-done.3
  79.6 8.9 %shard_map.188 = (bf16[1024,128]{1,0:T(8,128)(2,1)}, bf16[1024,128]{1,0:T(8,128)(2,1)}, bf16[1024,128]{1,0:T(8,128)(2,1)}, f32[1024,128]{1,0:T(8,128)}, f32[64,128]{1,0:T(8,128)S(1)}) custom-call(s32[5]{0:T(128)S(1)} %stack.23.spots, s32[8]{0:T(128)S(1)} %convert_reduce_fusion.starts, s32[64]{0:T(128)S(1)} %get-tuple-element.37.picks, ...), custom_call_target="tpu_custom_call" | custom-call | flops 2000000000 | bytes 8000000 | tf_op jit(solution)/shard_map/pallas_call | solution.py:236
  88.6 1.2 %all-to-all-done.2 = f32[16,1,128]{2,1,0:T(1,128)S(1)} async-done(((f32[16,1,128]{2,1,0:T(1,128)}), f32[16,1,128]{2,1,0:T(1,128)S(1)}, u32[]{:S(2)}, u32[]{:S(2)}) %all-to-all-start.2) | async-done | bytes 8224 | tf_op jit(solution)/shard_map/all_to_all | solution.py:31
  89.7 5.9 %collective-permute-start.6 = (f32[64,128]{1,0:T(8,128)S(1)}, f32[64,128]{1,0:T(8,128)S(1)}, u32[]{:S(2)}, u32[]{:S(2)}) collective-permute-start(f32[64,128]{1,0:T(8,128)S(1)} %get-tuple-element.26), channel_id=1, source_target_pairs={{0,504},{8,16},{16,8},{24,32},{32,24},{40,48},{48,40},{56,64},{64,... | collective-permute-start | bytes 98312 | tf_op jit(solution)/shard_map/ppermute | solution.py:24
  95.6 1.9 %collective-permute-start.7 = (f32[64,128]{1,0:T(8,128)S(1)}, f32[64,128]{1,0:T(8,128)S(1)}, u32[]{:S(2)}, u32[]{:S(2)}) collective-permute-start(f32[64,128]{1,0:T(8,128)S(1)} %get-tuple-element.26), channel_id=1, source_target_pairs={{0,8},{8,0},{16,24},{24,16},{32,40},{40,32},{48,56},{56,48},{64,72... | collective-permute-start | bytes 98312 | tf_op jit(solution)/shard_map/ppermute | solution.py:25
  97.6 0.9 fusion.12
  98.5 0.6 reduce_sum.39
  99.7 4.1 %collective-permute-done.6.far = f32[64,128]{1,0:T(8,128)S(1)} collective-permute-done((f32[64,128]{1,0:T(8,128)S(1)}, f32[64,128]{1,0:T(8,128)S(1)}, u32[]{:S(2)}, u32[]{:S(2)}) %collective-permute-start.6) | collective-permute-done | bytes 32800 | tf_op jit(solution)/shard_map/ppermute | solution.py:24
  103.8 0.0 collective-permute-done.7.near
  103.8 1.5 %shard_map.189 = bf16[1024,128]{1,0:T(8,128)(2,1)} custom-call(s32[64]{0:T(128)S(1)} %get-tuple-element.44.far_picks, s32[64]{0:T(128)S(1)} %get-tuple-element.33.near_picks, f32[64,128]{1,0:T(8,128)S(1)} %collective-permute-done.6.far, f32[64,128]{1,0:T(8,128)S(1)} %collective-permute-done.7.near, f32[1024,128]{1,0:T(8,128)S(1)} %copy-done, ...), custom_call_target="tpu_custom_call" | custom-call | flops 1000000 | bytes 1000000 | tf_op jit(solution)/shard_map/pallas_call | solution.py:281
  (16 shorter events, 0.1 us)
Async XLA Ops:
  1.4 18.5 %copy-start.9 = (bf16[1,128,1024]{2,1,0:T(8,128)(2,1)S(1)}, bf16[1,128,1024]{2,1,0:T(8,128)(2,1)}, u32[]{:S(2)}) copy-start(bf16[1,128,1024]{2,1,0:T(8,128)(2,1)} %param.20) | copy-start | bytes 786436
  3.2 31.2 %collective-permute-start = (bf16[64,128]{1,0:T(8,128)(2,1)S(1)}, bf16[64,128]{1,0:T(8,128)(2,1)S(1)}, u32[]{:S(2)}, u32[]{:S(2)}) collective-permute-start(bf16[64,128]{1,0:T(8,128)(2,1)S(1)} %get-tuple-element.39), channel_id=1, source_target_pairs={{0,504},{8,16},{16,8},{24,32},{32,24},{40,48},{48,40},{56,64},{64,... | collective-permute-start | bytes 49160 | tf_op jit(solution)/shard_map/ppermute | solution.py:24
  18.0 16.4 %collective-permute-start.1 = (bf16[64,128]{1,0:T(8,128)(2,1)S(1)}, bf16[64,128]{1,0:T(8,128)(2,1)S(1)}, u32[]{:S(2)}, u32[]{:S(2)}) collective-permute-start(bf16[64,128]{1,0:T(8,128)(2,1)S(1)} %get-tuple-element.39), channel_id=1, source_target_pairs={{0,8},{8,0},{16,24},{24,16},{32,40},{40,32},{48,56},{56,48},{64,72... | collective-permute-start | bytes 49160 | tf_op jit(solution)/shard_map/ppermute | solution.py:25
  19.9 40.3 %collective-permute-start.2 = (bf16[128,1024]{1,0:T(8,128)(2,1)S(1)}, bf16[128,1024]{1,0:T(8,128)(2,1)S(1)}, u32[]{:S(2)}, u32[]{:S(2)}) collective-permute-start(bf16[128,1024]{1,0:T(8,128)(2,1)S(1)} %bitcast.98), channel_id=1, source_target_pairs={{0,4},{4,0},{1,5},{5,1},{2,6},{6,2},{3,7},{7,3},{8,12},{12,8},{9,1... | collective-permute-start | bytes 786440 | tf_op jit(solution)/shard_map/ppermute | solution.py:312
  29.3 5.1 %copy-start.6 = (bf16[1,1024,128]{2,1,0:T(8,128)(2,1)S(1)}, bf16[1,1024,128]{2,1,0:T(8,128)(2,1)}, u32[]{:S(2)}) copy-start(bf16[1,1024,128]{2,1,0:T(8,128)(2,1)} %param.15) | copy-start | bytes 786436
  29.3 19.3 %all-to-all-start = ((bf16[4,128,1024]{2,1,0:T(8,128)(2,1)}), bf16[4,128,1024]{2,1,0:T(8,128)(2,1)}, u32[]{:S(2)}, u32[]{:S(2)}) async-start(bf16[4,128,1024]{2,1,0:T(8,128)(2,1)} %broadcast_in_dim.41), calls=%async_computation | async-start | bytes 2097152 | tf_op jit(solution)/shard_map/all_to_all | solution.py:41
  34.4 0.9 copy-start.5
  35.0 1.7 %copy-start.11 = (bf16[1024,128]{1,0:T(8,128)(2,1)}, bf16[1024,128]{1,0:T(8,128)(2,1)S(1)}, u32[]{:S(2)}) copy-start(bf16[1024,128]{1,0:T(8,128)(2,1)S(1)} %fusion.1) | copy-start | bytes 786436
  35.4 18.7 %copy-start.10 = (s32[1,1024]{1,0:T(1,128)S(1)}, s32[1,1024]{1,0:T(1,128)}, u32[]{:S(2)}) copy-start(s32[1,1024]{1,0:T(1,128)} %param.21) | copy-start | bytes 12292
  35.4 34.9 %copy-start.4 = (f32[1,1024,128]{2,1,0:T(8,128)S(1)}, f32[1,1024,128]{2,1,0:T(8,128)}, u32[]{:S(2)}) copy-start(f32[1,1024,128]{2,1,0:T(8,128)} %param.13) | copy-start | bytes 1572868
  35.4 34.9 %copy-start.7 = (bf16[1,1024,128]{2,1,0:T(8,128)(2,1)S(1)}, bf16[1,1024,128]{2,1,0:T(8,128)(2,1)}, u32[]{:S(2)}) copy-start(bf16[1,1024,128]{2,1,0:T(8,128)(2,1)} %param.16) | copy-start | bytes 786436
  49.2 11.0 %all-to-all-start.1 = ((f32[32,1,128]{2,1,0:T(1,128)}), f32[32,1,128]{2,1,0:T(1,128)S(1)}, u32[]{:S(2)}, u32[]{:S(2)}) async-start(f32[32,1,128]{2,1,0:T(1,128)} %broadcast_in_dim.43), calls=%async_computation.1 | async-start | bytes 32768 | tf_op jit(solution)/shard_map/all_to_all | solution.py:31
  60.2 19.4 %copy-start.2 = (bf16[1024,128]{1,0:T(8,128)(2,1)S(1)}, bf16[1024,128]{1,0:T(8,128)(2,1)}, u32[]{:S(2)}) copy-start(bf16[1024,128]{1,0:T(8,128)(2,1)} %key_weight.1) | copy-start | bytes 786436
  60.2 19.4 %copy-start.3 = (bf16[1024,128]{1,0:T(8,128)(2,1)S(1)}, bf16[1024,128]{1,0:T(8,128)(2,1)}, u32[]{:S(2)}) copy-start(bf16[1024,128]{1,0:T(8,128)(2,1)} %value_weight.1) | copy-start | bytes 786436
  60.2 17.2 %collective-permute-start.3 = (bf16[128,1024]{1,0:T(8,128)(2,1)S(1)}, bf16[128,1024]{1,0:T(8,128)(2,1)S(1)}, u32[]{:S(2)}, u32[]{:S(2)}) collective-permute-start(bf16[128,1024]{1,0:T(8,128)(2,1)S(1)} %collective-permute-done.2.other_0), channel_id=1, source_target_pairs={{0,1},{1,2},{2,3},{3,0},{4,5},{5,6},{6,7},{7,4},{8,9},{9,10},{10,1... | collective-permute-start | bytes 786440 | tf_op jit(solution)/shard_map/ppermute | solution.py:49
  62.9 14.5 %collective-permute-start.4 = (bf16[128,1024]{1,0:T(8,128)(2,1)S(1)}, bf16[128,1024]{1,0:T(8,128)(2,1)S(1)}, u32[]{:S(2)}, u32[]{:S(2)}) collective-permute-start(bf16[128,1024]{1,0:T(8,128)(2,1)S(1)} %collective-permute-done.2.other_0), channel_id=1, source_target_pairs={{0,2},{1,3},{2,0},{3,1},{4,6},{5,7},{6,4},{7,5},{8,10},{9,11},{10,... | collective-permute-start | bytes 786440 | tf_op jit(solution)/shard_map/ppermute | solution.py:49
  67.7 11.9 %collective-permute-start.5 = (bf16[128,1024]{1,0:T(8,128)(2,1)S(1)}, bf16[128,1024]{1,0:T(8,128)(2,1)S(1)}, u32[]{:S(2)}, u32[]{:S(2)}) collective-permute-start(bf16[128,1024]{1,0:T(8,128)(2,1)S(1)} %collective-permute-done.2.other_0), channel_id=1, source_target_pairs={{0,3},{1,0},{2,1},{3,2},{4,7},{5,4},{6,5},{7,6},{8,11},{9,8},{10,9... | collective-permute-start | bytes 786440 | tf_op jit(solution)/shard_map/ppermute | solution.py:49
  71.0 18.7 %all-to-all-start.2 = ((f32[16,1,128]{2,1,0:T(1,128)}), f32[16,1,128]{2,1,0:T(1,128)S(1)}, u32[]{:S(2)}, u32[]{:S(2)}) async-start(f32[16,1,128]{2,1,0:T(1,128)} %broadcast_in_dim.47), calls=%async_computation.2 | async-start | bytes 16384 | tf_op jit(solution)/shard_map/all_to_all | solution.py:31
  79.6 17.9 %copy-start.8 = (bf16[1,1024,128]{2,1,0:T(8,128)(2,1)S(1)}, bf16[1,1024,128]{2,1,0:T(8,128)(2,1)}, u32[]{:S(2)}) copy-start(bf16[1,1024,128]{2,1,0:T(8,128)(2,1)} %param.16) | copy-start | bytes 786436
  89.7 14.1 %copy-start = (f32[1024,128]{1,0:T(8,128)S(1)}, f32[1024,128]{1,0:T(8,128)}, u32[]{:S(2)}) copy-start(f32[1024,128]{1,0:T(8,128)} %get-tuple-element.27.update) | copy-start | bytes 1572868
  89.7 14.1 %copy-start.1 = (bf16[1,1024,128]{2,1,0:T(8,128)(2,1)S(1)}, bf16[1,1024,128]{2,1,0:T(8,128)(2,1)}, u32[]{:S(2)}) copy-start(bf16[1,1024,128]{2,1,0:T(8,128)(2,1)} %param.18) | copy-start | bytes 786436
  89.7 14.1 %collective-permute-start.6 = (f32[64,128]{1,0:T(8,128)S(1)}, f32[64,128]{1,0:T(8,128)S(1)}, u32[]{:S(2)}, u32[]{:S(2)}) collective-permute-start(f32[64,128]{1,0:T(8,128)S(1)} %get-tuple-element.26), channel_id=1, source_target_pairs={{0,504},{8,16},{16,8},{24,32},{32,24},{40,48},{48,40},{56,64},{64,... | collective-permute-start | bytes 98312 | tf_op jit(solution)/shard_map/ppermute | solution.py:24
  95.6 8.2 %collective-permute-start.7 = (f32[64,128]{1,0:T(8,128)S(1)}, f32[64,128]{1,0:T(8,128)S(1)}, u32[]{:S(2)}, u32[]{:S(2)}) collective-permute-start(f32[64,128]{1,0:T(8,128)S(1)} %get-tuple-element.26), channel_id=1, source_target_pairs={{0,8},{8,0},{16,24},{24,16},{32,40},{40,32},{48,56},{56,48},{64,72... | collective-permute-start | bytes 98312 | tf_op jit(solution)/shard_map/ppermute | solution.py:25

commit v6 on v5

--- a/solution.py
+++ b/solution.py
@@ -333,10 +333,9 @@
         jnp.bfloat16
     )
     partial_sums = gap_rows(mixed_new, copies_new)
-    own_half, partial_sums = lax.optimization_barrier((own_half, partial_sums))
-    partial_sums = spread_sum(partial_sums, ("blk_0", "blk_2", "tp_1"))
-    other, partial_sums = lax.optimization_barrier((other, partial_sums))
+    own_half, other = lax.optimization_barrier((own_half, other))
     blocks = pass_tokens(other)
+    _, partial_sums = lax.optimization_barrier((other, partial_sums))
     partial_sums = spread_rows(partial_sums, ("blk_1", "tp_0"))
     spots = [high * half] + [
         (1 - high) * half + ((place - shift) % len(blocks)) * height for shift in range(len(blocks))
@@ -359,8 +358,14 @@
     )
     tracker_values, partial_sums = lax.optimization_barrier((tracker_values, partial_sums))
     near, far = swaps(tracker_values)
+    partial_sums = spread_rows(
+        jnp.sum(partial_sums, axis=0, keepdims=True), ("blk_0", "blk_2", "tp_1")
+    )
+    tracker_mixed_new = mix_step(
+        picks[2][1], picks[1][1], far, near, update, tracker_mixed[0]
+    )
+    tracker_mixed_new, partial_sums = lax.optimization_barrier((tracker_mixed_new, partial_sums))
     consensus = consensus_of(partial_sums, model_width)
-    tracker_mixed_new = mix_step(picks[2][1], picks[1][1], far, near, update, tracker_mixed[0])
     return (
         weights_new[None],
         copies_new[None],

time: 107 us -> 102 us (0.953)
  the two profiles are of different devices: /device:TPU:8 before, /device:TPU:1 now
where the time goes in v6:
time: 102 us; the launch traced here: 101 us
  starting transfers between devices  70.7 us (69%)
  Pallas kernels  10.5 us (10%)
  waiting for transfers between devices  7.97 us (8%)
  local copies, waits for them, and re-layouts  5.11 us (5%)
  between operations  2.72 us (3%)
  matrix products  2.45 us (2%)
  other arithmetic  1.93 us (2%)
    all_to_all x2, starting transfers between devices, spread_rows(): return lax.all_to_all(rows, axes, 0, 0, tiled=True)  18.9 us
    ppermute x1, starting transfers between devices, per_device(): other = lax.ppermute(tokens[0], 'tp_0', [(0, 1), (1, 0)])  16.3 us
    ppermute x2, starting transfers between devices, swaps(): return (lax.ppermute(value, BLK, near), from_far)  12.6 us
    ppermute x2, starting transfers between devices, swaps(): from_far = lax.ppermute(value, BLK, far)  9.46 us
    ppermute x3, starting transfers between devices, pass_tokens(): blocks.append(lax.ppermute(value, 'tp_1', pairs))  9.08 us
    pallas_call x1, Pallas kernels, gradient_step(): pl.pallas_call(gradient_kernel, out_shape=(narrow, narrow, narrow, jax.Sh...  8.95 us
    all_to_all x2, waiting for transfers between devices, spread_rows(): return lax.all_to_all(rows, axes, 0, 0, tiled=True)  6.32 us
    all_to_all x1, starting transfers between devices, spread_tokens(): lax.all_to_all(blocks, 'tp_1', 0, 0, tiled=True).reshape(-1, value.shape[1])  4.38 us
  transfers between devices with their start and end apart: 11, of which 3 were waited for; matrix products, arithmetic and copies ran while one was open for 8% of the time, Pallas kernels for 10%

profile of v6, /device:TPU:1, one launch (start us, length us, event | category | flops | bytes accessed | tf_op | source)
XLA Modules:
  0.0 101.3 jit_solution(598354008136372741)
XLA Ops:
  0.6 16.3 %collective-permute-start.2 = (bf16[128,1024]{1,0:T(8,128)(2,1)}, bf16[128,1024]{1,0:T(8,128)(2,1)S(1)}, u32[]{:S(2)}, u32[]{:S(2)}) collective-permute-start(bf16[128,1024]{1,0:T(8,128)(2,1)} %bitcast.96), channel_id=1, source_target_pairs={{0,4},{4,0},{1,5},{5,1},{2,6},{6,2},{3,7},{7,3},{8,12},{12,8},{9,1... | collective-permute-start | bytes 786440 | tf_op jit(solution)/shard_map/ppermute | solution.py:312
  16.9 2.1 %broadcast_in_dim.39 = bf16[4,128,1024]{2,1,0:T(8,128)(2,1)} broadcast(bf16[128,1024]{1,0:T(8,128)(2,1)} %bitcast.97), dimensions={1,2} | broadcast | bytes 1310720 | tf_op jit(solution)/shard_map/broadcast_in_dim | solution.py:40
  19.0 4.4 %all-to-all-start = ((bf16[4,128,1024]{2,1,0:T(8,128)(2,1)}), bf16[4,128,1024]{2,1,0:T(8,128)(2,1)}, u32[]{:S(2)}, u32[]{:S(2)}) async-start(bf16[4,128,1024]{2,1,0:T(8,128)(2,1)} %broadcast_in_dim.39), calls=%async_computation | async-start | bytes 2097152 | tf_op jit(solution)/shard_map/all_to_all | solution.py:41
  23.4 0.7 constant_dynamic-slice_fusion.1
  24.1 0.0 copy-done.4
  24.2 0.5 fusion.26
  24.7 3.7 %collective-permute-start = (bf16[64,128]{1,0:T(8,128)(2,1)S(1)}, bf16[64,128]{1,0:T(8,128)(2,1)S(1)}, u32[]{:S(2)}, u32[]{:S(2)}) collective-permute-start(bf16[64,128]{1,0:T(8,128)(2,1)S(1)} %get-tuple-element.41), channel_id=1, source_target_pairs={{0,504},{8,16},{16,8},{24,32},{32,24},{40,48},{48,40},{56,64},{64,... | collective-permute-start | bytes 49160 | tf_op jit(solution)/shard_map/ppermute | solution.py:24
  28.3 6.2 %collective-permute-start.1 = (bf16[64,128]{1,0:T(8,128)(2,1)S(1)}, bf16[64,128]{1,0:T(8,128)(2,1)S(1)}, u32[]{:S(2)}, u32[]{:S(2)}) collective-permute-start(bf16[64,128]{1,0:T(8,128)(2,1)S(1)} %get-tuple-element.41), channel_id=1, source_target_pairs={{0,8},{8,0},{16,24},{24,16},{32,40},{40,32},{48,56},{56,48},{64,72... | collective-permute-start | bytes 49160 | tf_op jit(solution)/shard_map/ppermute | solution.py:25
  34.6 0.2 multiply_convert_fusion.query_weight
  34.7 0.0 copy-start.9
  34.8 0.7 copy-done.9
  35.4 0.1 convert_reduce_fusion.starts
  35.5 0.1 pad_add_fusion
  35.6 0.1 stack.23.spots
  35.7 0.0 collective-permute-done.2.other_0
  35.7 1.6 %all-to-all-done = bf16[4,128,1024]{2,1,0:T(8,128)(2,1)} async-done(((bf16[4,128,1024]{2,1,0:T(8,128)(2,1)}), bf16[4,128,1024]{2,1,0:T(8,128)(2,1)}, u32[]{:S(2)}, u32[]{:S(2)}) %all-to-all-start) | async-done | bytes 1048608 | tf_op jit(solution)/shard_map/all_to_all | solution.py:41
  37.3 2.4 %collective-permute-start.3 = (bf16[128,1024]{1,0:T(8,128)(2,1)S(1)}, bf16[128,1024]{1,0:T(8,128)(2,1)S(1)}, u32[]{:S(2)}, u32[]{:S(2)}) collective-permute-start(bf16[128,1024]{1,0:T(8,128)(2,1)S(1)} %collective-permute-done.2.other_0), channel_id=1, source_target_pairs={{0,1},{1,2},{2,3},{3,0},{4,5},{5,6},{6,7},{7,4},{8,9},{9,10},{10,1... | collective-permute-start | bytes 786440 | tf_op jit(solution)/shard_map/ppermute | solution.py:49
  39.7 3.8 %collective-permute-start.4 = (bf16[128,1024]{1,0:T(8,128)(2,1)S(1)}, bf16[128,1024]{1,0:T(8,128)(2,1)S(1)}, u32[]{:S(2)}, u32[]{:S(2)}) collective-permute-start(bf16[128,1024]{1,0:T(8,128)(2,1)S(1)} %collective-permute-done.2.other_0), channel_id=1, source_target_pairs={{0,2},{1,3},{2,0},{3,1},{4,6},{5,7},{6,4},{7,5},{8,10},{9,11},{10,... | collective-permute-start | bytes 786440 | tf_op jit(solution)/shard_map/ppermute | solution.py:49
  43.5 3.0 %collective-permute-start.5 = (bf16[128,1024]{1,0:T(8,128)(2,1)S(1)}, bf16[128,1024]{1,0:T(8,128)(2,1)S(1)}, u32[]{:S(2)}, u32[]{:S(2)}) collective-permute-start(bf16[128,1024]{1,0:T(8,128)(2,1)S(1)} %collective-permute-done.2.other_0), channel_id=1, source_target_pairs={{0,3},{1,0},{2,1},{3,2},{4,7},{5,4},{6,5},{7,6},{8,11},{9,8},{10,9... | collective-permute-start | bytes 786440 | tf_op jit(solution)/shard_map/ppermute | solution.py:49
  46.4 0.0 collective-permute-done
  46.5 0.0 collective-permute-done.1
  46.5 0.6 fusion.1
  47.0 0.0 copy-start.10
  47.1 0.0 copy-start.2
  47.1 0.0 copy-start.3
  47.1 1.4 %multiply_reduce_fusion = (f32[128]{0:T(128)S(1)}, bf16[1024,128]{1,0:T(8,128)(2,1)}) fusion(bf16[1024,128]{1,0:T(8,128)(2,1)S(1)} %fusion.1, f32[64,128]{1,0:T(8,128)S(1)} %get-tuple-element.42, s32[64]{0:T(128)S(1)} %get-tuple-element.40, bf16[1,1024,128]{2,1,0:T(8,128)(2,1)S(1)} %copy-done.5), kind=kOutput, calls=%fused_computation.18 | convolution fusion | flops 101777280 | bytes 819968 | tf_op jit(solution)/shard_map/dot_general | solution.py:64
  48.5 0.6 broadcast_in_dim.43
  49.1 15.3 %all-to-all-start.1 = ((f32[16,1,128]{2,1,0:T(1,128)}), f32[16,1,128]{2,1,0:T(1,128)S(1)}, u32[]{:S(2)}, u32[]{:S(2)}) async-start(f32[16,1,128]{2,1,0:T(1,128)} %broadcast_in_dim.43), calls=%async_computation.1 | async-start | bytes 16384 | tf_op jit(solution)/shard_map/all_to_all | solution.py:31
  64.4 0.0 collective-permute-done.3.other_1
  64.4 0.0 collective-permute-done.4.other_2
  64.4 0.0 collective-permute-done.5.other_3
  64.4 0.0 copy-start.8
  64.5 9.0 %shard_map.188 = (bf16[1024,128]{1,0:T(8,128)(2,1)}, bf16[1024,128]{1,0:T(8,128)(2,1)}, bf16[1024,128]{1,0:T(8,128)(2,1)}, f32[1024,128]{1,0:T(8,128)}, f32[64,128]{1,0:T(8,128)S(1)}) custom-call(s32[5]{0:T(128)S(1)} %stack.23.spots, s32[8]{0:T(128)S(1)} %convert_reduce_fusion.starts, s32[64]{0:T(128)S(1)} %get-tuple-element.39.picks, ...), custom_call_target="tpu_custom_call" | custom-call | flops 2000000000 | bytes 8000000 | tf_op jit(solution)/shard_map/pallas_call | solution.py:236
  73.4 2.2 %all-to-all-done.1 = f32[16,1,128]{2,1,0:T(1,128)S(1)} async-done(((f32[16,1,128]{2,1,0:T(1,128)}), f32[16,1,128]{2,1,0:T(1,128)S(1)}, u32[]{:S(2)}, u32[]{:S(2)}) %all-to-all-start.1) | async-done | bytes 8224 | tf_op jit(solution)/shard_map/all_to_all | solution.py:31
  75.6 5.8 %collective-permute-start.6 = (f32[64,128]{1,0:T(8,128)S(1)}, f32[64,128]{1,0:T(8,128)S(1)}, u32[]{:S(2)}, u32[]{:S(2)}) collective-permute-start(f32[64,128]{1,0:T(8,128)S(1)} %get-tuple-element.26), channel_id=1, source_target_pairs={{0,504},{8,16},{16,8},{24,32},{32,24},{40,48},{48,40},{56,64},{64,... | collective-permute-start | bytes 98312 | tf_op jit(solution)/shard_map/ppermute | solution.py:24
  81.4 6.4 %collective-permute-start.7 = (f32[64,128]{1,0:T(8,128)S(1)}, f32[64,128]{1,0:T(8,128)S(1)}, u32[]{:S(2)}, u32[]{:S(2)}) collective-permute-start(f32[64,128]{1,0:T(8,128)S(1)} %get-tuple-element.26), channel_id=1, source_target_pairs={{0,8},{8,0},{16,24},{24,16},{32,40},{40,32},{48,56},{56,48},{64,72... | collective-permute-start | bytes 98312 | tf_op jit(solution)/shard_map/ppermute | solution.py:25
  87.8 0.6 broadcast_in_dim.44
  88.4 3.6 %all-to-all-start.2 = ((f32[32,1,128]{2,1,0:T(1,128)}), f32[32,1,128]{2,1,0:T(1,128)S(1)}, u32[]{:S(2)}, u32[]{:S(2)}) async-start(f32[32,1,128]{2,1,0:T(1,128)} %broadcast_in_dim.44), calls=%async_computation.2 | async-start | bytes 32768 | tf_op jit(solution)/shard_map/all_to_all | solution.py:31
  92.0 0.0 copy-done.8
  92.0 0.0 copy-start.1
  92.0 0.9 fusion.12
  93.0 0.0 collective-permute-done.6.far
  93.0 0.0 collective-permute-done.7.near
  93.0 0.1 copy-done
  93.0 0.2 copy-done.1
  93.3 1.5 %shard_map.189 = bf16[1024,128]{1,0:T(8,128)(2,1)} custom-call(s32[64]{0:T(128)S(1)} %get-tuple-element.46.far_picks, s32[64]{0:T(128)S(1)} %get-tuple-element.35.near_picks, f32[64,128]{1,0:T(8,128)S(1)} %collective-permute-done.6.far, f32[64,128]{1,0:T(8,128)S(1)} %collective-permute-done.7.near, f32[1024,128]{1,0:T(8,128)S(1)} %copy-done, ...), custom_call_target="tpu_custom_call" | custom-call | flops 1000000 | bytes 1000000 | tf_op jit(solution)/shard_map/pallas_call | solution.py:281
  94.8 4.2 %all-to-all-done.2 = f32[32,1,128]{2,1,0:T(1,128)S(1)} async-done(((f32[32,1,128]{2,1,0:T(1,128)}), f32[32,1,128]{2,1,0:T(1,128)S(1)}, u32[]{:S(2)}, u32[]{:S(2)}) %all-to-all-start.2) | async-done | bytes 16416 | tf_op jit(solution)/shard_map/all_to_all | solution.py:31
  99.0 0.6 reduce_sum.39
  (14 shorter events, 0.1 us)
Async XLA Ops:
  0.6 35.1 %collective-permute-start.2 = (bf16[128,1024]{1,0:T(8,128)(2,1)}, bf16[128,1024]{1,0:T(8,128)(2,1)S(1)}, u32[]{:S(2)}, u32[]{:S(2)}) collective-permute-start(bf16[128,1024]{1,0:T(8,128)(2,1)} %bitcast.96), channel_id=1, source_target_pairs={{0,4},{4,0},{1,5},{5,1},{2,6},{6,2},{3,7},{7,3},{8,12},{12,8},{9,1... | collective-permute-start | bytes 786440 | tf_op jit(solution)/shard_map/ppermute | solution.py:312
  19.0 5.2 %copy-start.4 = (f32[1,1024,128]{2,1,0:T(8,128)S(1)}, f32[1,1024,128]{2,1,0:T(8,128)}, u32[]{:S(2)}) copy-start(f32[1,1024,128]{2,1,0:T(8,128)} %param.13) | copy-start | bytes 1572868
  19.0 5.2 %copy-start.5 = (bf16[1,1024,128]{2,1,0:T(8,128)(2,1)S(1)}, bf16[1,1024,128]{2,1,0:T(8,128)(2,1)}, u32[]{:S(2)}) copy-start(bf16[1,1024,128]{2,1,0:T(8,128)(2,1)} %param.14) | copy-start | bytes 786436
  19.0 5.2 %copy-start.6 = (bf16[1,1024,128]{2,1,0:T(8,128)(2,1)S(1)}, bf16[1,1024,128]{2,1,0:T(8,128)(2,1)}, u32[]{:S(2)}) copy-start(bf16[1,1024,128]{2,1,0:T(8,128)(2,1)} %param.15) | copy-start | bytes 786436
  19.0 5.2 %copy-start.7 = (bf16[1,1024,128]{2,1,0:T(8,128)(2,1)S(1)}, bf16[1,1024,128]{2,1,0:T(8,128)(2,1)}, u32[]{:S(2)}) copy-start(bf16[1,1024,128]{2,1,0:T(8,128)(2,1)} %param.16) | copy-start | bytes 786436
  19.0 18.3 %all-to-all-start = ((bf16[4,128,1024]{2,1,0:T(8,128)(2,1)}), bf16[4,128,1024]{2,1,0:T(8,128)(2,1)}, u32[]{:S(2)}, u32[]{:S(2)}) async-start(bf16[4,128,1024]{2,1,0:T(8,128)(2,1)} %broadcast_in_dim.39), calls=%async_computation | async-start | bytes 2097152 | tf_op jit(solution)/shard_map/all_to_all | solution.py:41
  24.7 21.8 %collective-permute-start = (bf16[64,128]{1,0:T(8,128)(2,1)S(1)}, bf16[64,128]{1,0:T(8,128)(2,1)S(1)}, u32[]{:S(2)}, u32[]{:S(2)}) collective-permute-start(bf16[64,128]{1,0:T(8,128)(2,1)S(1)} %get-tuple-element.41), channel_id=1, source_target_pairs={{0,504},{8,16},{16,8},{24,32},{32,24},{40,48},{48,40},{56,64},{64,... | collective-permute-start | bytes 49160 | tf_op jit(solution)/shard_map/ppermute | solution.py:24
  28.3 18.1 %collective-permute-start.1 = (bf16[64,128]{1,0:T(8,128)(2,1)S(1)}, bf16[64,128]{1,0:T(8,128)(2,1)S(1)}, u32[]{:S(2)}, u32[]{:S(2)}) collective-permute-start(bf16[64,128]{1,0:T(8,128)(2,1)S(1)} %get-tuple-element.41), channel_id=1, source_target_pairs={{0,8},{8,0},{16,24},{24,16},{32,40},{40,32},{48,56},{56,48},{64,72... | collective-permute-start | bytes 49160 | tf_op jit(solution)/shard_map/ppermute | solution.py:25
  34.7 0.7 copy-start.9
  37.3 27.1 %collective-permute-start.3 = (bf16[128,1024]{1,0:T(8,128)(2,1)S(1)}, bf16[128,1024]{1,0:T(8,128)(2,1)S(1)}, u32[]{:S(2)}, u32[]{:S(2)}) collective-permute-start(bf16[128,1024]{1,0:T(8,128)(2,1)S(1)} %collective-permute-done.2.other_0), channel_id=1, source_target_pairs={{0,1},{1,2},{2,3},{3,0},{4,5},{5,6},{6,7},{7,4},{8,9},{9,10},{10,1... | collective-permute-start | bytes 786440 | tf_op jit(solution)/shard_map/ppermute | solution.py:49
  39.7 24.7 %collective-permute-start.4 = (bf16[128,1024]{1,0:T(8,128)(2,1)S(1)}, bf16[128,1024]{1,0:T(8,128)(2,1)S(1)}, u32[]{:S(2)}, u32[]{:S(2)}) collective-permute-start(bf16[128,1024]{1,0:T(8,128)(2,1)S(1)} %collective-permute-done.2.other_0), channel_id=1, source_target_pairs={{0,2},{1,3},{2,0},{3,1},{4,6},{5,7},{6,4},{7,5},{8,10},{9,11},{10,... | collective-permute-start | bytes 786440 | tf_op jit(solution)/shard_map/ppermute | solution.py:49
  43.5 21.0 %collective-permute-start.5 = (bf16[128,1024]{1,0:T(8,128)(2,1)S(1)}, bf16[128,1024]{1,0:T(8,128)(2,1)S(1)}, u32[]{:S(2)}, u32[]{:S(2)}) collective-permute-start(bf16[128,1024]{1,0:T(8,128)(2,1)S(1)} %collective-permute-done.2.other_0), channel_id=1, source_target_pairs={{0,3},{1,0},{2,1},{3,2},{4,7},{5,4},{6,5},{7,6},{8,11},{9,8},{10,9... | collective-permute-start | bytes 786440 | tf_op jit(solution)/shard_map/ppermute | solution.py:49
  47.0 1.4 %copy-start.10 = (bf16[1024,128]{1,0:T(8,128)(2,1)}, bf16[1024,128]{1,0:T(8,128)(2,1)S(1)}, u32[]{:S(2)}) copy-start(bf16[1024,128]{1,0:T(8,128)(2,1)S(1)} %fusion.1) | copy-start | bytes 786436
  47.1 17.4 %copy-start.2 = (bf16[1024,128]{1,0:T(8,128)(2,1)S(1)}, bf16[1024,128]{1,0:T(8,128)(2,1)}, u32[]{:S(2)}) copy-start(bf16[1024,128]{1,0:T(8,128)(2,1)} %key_weight.1) | copy-start | bytes 786436
  47.1 17.4 %copy-start.3 = (bf16[1024,128]{1,0:T(8,128)(2,1)S(1)}, bf16[1024,128]{1,0:T(8,128)(2,1)}, u32[]{:S(2)}) copy-start(bf16[1024,128]{1,0:T(8,128)(2,1)} %value_weight.1) | copy-start | bytes 786436
  49.1 26.5 %all-to-all-start.1 = ((f32[16,1,128]{2,1,0:T(1,128)}), f32[16,1,128]{2,1,0:T(1,128)S(1)}, u32[]{:S(2)}, u32[]{:S(2)}) async-start(f32[16,1,128]{2,1,0:T(1,128)} %broadcast_in_dim.43), calls=%async_computation.1 | async-start | bytes 16384 | tf_op jit(solution)/shard_map/all_to_all | solution.py:31
  64.4 27.6 %copy-start.8 = (bf16[1,1024,128]{2,1,0:T(8,128)(2,1)S(1)}, bf16[1,1024,128]{2,1,0:T(8,128)(2,1)}, u32[]{:S(2)}) copy-start(bf16[1,1024,128]{2,1,0:T(8,128)(2,1)} %param.16) | copy-start | bytes 786436
  75.6 17.4 %collective-permute-start.6 = (f32[64,128]{1,0:T(8,128)S(1)}, f32[64,128]{1,0:T(8,128)S(1)}, u32[]{:S(2)}, u32[]{:S(2)}) collective-permute-start(f32[64,128]{1,0:T(8,128)S(1)} %get-tuple-element.26), channel_id=1, source_target_pairs={{0,504},{8,16},{16,8},{24,32},{32,24},{40,48},{48,40},{56,64},{64,... | collective-permute-start | bytes 98312 | tf_op jit(solution)/shard_map/ppermute | solution.py:24
  81.4 11.6 %collective-permute-start.7 = (f32[64,128]{1,0:T(8,128)S(1)}, f32[64,128]{1,0:T(8,128)S(1)}, u32[]{:S(2)}, u32[]{:S(2)}) collective-permute-start(f32[64,128]{1,0:T(8,128)S(1)} %get-tuple-element.26), channel_id=1, source_target_pairs={{0,8},{8,0},{16,24},{24,16},{32,40},{40,32},{48,56},{56,48},{64,72... | collective-permute-start | bytes 98312 | tf_op jit(solution)/shard_map/ppermute | solution.py:25
  88.4 10.5 %all-to-all-start.2 = ((f32[32,1,128]{2,1,0:T(1,128)}), f32[32,1,128]{2,1,0:T(1,128)S(1)}, u32[]{:S(2)}, u32[]{:S(2)}) async-start(f32[32,1,128]{2,1,0:T(1,128)} %broadcast_in_dim.44), calls=%async_computation.2 | async-start | bytes 32768 | tf_op jit(solution)/shard_map/all_to_all | solution.py:31
  92.0 1.0 %copy-start = (f32[1024,128]{1,0:T(8,128)S(1)}, f32[1024,128]{1,0:T(8,128)}, u32[]{:S(2)}) copy-start(f32[1024,128]{1,0:T(8,128)} %get-tuple-element.27.update) | copy-start | bytes 1572868
  92.0 1.2 %copy-start.1 = (bf16[1,1024,128]{2,1,0:T(8,128)(2,1)S(1)}, bf16[1,1024,128]{2,1,0:T(8,128)(2,1)}, u32[]{:S(2)}) copy-start(bf16[1,1024,128]{2,1,0:T(8,128)(2,1)} %param.18) | copy-start | bytes 786436

commit v7 on v6

--- a/solution.py
+++ b/solution.py
@@ -57,13 +57,6 @@
 
 def select_rows(picks, field):
     return jnp.dot(pick_matrix(picks, field.shape[0]), field, precision=lax.Precision.HIGHEST)
-
-
-def place_rows(picks, values, total_rows):
-    matrix = pick_matrix(picks, total_rows)
-    return lax.dot_general(
-        matrix, values, (((0,), (0,)), ((), ())), precision=lax.Precision.HIGHEST
-    )
 
 
 def neighbour_picks(row_picks):
@@ -74,15 +67,6 @@
     return [
         lax.dynamic_index_in_dim(row_picks, place, 0, keepdims=False) for place in (rank, near, far)
     ]
-
-
-def mix_stream(received, picks, total_rows):
-    return place_rows(jnp.concatenate(picks), received, total_rows) / 3.0
-
-
-def gap_rows(mixed_new, copies_new):
-    gap_value = mixed_new.astype(jnp.float32) - copies_new.astype(jnp.float32)
-    return jnp.sum(gap_value * gap_value, axis=0, keepdims=True)
 
 
 def consensus_of(partial_sums, width):
@@ -260,17 +244,63 @@
     )(spots, starts, picks, *arrays)
 
 
+def scatter_rows(total, picks, values):
+    for low in range(0, picks.shape[0], 8):
+        places = [pl.ds(picks[low + step], 1) for step in range(8)]
+        sums = [
+            total[place, :] + values[low + step : low + step + 1, :]
+            for step, place in enumerate(places)
+        ]
+        for place, row in zip(places, sums):
+            total[place, :] = row
+
+
+def param_kernel(
+    own_picks,
+    far_picks,
+    near_picks,
+    own,
+    far,
+    near,
+    copies,
+    mixed,
+    copies_new,
+    mixed_new,
+    gaps,
+    total,
+):
+    total[...] = jnp.zeros_like(total)
+    scatter_rows(total, own_picks, own[...])
+    fresh = (copies[...].astype(jnp.float32) + total[...]).astype(jnp.bfloat16)
+    copies_new[...] = fresh
+    scatter_rows(total, far_picks, far[...].astype(jnp.float32))
+    scatter_rows(total, near_picks, near[...].astype(jnp.float32))
+    blend = (mixed[...].astype(jnp.float32) + total[...] / 3.0).astype(jnp.bfloat16)
+    mixed_new[...] = blend
+    gap = blend.astype(jnp.float32) - fresh.astype(jnp.float32)
+    gaps[...] = jnp.sum(gap * gap, axis=0, keepdims=True)
+
+
+def param_step(own_picks, far_picks, near_picks, *arrays):
+    scalars = [pl.BlockSpec(memory_space=pltpu.SMEM)] * 3
+    whole = pl.BlockSpec(memory_space=pltpu.VMEM)
+    rows, width = arrays[3].shape
+    narrow = jax.ShapeDtypeStruct((rows, width), jnp.bfloat16)
+    return pl.pallas_call(
+        param_kernel,
+        out_shape=(narrow, narrow, jax.ShapeDtypeStruct((1, width), jnp.float32)),
+        in_specs=scalars + [whole] * len(arrays),
+        out_specs=(whole,) * 3,
+        scratch_shapes=[pltpu.VMEM((rows, width), jnp.float32)],
+        compiler_params=pltpu.CompilerParams(vmem_limit_bytes=8 * 2**20),
+        cost_estimate=pl.CostEstimate(flops=1000, bytes_accessed=1000, transcendentals=0),
+    )(own_picks, far_picks, near_picks, *arrays)
+
+
 def mix_kernel(far_picks, near_picks, far, near, update, mixed, mixed_new, total):
     total[...] = update[...]
-    for picks, values in ((near_picks, near), (far_picks, far)):
-        for low in range(0, picks.shape[0], 8):
-            places = [pl.ds(picks[low + step], 1) for step in range(8)]
-            sums = [
-                total[place, :] + values[low + step : low + step + 1, :]
-                for step, place in enumerate(places)
-            ]
-            for place, row in zip(places, sums):
-                total[place, :] = row
+    scatter_rows(total, far_picks, far[...])
+    scatter_rows(total, near_picks, near[...])
     mixed_new[...] = (mixed[...].astype(jnp.float32) + total[...] / 3.0).astype(jnp.bfloat16)
 
 
@@ -321,30 +351,30 @@
         - step_rate * tracker[0].astype(jnp.float32)
     )
     param_values = select_rows(own_picks[0], weights_new - copy_value)
-    copies_new = (copy_value + place_rows(own_picks[0], param_values, model_width)).astype(
-        jnp.bfloat16
-    )
-    param_sent = param_values.astype(jnp.bfloat16)
-    param_near, param_far = swaps(param_sent)
-    param_received = jnp.concatenate((param_sent, param_far, param_near), axis=0).astype(
-        jnp.float32
-    )
-    mixed_new = (mixed_value + mix_stream(param_received, [own_picks[0], picks[2][0], picks[1][0]], model_width)).astype(
-        jnp.bfloat16
-    )
-    partial_sums = gap_rows(mixed_new, copies_new)
-    own_half, other = lax.optimization_barrier((own_half, other))
+    param_near, param_far = swaps(param_values.astype(jnp.bfloat16))
+    param_picks = (picks[0][0], picks[2][0], picks[1][0])
+    query_weight = (weights_new * model_width ** (-0.5)).astype(jnp.bfloat16)
+    early = (query_weight, image_starts(image_ids[0]), [kept[1] for kept in picks], param_picks)
+    own_half, other, early = lax.optimization_barrier((own_half, other, early))
+    query_weight, starts, later_picks, param_picks = early
+    copies_new, mixed_new, partial_sums = param_step(
+        *param_picks,
+        param_values,
+        param_far,
+        param_near,
+        copies[0],
+        copies_mixed[0],
+    )
     blocks = pass_tokens(other)
     _, partial_sums = lax.optimization_barrier((other, partial_sums))
     partial_sums = spread_rows(partial_sums, ("blk_1", "tp_0"))
     spots = [high * half] + [
         (1 - high) * half + ((place - shift) % len(blocks)) * height for shift in range(len(blocks))
     ]
-    query_weight = (weights_new * model_width ** (-0.5)).astype(jnp.bfloat16)
     grad_new, tracker_new, tracker_copy_new, update, tracker_values = gradient_step(
         jnp.stack(spots).astype(jnp.int32),
-        image_starts(image_ids[0]),
-        own_picks[1],
+        starts,
+        later_picks[0],
         own_half,
         *blocks,
         query_weight,
@@ -356,13 +386,13 @@
         tracker_mixed[0],
         grad_prev[0],
     )
-    tracker_values, partial_sums = lax.optimization_barrier((tracker_values, partial_sums))
     near, far = swaps(tracker_values)
+    _, partial_sums = lax.optimization_barrier((tracker_values, partial_sums))
     partial_sums = spread_rows(
         jnp.sum(partial_sums, axis=0, keepdims=True), ("blk_0", "blk_2", "tp_1")
     )
     tracker_mixed_new = mix_step(
-        picks[2][1], picks[1][1], far, near, update, tracker_mixed[0]
+        later_picks[2], later_picks[1], far, near, update, tracker_mixed[0]
     )
     tracker_mixed_new, partial_sums = lax.optimization_barrier((tracker_mixed_new, partial_sums))
     consensus = consensus_of(partial_sums, model_width)

time: 102 us -> 110 us (1.078)
  waiting for transfers between devices: 7.97 us -> 17.2 us
  matrix products: 2.45 us -> 0.49 us
  Pallas kernels: 10.5 us -> 12.2 us
    all_to_all x1, waiting for transfers between devices: 1.63 us -> 12.1 us  [spread_tokens(): lax.all_to_all(blocks, 'tp_1', 0, 0, tiled=True).reshape(-1, value.shape[1])]
    ppermute x2, starting transfers between devices: 9.46 us -> 13.5 us  [swaps(): from_far = lax.ppermute(value, BLK, far)]
    all_to_all x2, starting transfers between devices: 18.9 us -> 15 us  [spread_rows(): return lax.all_to_all(rows, axes, 0, 0, tiled=True)]
    all_to_all x2, waiting for transfers between devices: 6.32 us -> 4.05 us  [spread_rows(): return lax.all_to_all(rows, axes, 0, 0, tiled=True)]
    dot_general x2 -> x0, matrix products: 1.96 us -> none  [place_rows(): lax.dot_general(matrix, values, (((0,), (0,)), ((), ())), precision=lax.P...]
    pallas_call x0 -> x1, Pallas kernels: none -> 1.74 us  [param_step(): pl.pallas_call(param_kernel, out_shape=(narrow, narrow, jax.ShapeDtypeStr...]
  transfers between devices with their start and end apart: 11 -> 11, of which waited for: 3 -> 3; matrix products, arithmetic and copies ran while one was open for 8% -> 5% of each run, Pallas kernels for 10% -> 11%
where the time goes in v7:
time: 110 us
  starting transfers between devices  70.1 us (64%)
  waiting for transfers between devices  17.2 us (16%)
  Pallas kernels  12.2 us (11%)
  local copies, waits for them, and re-layouts  5.1 us (5%)
  between operations  2.77 us (3%)
  other arithmetic  1.85 us (2%)
    ppermute x1, starting transfers between devices, per_device(): other = lax.ppermute(tokens[0], 'tp_0', [(0, 1), (1, 0)])  16.3 us
    all_to_all x2, starting transfers between devices, spread_rows(): return lax.all_to_all(rows, axes, 0, 0, tiled=True)  15 us
    ppermute x2, starting transfers between devices, swaps(): from_far = lax.ppermute(value, BLK, far)  13.5 us
    ppermute x2, starting transfers between devices, swaps(): return (lax.ppermute(value, BLK, near), from_far)  12.4 us
    all_to_all x1, waiting for transfers between devices, spread_tokens(): lax.all_to_all(blocks, 'tp_1', 0, 0, tiled=True).reshape(-1, value.shape[1])  12.1 us
    pallas_call x1, Pallas kernels, gradient_step(): pl.pallas_call(gradient_kernel, out_shape=(narrow, narrow, narrow, jax.Sh...  8.94 us
    ppermute x3, starting transfers between devices, pass_tokens(): blocks.append(lax.ppermute(value, 'tp_1', pairs))  8.55 us
    all_to_all x1, starting transfers between devices, spread_tokens(): lax.all_to_all(blocks, 'tp_1', 0, 0, tiled=True).reshape(-1, value.shape[1])  4.38 us
  transfers between devices with their start and end apart: 11, of which 3 were waited for; matrix products, arithmetic and copies ran while one was open for 5% of the time, Pallas kernels for 11%

profile of v7, /device:TPU:1, one launch (start us, length us, event | category | flops | bytes accessed | tf_op | source)
XLA Modules:
  0.0 109.7 jit_solution(11053397773528212117)
XLA Ops:
  0.6 16.3 %collective-permute-start = (bf16[128,1024]{1,0:T(8,128)(2,1)}, bf16[128,1024]{1,0:T(8,128)(2,1)S(1)}, u32[]{:S(2)}, u32[]{:S(2)}) collective-permute-start(bf16[128,1024]{1,0:T(8,128)(2,1)} %bitcast.72), channel_id=1, source_target_pairs={{0,4},{4,0},{1,5},{5,1},{2,6},{6,2},{3,7},{7,3},{8,12},{12,8},{9,1... | collective-permute-start | bytes 786440 | tf_op jit(solution)/shard_map/ppermute | solution.py:342
  16.9 2.1 %broadcast_in_dim.33 = bf16[4,128,1024]{2,1,0:T(8,128)(2,1)} broadcast(bf16[128,1024]{1,0:T(8,128)(2,1)} %bitcast.73), dimensions={1,2} | broadcast | bytes 1310720 | tf_op jit(solution)/shard_map/broadcast_in_dim | solution.py:40
  19.0 4.4 %all-to-all-start = ((bf16[4,128,1024]{2,1,0:T(8,128)(2,1)}), bf16[4,128,1024]{2,1,0:T(8,128)(2,1)}, u32[]{:S(2)}, u32[]{:S(2)}) async-start(bf16[4,128,1024]{2,1,0:T(8,128)(2,1)} %broadcast_in_dim.33), calls=%async_computation | async-start | bytes 2097152 | tf_op jit(solution)/shard_map/all_to_all | solution.py:41
  23.4 0.0 copy-start.9
  23.4 0.7 copy-done.9
  24.1 0.1 convert_reduce_fusion.starts
  24.2 0.7 constant_dynamic-slice_fusion
  25.0 0.0 copy-done
  25.0 0.0 copy-done.1
  25.0 0.0 copy-done.6
  25.0 0.0 copy-done.7
  25.0 0.2 multiply_convert_fusion.query_weight
  25.2 0.0 collective-permute-done.other_0
  25.2 12.1 %all-to-all-done = bf16[4,128,1024]{2,1,0:T(8,128)(2,1)} async-done(((bf16[4,128,1024]{2,1,0:T(8,128)(2,1)}), bf16[4,128,1024]{2,1,0:T(8,128)(2,1)}, u32[]{:S(2)}, u32[]{:S(2)}) %all-to-all-start) | async-done | bytes 1048608 | tf_op jit(solution)/shard_map/all_to_all | solution.py:41
  37.3 2.3 %collective-permute-start.3 = (bf16[128,1024]{1,0:T(8,128)(2,1)S(1)}, bf16[128,1024]{1,0:T(8,128)(2,1)S(1)}, u32[]{:S(2)}, u32[]{:S(2)}) collective-permute-start(bf16[128,1024]{1,0:T(8,128)(2,1)S(1)} %collective-permute-done.other_0), channel_id=1, source_target_pairs={{0,1},{1,2},{2,3},{3,0},{4,5},{5,6},{6,7},{7,4},{8,9},{9,10},{10,1... | collective-permute-start | bytes 786440 | tf_op jit(solution)/shard_map/ppermute | solution.py:49
  39.7 3.5 %collective-permute-start.4 = (bf16[128,1024]{1,0:T(8,128)(2,1)S(1)}, bf16[128,1024]{1,0:T(8,128)(2,1)S(1)}, u32[]{:S(2)}, u32[]{:S(2)}) collective-permute-start(bf16[128,1024]{1,0:T(8,128)(2,1)S(1)} %collective-permute-done.other_0), channel_id=1, source_target_pairs={{0,2},{1,3},{2,0},{3,1},{4,6},{5,7},{6,4},{7,5},{8,10},{9,11},{10,... | collective-permute-start | bytes 786440 | tf_op jit(solution)/shard_map/ppermute | solution.py:49
  43.2 2.7 %collective-permute-start.5 = (bf16[128,1024]{1,0:T(8,128)(2,1)S(1)}, bf16[128,1024]{1,0:T(8,128)(2,1)S(1)}, u32[]{:S(2)}, u32[]{:S(2)}) collective-permute-start(bf16[128,1024]{1,0:T(8,128)(2,1)S(1)} %collective-permute-done.other_0), channel_id=1, source_target_pairs={{0,3},{1,0},{2,1},{3,2},{4,7},{5,4},{6,5},{7,6},{8,11},{9,8},{10,9... | collective-permute-start | bytes 786440 | tf_op jit(solution)/shard_map/ppermute | solution.py:49
  45.9 0.5 fusion.11
  46.4 9.6 %collective-permute-start.1 = (bf16[64,128]{1,0:T(8,128)(2,1)S(1)}, bf16[64,128]{1,0:T(8,128)(2,1)S(1)}, u32[]{:S(2)}, u32[]{:S(2)}) collective-permute-start(bf16[64,128]{1,0:T(8,128)(2,1)S(1)} %get-tuple-element.61), channel_id=1, source_target_pairs={{0,504},{8,16},{16,8},{24,32},{32,24},{40,48},{48,40},{56,64},{64,... | collective-permute-start | bytes 49160 | tf_op jit(solution)/shard_map/ppermute | solution.py:24
  56.1 1.9 %collective-permute-start.2 = (bf16[64,128]{1,0:T(8,128)(2,1)S(1)}, bf16[64,128]{1,0:T(8,128)(2,1)S(1)}, u32[]{:S(2)}, u32[]{:S(2)}) collective-permute-start(bf16[64,128]{1,0:T(8,128)(2,1)S(1)} %get-tuple-element.61), channel_id=1, source_target_pairs={{0,8},{8,0},{16,24},{24,16},{32,40},{40,32},{48,56},{56,48},{64,72... | collective-permute-start | bytes 49160 | tf_op jit(solution)/shard_map/ppermute | solution.py:25
  58.0 0.1 stack.23.spots
  58.1 0.0 collective-permute-done.1.far
  58.1 1.0 collective-permute-done.2.near
  59.1 1.7 %shard_map.188 = (bf16[1024,128]{1,0:T(8,128)(2,1)}, bf16[1024,128]{1,0:T(8,128)(2,1)}, f32[1,128]{1,0:T(1,128)S(1)}) custom-call(s32[64]{0:T(128)S(1)} %get-tuple-element.30.own_picks, s32[64]{0:T(128)S(1)} %get-tuple-element.31.far_picks, s32[64]{0:T(128)S(1)} %get-tuple-element.32.near_picks, f32[64,128]{1,0:T(8,128)S(1)} %get-tuple-element.62.own, ...), custom_call_target="tpu_custom_call" | custom-call | flops 1000 | bytes 1000 | tf_op jit(solution)/shard_map/pallas_call | solution.py:289
  60.9 0.6 broadcast_in_dim.38
  61.5 11.3 %all-to-all-start.1 = ((f32[16,1,128]{2,1,0:T(1,128)}), f32[16,1,128]{2,1,0:T(1,128)S(1)}, u32[]{:S(2)}, u32[]{:S(2)}) async-start(f32[16,1,128]{2,1,0:T(1,128)} %broadcast_in_dim.38), calls=%async_computation.1 | async-start | bytes 16384 | tf_op jit(solution)/shard_map/all_to_all | solution.py:31
  72.8 0.0 collective-permute-done.3.other_1
  72.8 0.0 collective-permute-done.4.other_2
  72.8 0.0 collective-permute-done.5.other_3
  72.8 0.0 copy-done.4
  72.8 0.0 copy-done.5
  72.9 0.0 copy-start.8
  72.9 8.9 %shard_map.189 = (bf16[1024,128]{1,0:T(8,128)(2,1)}, bf16[1024,128]{1,0:T(8,128)(2,1)}, bf16[1024,128]{1,0:T(8,128)(2,1)}, f32[1024,128]{1,0:T(8,128)}, f32[64,128]{1,0:T(8,128)S(1)}) custom-call(s32[5]{0:T(128)S(1)} %stack.23.spots, s32[8]{0:T(128)S(1)} %convert_reduce_fusion.starts, s32[64]{0:T(128)S(1)} %get-tuple-element.36.picks, ...), custom_call_target="tpu_custom_call" | custom-call | flops 2000000000 | bytes 8000000 | tf_op jit(solution)/shard_map/pallas_call | solution.py:220
  81.8 3.9 %collective-permute-start.6 = (f32[64,128]{1,0:T(8,128)S(1)}, f32[64,128]{1,0:T(8,128)S(1)}, u32[]{:S(2)}, u32[]{:S(2)}) collective-permute-start(f32[64,128]{1,0:T(8,128)S(1)} %get-tuple-element.44), channel_id=1, source_target_pairs={{0,504},{8,16},{16,8},{24,32},{32,24},{40,48},{48,40},{56,64},{64,... | collective-permute-start | bytes 98312 | tf_op jit(solution)/shard_map/ppermute | solution.py:24
  85.7 10.5 %collective-permute-start.7 = (f32[64,128]{1,0:T(8,128)S(1)}, f32[64,128]{1,0:T(8,128)S(1)}, u32[]{:S(2)}, u32[]{:S(2)}) collective-permute-start(f32[64,128]{1,0:T(8,128)S(1)} %get-tuple-element.44), channel_id=1, source_target_pairs={{0,8},{8,0},{16,24},{24,16},{32,40},{40,32},{48,56},{56,48},{64,72... | collective-permute-start | bytes 98312 | tf_op jit(solution)/shard_map/ppermute | solution.py:25
  96.2 0.0 all-to-all-done.1
  96.3 0.6 broadcast_in_dim.39
  96.9 3.6 %all-to-all-start.2 = ((f32[32,1,128]{2,1,0:T(1,128)}), f32[32,1,128]{2,1,0:T(1,128)S(1)}, u32[]{:S(2)}, u32[]{:S(2)}) async-start(f32[32,1,128]{2,1,0:T(1,128)} %broadcast_in_dim.39), calls=%async_computation.2 | async-start | bytes 32768 | tf_op jit(solution)/shard_map/all_to_all | solution.py:31
  100.5 0.0 copy-done.8
  100.5 0.0 copy-start.3
  100.5 0.9 multiply_subtract_fusion
  101.5 0.0 collective-permute-done.6.far
  101.5 0.0 collective-permute-done.7.near
  101.5 0.1 copy-done.2
  101.6 0.2 copy-done.3
  101.8 1.5 %shard_map.190 = bf16[1024,128]{1,0:T(8,128)(2,1)} custom-call(s32[64]{0:T(128)S(1)} %get-tuple-element.42.far_picks, s32[64]{0:T(128)S(1)} %get-tuple-element.43.near_picks, f32[64,128]{1,0:T(8,128)S(1)} %collective-permute-done.6.far, f32[64,128]{1,0:T(8,128)S(1)} %collective-permute-done.7.near, f32[1024,128]{1,0:T(8,128)S(1)} %copy-done.2, ...), custom_call_target="tpu_custom_call" | custom-call | flops 1000000 | bytes 1000000 | tf_op jit(solution)/shard_map/pallas_call | solution.py:311
  103.3 4.0 %all-to-all-done.2 = f32[32,1,128]{2,1,0:T(1,128)S(1)} async-done(((f32[32,1,128]{2,1,0:T(1,128)}), f32[32,1,128]{2,1,0:T(1,128)S(1)}, u32[]{:S(2)}, u32[]{:S(2)}) %all-to-all-start.2) | async-done | bytes 16416 | tf_op jit(solution)/shard_map/all_to_all | solution.py:31
  107.4 0.6 reduce_sum.29
  (10 shorter events, 0.0 us)
Async XLA Ops:
  0.6 24.6 %collective-permute-start = (bf16[128,1024]{1,0:T(8,128)(2,1)}, bf16[128,1024]{1,0:T(8,128)(2,1)S(1)}, u32[]{:S(2)}, u32[]{:S(2)}) collective-permute-start(bf16[128,1024]{1,0:T(8,128)(2,1)} %bitcast.72), channel_id=1, source_target_pairs={{0,4},{4,0},{1,5},{5,1},{2,6},{6,2},{3,7},{7,3},{8,12},{12,8},{9,1... | collective-permute-start | bytes 786440 | tf_op jit(solution)/shard_map/ppermute | solution.py:342
  19.0 6.0 %copy-start = (bf16[1,1024,128]{2,1,0:T(8,128)(2,1)S(1)}, bf16[1,1024,128]{2,1,0:T(8,128)(2,1)}, u32[]{:S(2)}) copy-start(bf16[1,1024,128]{2,1,0:T(8,128)(2,1)} %param.14) | copy-start | bytes 786436
  19.0 6.0 %copy-start.1 = (bf16[1,1024,128]{2,1,0:T(8,128)(2,1)S(1)}, bf16[1,1024,128]{2,1,0:T(8,128)(2,1)}, u32[]{:S(2)}) copy-start(bf16[1,1024,128]{2,1,0:T(8,128)(2,1)} %param.15) | copy-start | bytes 786436
  19.0 6.0 %copy-start.6 = (f32[1,1024,128]{2,1,0:T(8,128)S(1)}, f32[1,1024,128]{2,1,0:T(8,128)}, u32[]{:S(2)}) copy-start(f32[1,1024,128]{2,1,0:T(8,128)} %param.13) | copy-start | bytes 1572868
  19.0 6.0 %copy-start.7 = (bf16[1,1024,128]{2,1,0:T(8,128)(2,1)S(1)}, bf16[1,1024,128]{2,1,0:T(8,128)(2,1)}, u32[]{:S(2)}) copy-start(bf16[1,1024,128]{2,1,0:T(8,128)(2,1)} %param.16) | copy-start | bytes 786436
  19.0 18.4 %all-to-all-start = ((bf16[4,128,1024]{2,1,0:T(8,128)(2,1)}), bf16[4,128,1024]{2,1,0:T(8,128)(2,1)}, u32[]{:S(2)}, u32[]{:S(2)}) async-start(bf16[4,128,1024]{2,1,0:T(8,128)(2,1)} %broadcast_in_dim.33), calls=%async_computation | async-start | bytes 2097152 | tf_op jit(solution)/shard_map/all_to_all | solution.py:41
  23.4 0.7 copy-start.9
  37.3 35.5 %collective-permute-start.3 = (bf16[128,1024]{1,0:T(8,128)(2,1)S(1)}, bf16[128,1024]{1,0:T(8,128)(2,1)S(1)}, u32[]{:S(2)}, u32[]{:S(2)}) collective-permute-start(bf16[128,1024]{1,0:T(8,128)(2,1)S(1)} %collective-permute-done.other_0), channel_id=1, source_target_pairs={{0,1},{1,2},{2,3},{3,0},{4,5},{5,6},{6,7},{7,4},{8,9},{9,10},{10,1... | collective-permute-start | bytes 786440 | tf_op jit(solution)/shard_map/ppermute | solution.py:49
  39.7 33.1 %collective-permute-start.4 = (bf16[128,1024]{1,0:T(8,128)(2,1)S(1)}, bf16[128,1024]{1,0:T(8,128)(2,1)S(1)}, u32[]{:S(2)}, u32[]{:S(2)}) collective-permute-start(bf16[128,1024]{1,0:T(8,128)(2,1)S(1)} %collective-permute-done.other_0), channel_id=1, source_target_pairs={{0,2},{1,3},{2,0},{3,1},{4,6},{5,7},{6,4},{7,5},{8,10},{9,11},{10,... | collective-permute-start | bytes 786440 | tf_op jit(solution)/shard_map/ppermute | solution.py:49
  43.2 29.6 %collective-permute-start.5 = (bf16[128,1024]{1,0:T(8,128)(2,1)S(1)}, bf16[128,1024]{1,0:T(8,128)(2,1)S(1)}, u32[]{:S(2)}, u32[]{:S(2)}) collective-permute-start(bf16[128,1024]{1,0:T(8,128)(2,1)S(1)} %collective-permute-done.other_0), channel_id=1, source_target_pairs={{0,3},{1,0},{2,1},{3,2},{4,7},{5,4},{6,5},{7,6},{8,11},{9,8},{10,9... | collective-permute-start | bytes 786440 | tf_op jit(solution)/shard_map/ppermute | solution.py:49
  46.4 11.7 %collective-permute-start.1 = (bf16[64,128]{1,0:T(8,128)(2,1)S(1)}, bf16[64,128]{1,0:T(8,128)(2,1)S(1)}, u32[]{:S(2)}, u32[]{:S(2)}) collective-permute-start(bf16[64,128]{1,0:T(8,128)(2,1)S(1)} %get-tuple-element.61), channel_id=1, source_target_pairs={{0,504},{8,16},{16,8},{24,32},{32,24},{40,48},{48,40},{56,64},{64,... | collective-permute-start | bytes 49160 | tf_op jit(solution)/shard_map/ppermute | solution.py:24
  56.1 3.1 %collective-permute-start.2 = (bf16[64,128]{1,0:T(8,128)(2,1)S(1)}, bf16[64,128]{1,0:T(8,128)(2,1)S(1)}, u32[]{:S(2)}, u32[]{:S(2)}) collective-permute-start(bf16[64,128]{1,0:T(8,128)(2,1)S(1)} %get-tuple-element.61), channel_id=1, source_target_pairs={{0,8},{8,0},{16,24},{24,16},{32,40},{40,32},{48,56},{56,48},{64,72... | collective-permute-start | bytes 49160 | tf_op jit(solution)/shard_map/ppermute | solution.py:25
  59.1 13.7 %copy-start.4 = (bf16[1024,128]{1,0:T(8,128)(2,1)S(1)}, bf16[1024,128]{1,0:T(8,128)(2,1)}, u32[]{:S(2)}) copy-start(bf16[1024,128]{1,0:T(8,128)(2,1)} %key_weight.1) | copy-start | bytes 786436
  59.1 13.7 %copy-start.5 = (bf16[1024,128]{1,0:T(8,128)(2,1)S(1)}, bf16[1024,128]{1,0:T(8,128)(2,1)}, u32[]{:S(2)}) copy-start(bf16[1024,128]{1,0:T(8,128)(2,1)} %value_weight.1) | copy-start | bytes 786436
  61.5 34.8 %all-to-all-start.1 = ((f32[16,1,128]{2,1,0:T(1,128)}), f32[16,1,128]{2,1,0:T(1,128)S(1)}, u32[]{:S(2)}, u32[]{:S(2)}) async-start(f32[16,1,128]{2,1,0:T(1,128)} %broadcast_in_dim.38), calls=%async_computation.1 | async-start | bytes 16384 | tf_op jit(solution)/shard_map/all_to_all | solution.py:31
  72.9 27.7 %copy-start.8 = (bf16[1,1024,128]{2,1,0:T(8,128)(2,1)S(1)}, bf16[1,1024,128]{2,1,0:T(8,128)(2,1)}, u32[]{:S(2)}) copy-start(bf16[1,1024,128]{2,1,0:T(8,128)(2,1)} %param.16) | copy-start | bytes 786436
  81.8 19.7 %collective-permute-start.6 = (f32[64,128]{1,0:T(8,128)S(1)}, f32[64,128]{1,0:T(8,128)S(1)}, u32[]{:S(2)}, u32[]{:S(2)}) collective-permute-start(f32[64,128]{1,0:T(8,128)S(1)} %get-tuple-element.44), channel_id=1, source_target_pairs={{0,504},{8,16},{16,8},{24,32},{32,24},{40,48},{48,40},{56,64},{64,... | collective-permute-start | bytes 98312 | tf_op jit(solution)/shard_map/ppermute | solution.py:24
  85.7 15.8 %collective-permute-start.7 = (f32[64,128]{1,0:T(8,128)S(1)}, f32[64,128]{1,0:T(8,128)S(1)}, u32[]{:S(2)}, u32[]{:S(2)}) collective-permute-start(f32[64,128]{1,0:T(8,128)S(1)} %get-tuple-element.44), channel_id=1, source_target_pairs={{0,8},{8,0},{16,24},{24,16},{32,40},{40,32},{48,56},{56,48},{64,72... | collective-permute-start | bytes 98312 | tf_op jit(solution)/shard_map/ppermute | solution.py:25
  96.9 10.5 %all-to-all-start.2 = ((f32[32,1,128]{2,1,0:T(1,128)}), f32[32,1,128]{2,1,0:T(1,128)S(1)}, u32[]{:S(2)}, u32[]{:S(2)}) async-start(f32[32,1,128]{2,1,0:T(1,128)} %broadcast_in_dim.39), calls=%async_computation.2 | async-start | bytes 32768 | tf_op jit(solution)/shard_map/all_to_all | solution.py:31
  100.5 1.0 copy-start.2
  100.5 1.2 %copy-start.3 = (bf16[1,1024,128]{2,1,0:T(8,128)(2,1)S(1)}, bf16[1,1024,128]{2,1,0:T(8,128)(2,1)}, u32[]{:S(2)}) copy-start(bf16[1,1024,128]{2,1,0:T(8,128)(2,1)} %param.18) | copy-start | bytes 786436

commit v8 on v7

--- a/solution.py
+++ b/solution.py
@@ -76,6 +76,52 @@
 def image_starts(ids):
     marks = lax.broadcasted_iota(jnp.int32, (8, ids.shape[0]), 0)
     return jnp.sum((ids[None, :] < marks).astype(jnp.int32), axis=1)
+
+
+def fresh_tracker(tracker, copy_value, mixed, gradient, grad_prev):
+    return (
+        tracker.astype(jnp.float32)
+        + mixing_rate * (mixed.astype(jnp.float32) - copy_value)
+        + gradient.astype(jnp.float32)
+        - grad_prev.astype(jnp.float32)
+    ).astype(jnp.bfloat16)
+
+
+def tracker_kernel(
+    picks,
+    kept,
+    gradient,
+    tracker,
+    tracker_copy,
+    tracker_mixed,
+    grad_prev,
+    tracker_new,
+    tracker_copy_new,
+    update,
+):
+    copy_value = tracker_copy[...].astype(jnp.float32)
+    tracker_new[...] = fresh_tracker(
+        tracker[...], copy_value, tracker_mixed[...], gradient[...], grad_prev[...]
+    )
+    update[...] = jnp.zeros_like(update)
+    scatter_rows(update, picks, kept[...])
+    tracker_copy_new[...] = (copy_value + update[...]).astype(jnp.bfloat16)
+
+
+def tracker_step(picks, *arrays):
+    whole = pl.BlockSpec(memory_space=pltpu.VMEM)
+    rows, width = arrays[1].shape
+    narrow = jax.ShapeDtypeStruct((rows, width), jnp.bfloat16)
+    return pl.pallas_call(
+        tracker_kernel,
+        out_shape=(narrow, narrow, jax.ShapeDtypeStruct((rows, width), jnp.float32)),
+        in_specs=[pl.BlockSpec(memory_space=pltpu.SMEM)] + [whole] * len(arrays),
+        out_specs=(whole,) * 3,
+        compiler_params=pltpu.CompilerParams(vmem_limit_bytes=8 * 2**20),
+        cost_estimate=pl.CostEstimate(
+            flops=10**6, bytes_accessed=3 * 10**6, transcendentals=0
+        ),
+    )(picks, *arrays)
 
 
 def gradient_kernel(
@@ -96,9 +142,6 @@
     tracker_mixed_in,
     grad_prev_in,
     grad_new,
-    tracker_new,
-    tracker_copy_new,
-    update,
     kept,
     joined,
     tokens,
@@ -194,21 +237,10 @@
     for copy in late:
         copy.wait()
     copy_value = tracker_copy[...].astype(jnp.float32)
-    fresh = (
-        tracker[...].astype(jnp.float32)
-        + mixing_rate * (tracker_mixed[...].astype(jnp.float32) - copy_value)
-        + gradient.astype(jnp.float32)
-        - grad_prev[...].astype(jnp.float32)
-    ).astype(jnp.bfloat16)
-    tracker_new[...] = fresh
+    fresh = fresh_tracker(tracker[...], copy_value, tracker_mixed[...], gradient, grad_prev[...])
     change[...] = fresh.astype(jnp.float32) - copy_value
-    update[...] = jnp.zeros_like(update)
     for index in range(picks.shape[0]):
-        place = picks[index]
-        row = change[pl.ds(place, 1), :]
-        kept[pl.ds(index, 1), :] = row
-        update[pl.ds(place, 1), :] = row
-    tracker_copy_new[...] = (copy_value + update[...]).astype(jnp.bfloat16)
+        kept[pl.ds(index, 1), :] = change[pl.ds(picks[index], 1), :]
 
 
 def gradient_step(spots, starts, picks, *arrays):
@@ -219,15 +251,9 @@
     narrow = jax.ShapeDtypeStruct((rows, width), jnp.bfloat16)
     return pl.pallas_call(
         gradient_kernel,
-        out_shape=(
-            narrow,
-            narrow,
-            narrow,
-            jax.ShapeDtypeStruct((rows, width), jnp.float32),
-            jax.ShapeDtypeStruct((picks.shape[0], width), jnp.float32),
-        ),
+        out_shape=(narrow, jax.ShapeDtypeStruct((picks.shape[0], width), jnp.float32)),
         in_specs=scalars + [pl.BlockSpec(memory_space=pl.ANY)] * len(arrays),
-        out_specs=(whole,) * 5,
+        out_specs=(whole,) * 2,
         scratch_shapes=[
             pltpu.VMEM((depth, 3 * width), jnp.bfloat16),
             pltpu.VMEM((rows, depth), jnp.bfloat16),
@@ -353,10 +379,9 @@
     param_values = select_rows(own_picks[0], weights_new - copy_value)
     param_near, param_far = swaps(param_values.astype(jnp.bfloat16))
     param_picks = (picks[0][0], picks[2][0], picks[1][0])
-    query_weight = (weights_new * model_width ** (-0.5)).astype(jnp.bfloat16)
-    early = (query_weight, image_starts(image_ids[0]), [kept[1] for kept in picks], param_picks)
-    own_half, other, early = lax.optimization_barrier((own_half, other, early))
-    query_weight, starts, later_picks, param_picks = early
+    own_half, other, starts, later_picks = lax.optimization_barrier(
+        (own_half, other, image_starts(image_ids[0]), [kept[1] for kept in picks])
+    )
     copies_new, mixed_new, partial_sums = param_step(
         *param_picks,
         param_values,
@@ -371,7 +396,8 @@
     spots = [high * half] + [
         (1 - high) * half + ((place - shift) % len(blocks)) * height for shift in range(len(blocks))
     ]
-    grad_new, tracker_new, tracker_copy_new, update, tracker_values = gradient_step(
+    query_weight = (weights_new * model_width ** (-0.5)).astype(jnp.bfloat16)
+    grad_new, tracker_values = gradient_step(
         jnp.stack(spots).astype(jnp.int32),
         starts,
         later_picks[0],
@@ -387,6 +413,15 @@
         grad_prev[0],
     )
     near, far = swaps(tracker_values)
+    tracker_new, tracker_copy_new, update = tracker_step(
+        later_picks[0],
+        tracker_values,
+        grad_new,
+        tracker[0],
+        tracker_copy[0],
+        tracker_mixed[0],
+        grad_prev[0],
+    )
     _, partial_sums = lax.optimization_barrier((tracker_values, partial_sums))
     partial_sums = spread_rows(
         jnp.sum(partial_sums, axis=0, keepdims=True), ("blk_0", "blk_2", "tp_1")

time: 110 us -> 101 us (0.918)
  waiting for transfers between devices: 17.2 us -> 4.83 us
  starting transfers between devices: 70.1 us -> 72.9 us
  Pallas kernels: 12.2 us -> 13.3 us
    all_to_all x1, waiting for transfers between devices: 12.1 us -> 2.65 us  [spread_tokens(): lax.all_to_all(blocks, 'tp_1', 0, 0, tiled=True).reshape(-1, value.shape[1])]
    all_to_all x2, starting transfers between devices: 15 us -> 19.4 us  [spread_rows(): return lax.all_to_all(rows, axes, 0, 0, tiled=True)]
    ppermute x2, starting transfers between devices: 13.5 us -> 9.62 us  [swaps(): from_far = lax.ppermute(value, BLK, far)]
    ppermute x2, starting transfers between devices: 12.4 us -> 14.6 us  [swaps(): return (lax.ppermute(value, BLK, near), from_far)]
    all_to_all x2, waiting for transfers between devices: 4.05 us -> 2.16 us  [spread_rows(): return lax.all_to_all(rows, axes, 0, 0, tiled=True)]
    pallas_call x1 -> x2, Pallas kernels: 8.94 us -> 10 us  [the longest x1 8.28 us: gradient_step(): pl.pallas_call(gradient_kernel, out_shape=(narrow, jax.ShapeDtypeStruct((...]
  transfers between devices with their start and end apart: 11 -> 11, of which waited for: 3 -> 2; matrix products, arithmetic and copies ran while one was open for 5% -> 6% of each run, Pallas kernels for 11% -> 13%
where the time goes in v8:
time: 101 us
  starting transfers between devices  72.9 us (72%)
  Pallas kernels  13.3 us (13%)
  waiting for transfers between devices  4.83 us (5%)
  local copies, waits for them, and re-layouts  4.54 us (4%)
  between operations  2.79 us (3%)
  other arithmetic  1.85 us (2%)
    all_to_all x2, starting transfers between devices, spread_rows(): return lax.all_to_all(rows, axes, 0, 0, tiled=True)  19.4 us
    ppermute x1, starting transfers between devices, per_device(): other = lax.ppermute(tokens[0], 'tp_0', [(0, 1), (1, 0)])  16.3 us
    ppermute x2, starting transfers between devices, swaps(): return (lax.ppermute(value, BLK, near), from_far)  14.6 us
    ppermute x2, starting transfers between devices, swaps(): from_far = lax.ppermute(value, BLK, far)  9.62 us
    ppermute x3, starting transfers between devices, pass_tokens(): blocks.append(lax.ppermute(value, 'tp_1', pairs))  8.56 us
    pallas_call x1, Pallas kernels, gradient_step(): pl.pallas_call(gradient_kernel, out_shape=(narrow, jax.ShapeDtypeStruct((...  8.28 us
    all_to_all x1, starting transfers between devices, spread_tokens(): lax.all_to_all(blocks, 'tp_1', 0, 0, tiled=True).reshape(-1, value.shape[1])  4.4 us
    all_to_all x1, waiting for transfers between devices, spread_tokens(): lax.all_to_all(blocks, 'tp_1', 0, 0, tiled=True).reshape(-1, value.shape[1])  2.65 us
  transfers between devices with their start and end apart: 11, of which 2 were waited for; matrix products, arithmetic and copies ran while one was open for 6% of the time, Pallas kernels for 13%

profile of v8, /device:TPU:1, one launch (start us, length us, event | category | flops | bytes accessed | tf_op | source)
XLA Modules:
  0.0 100.7 jit_solution(13570141601852873101)
XLA Ops:
  0.6 16.3 %collective-permute-start.2 = (bf16[128,1024]{1,0:T(8,128)(2,1)}, bf16[128,1024]{1,0:T(8,128)(2,1)S(1)}, u32[]{:S(2)}, u32[]{:S(2)}) collective-permute-start(bf16[128,1024]{1,0:T(8,128)(2,1)} %bitcast.79), channel_id=1, source_target_pairs={{0,4},{4,0},{1,5},{5,1},{2,6},{6,2},{3,7},{7,3},{8,12},{12,8},{9,1... | collective-permute-start | bytes 786440 | tf_op jit(solution)/shard_map/ppermute | solution.py:368
  16.9 2.1 %broadcast_in_dim.35 = bf16[4,128,1024]{2,1,0:T(8,128)(2,1)} broadcast(bf16[128,1024]{1,0:T(8,128)(2,1)} %bitcast.80), dimensions={1,2} | broadcast | bytes 1310720 | tf_op jit(solution)/shard_map/broadcast_in_dim | solution.py:40
  19.0 4.4 %all-to-all-start = ((bf16[4,128,1024]{2,1,0:T(8,128)(2,1)}), bf16[4,128,1024]{2,1,0:T(8,128)(2,1)}, u32[]{:S(2)}, u32[]{:S(2)}) async-start(bf16[4,128,1024]{2,1,0:T(8,128)(2,1)} %broadcast_in_dim.35), calls=%async_computation | async-start | bytes 2097152 | tf_op jit(solution)/shard_map/all_to_all | solution.py:41
  23.4 0.7 constant_dynamic-slice_fusion
  24.2 0.0 copy-done.2
  24.2 0.0 copy-done.3
  24.2 0.0 copy-start.11
  24.2 0.5 fusion.11
  24.7 3.6 %collective-permute-start = (bf16[64,128]{1,0:T(8,128)(2,1)S(1)}, bf16[64,128]{1,0:T(8,128)(2,1)S(1)}, u32[]{:S(2)}, u32[]{:S(2)}) collective-permute-start(bf16[64,128]{1,0:T(8,128)(2,1)S(1)} %get-tuple-element.53), channel_id=1, source_target_pairs={{0,504},{8,16},{16,8},{24,32},{32,24},{40,48},{48,40},{56,64},{64,... | collective-permute-start | bytes 49160 | tf_op jit(solution)/shard_map/ppermute | solution.py:24
  28.3 6.2 %collective-permute-start.1 = (bf16[64,128]{1,0:T(8,128)(2,1)S(1)}, bf16[64,128]{1,0:T(8,128)(2,1)S(1)}, u32[]{:S(2)}, u32[]{:S(2)}) collective-permute-start(bf16[64,128]{1,0:T(8,128)(2,1)S(1)} %get-tuple-element.53), channel_id=1, source_target_pairs={{0,8},{8,0},{16,24},{24,16},{32,40},{40,32},{48,56},{56,48},{64,72... | collective-permute-start | bytes 49160 | tf_op jit(solution)/shard_map/ppermute | solution.py:25
  34.6 0.1 convert_reduce_fusion.starts
  34.7 0.0 collective-permute-done.2.other_0
  34.7 2.6 %all-to-all-done = bf16[4,128,1024]{2,1,0:T(8,128)(2,1)} async-done(((bf16[4,128,1024]{2,1,0:T(8,128)(2,1)}), bf16[4,128,1024]{2,1,0:T(8,128)(2,1)}, u32[]{:S(2)}, u32[]{:S(2)}) %all-to-all-start) | async-done | bytes 1048608 | tf_op jit(solution)/shard_map/all_to_all | solution.py:41
  37.4 2.3 %collective-permute-start.3 = (bf16[128,1024]{1,0:T(8,128)(2,1)S(1)}, bf16[128,1024]{1,0:T(8,128)(2,1)S(1)}, u32[]{:S(2)}, u32[]{:S(2)}) collective-permute-start(bf16[128,1024]{1,0:T(8,128)(2,1)S(1)} %collective-permute-done.2.other_0), channel_id=1, source_target_pairs={{0,1},{1,2},{2,3},{3,0},{4,5},{5,6},{6,7},{7,4},{8,9},{9,10},{10,1... | collective-permute-start | bytes 786440 | tf_op jit(solution)/shard_map/ppermute | solution.py:49
  39.7 3.5 %collective-permute-start.4 = (bf16[128,1024]{1,0:T(8,128)(2,1)S(1)}, bf16[128,1024]{1,0:T(8,128)(2,1)S(1)}, u32[]{:S(2)}, u32[]{:S(2)}) collective-permute-start(bf16[128,1024]{1,0:T(8,128)(2,1)S(1)} %collective-permute-done.2.other_0), channel_id=1, source_target_pairs={{0,2},{1,3},{2,0},{3,1},{4,6},{5,7},{6,4},{7,5},{8,10},{9,11},{10,... | collective-permute-start | bytes 786440 | tf_op jit(solution)/shard_map/ppermute | solution.py:49
  43.3 2.7 %collective-permute-start.5 = (bf16[128,1024]{1,0:T(8,128)(2,1)S(1)}, bf16[128,1024]{1,0:T(8,128)(2,1)S(1)}, u32[]{:S(2)}, u32[]{:S(2)}) collective-permute-start(bf16[128,1024]{1,0:T(8,128)(2,1)S(1)} %collective-permute-done.2.other_0), channel_id=1, source_target_pairs={{0,3},{1,0},{2,1},{3,2},{4,7},{5,4},{6,5},{7,6},{8,11},{9,8},{10,9... | collective-permute-start | bytes 786440 | tf_op jit(solution)/shard_map/ppermute | solution.py:49
  46.0 0.2 multiply_convert_fusion.query_weight
  46.2 0.1 stack.23.spots
  46.3 0.0 collective-permute-done.far
  46.3 0.0 collective-permute-done.1.near
  46.3 0.0 copy-start.9
  46.3 1.7 %shard_map.188 = (bf16[1024,128]{1,0:T(8,128)(2,1)}, bf16[1024,128]{1,0:T(8,128)(2,1)}, f32[1,128]{1,0:T(1,128)S(1)}) custom-call(s32[64]{0:T(128)S(1)} %get-tuple-element.52.own_picks, s32[64]{0:T(128)S(1)} %get-tuple-element.48.far_picks, s32[64]{0:T(128)S(1)} %get-tuple-element.55.near_picks, f32[64,128]{1,0:T(8,128)S(1)} %get-tuple-element.54.own, ...), custom_call_target="tpu_custom_call" | custom-call | flops 1000 | bytes 1000 | tf_op jit(solution)/shard_map/pallas_call | solution.py:315
  48.1 0.6 broadcast_in_dim.38
  48.7 15.8 %all-to-all-start.1 = ((f32[16,1,128]{2,1,0:T(1,128)}), f32[16,1,128]{2,1,0:T(1,128)S(1)}, u32[]{:S(2)}, u32[]{:S(2)}) async-start(f32[16,1,128]{2,1,0:T(1,128)} %broadcast_in_dim.38), calls=%async_computation.1 | async-start | bytes 16384 | tf_op jit(solution)/shard_map/all_to_all | solution.py:31
  64.5 0.0 collective-permute-done.3.other_1
  64.5 0.0 collective-permute-done.4.other_2
  64.5 0.0 collective-permute-done.5.other_3
  64.5 0.0 copy-start.1
  64.5 8.3 %shard_map.189 = (bf16[1024,128]{1,0:T(8,128)(2,1)}, f32[64,128]{1,0:T(8,128)S(1)}) custom-call(s32[5]{0:T(128)S(1)} %stack.23.spots, s32[8]{0:T(128)S(1)} %convert_reduce_fusion.starts, s32[64]{0:T(128)S(1)} %get-tuple-element.28.picks, bf16[512,1024]{1,0:T(8,128)(2,1)} %bitcast.10.own, bf16[128,1024]{1,0:T(8,128)(2,1)S(1)} %collective-permute-done.2.other_0, ...), custom_call_target="tpu_custom_call" | custom-call | flops 2000000000 | bytes 8000000 | tf_op jit(solution)/shard_map/pallas_call | solution.py:252
  72.8 6.0 %collective-permute-start.6 = (f32[64,128]{1,0:T(8,128)S(1)}, f32[64,128]{1,0:T(8,128)S(1)}, u32[]{:S(2)}, u32[]{:S(2)}) collective-permute-start(f32[64,128]{1,0:T(8,128)S(1)} %get-tuple-element.32.kept), channel_id=1, source_target_pairs={{0,504},{8,16},{16,8},{24,32},{32,24},{40,48},{48,40},{56,64},{64,... | collective-permute-start | bytes 98312 | tf_op jit(solution)/shard_map/ppermute | solution.py:24
  78.8 8.4 %collective-permute-start.7 = (f32[64,128]{1,0:T(8,128)S(1)}, f32[64,128]{1,0:T(8,128)S(1)}, u32[]{:S(2)}, u32[]{:S(2)}) collective-permute-start(f32[64,128]{1,0:T(8,128)S(1)} %get-tuple-element.32.kept), channel_id=1, source_target_pairs={{0,8},{8,0},{16,24},{24,16},{32,40},{40,32},{48,56},{56,48},{64,72... | collective-permute-start | bytes 98312 | tf_op jit(solution)/shard_map/ppermute | solution.py:25
  87.2 0.0 all-to-all-done.1
  87.3 0.6 broadcast_in_dim.39
  87.9 3.6 %all-to-all-start.2 = ((f32[32,1,128]{2,1,0:T(1,128)}), f32[32,1,128]{2,1,0:T(1,128)S(1)}, u32[]{:S(2)}, u32[]{:S(2)}) async-start(f32[32,1,128]{2,1,0:T(1,128)} %broadcast_in_dim.39), calls=%async_computation.2 | async-start | bytes 32768 | tf_op jit(solution)/shard_map/all_to_all | solution.py:31
  91.5 0.0 copy-start.4
  91.5 0.0 copy-start.5
  91.5 0.0 copy-start.6
  91.5 0.0 copy-start.7
  91.6 0.9 multiply_subtract_fusion
  92.5 0.0 copy-done.5
  92.5 0.2 copy-done.6
  92.7 0.2 copy-done.7
  92.9 1.7 %shard_map.190 = (bf16[1024,128]{1,0:T(8,128)(2,1)}, bf16[1024,128]{1,0:T(8,128)(2,1)}, f32[1024,128]{1,0:T(8,128)S(1)}) custom-call(s32[64]{0:T(128)S(1)} %get-tuple-element.28.picks, f32[64,128]{1,0:T(8,128)S(1)} %get-tuple-element.32.kept, bf16[1024,128]{1,0:T(8,128)(2,1)S(1)} %copy-done.7, bf16[1024,128]{1,0:T(8,128)(2,1)S(1)} %bitcast.67, ...), custom_call_target="tpu_custom_call" | custom-call | flops 1000000 | bytes 3000000 | tf_op jit(solution)/shard_map/pallas_call | solution.py:115
  94.6 0.0 collective-permute-done.6.far
  94.6 0.0 collective-permute-done.7.near
  94.6 1.5 %shard_map.191 = bf16[1024,128]{1,0:T(8,128)(2,1)} custom-call(s32[64]{0:T(128)S(1)} %get-tuple-element.36.far_picks, s32[64]{0:T(128)S(1)} %get-tuple-element.37.near_picks, f32[64,128]{1,0:T(8,128)S(1)} %collective-permute-done.6.far, f32[64,128]{1,0:T(8,128)S(1)} %collective-permute-done.7.near, f32[1024,128]{1,0:T(8,128)S(1)} %get-tuple-element.38.update, ...), custom_call_target="tpu_custom_call" | custom-call | flops 1000000 | bytes 1000000 | tf_op jit(solution)/shard_map/pallas_call | solution.py:337
  96.2 2.2 %all-to-all-done.2 = f32[32,1,128]{2,1,0:T(1,128)S(1)} async-done(((f32[32,1,128]{2,1,0:T(1,128)}), f32[32,1,128]{2,1,0:T(1,128)S(1)}, u32[]{:S(2)}, u32[]{:S(2)}) %all-to-all-start.2) | async-done | bytes 16416 | tf_op jit(solution)/shard_map/all_to_all | solution.py:31
  98.3 0.6 reduce_sum.29
  (15 shorter events, 0.1 us)
Async XLA Ops:
  0.6 34.1 %collective-permute-start.2 = (bf16[128,1024]{1,0:T(8,128)(2,1)}, bf16[128,1024]{1,0:T(8,128)(2,1)S(1)}, u32[]{:S(2)}, u32[]{:S(2)}) collective-permute-start(bf16[128,1024]{1,0:T(8,128)(2,1)} %bitcast.79), channel_id=1, source_target_pairs={{0,4},{4,0},{1,5},{5,1},{2,6},{6,2},{3,7},{7,3},{8,12},{12,8},{9,1... | collective-permute-start | bytes 786440 | tf_op jit(solution)/shard_map/ppermute | solution.py:368
  19.0 5.2 %copy-start = (bf16[1,1024,128]{2,1,0:T(8,128)(2,1)S(1)}, bf16[1,1024,128]{2,1,0:T(8,128)(2,1)}, u32[]{:S(2)}) copy-start(bf16[1,1024,128]{2,1,0:T(8,128)(2,1)} %param.16) | copy-start | bytes 786436
  19.0 5.2 %copy-start.2 = (bf16[1,1024,128]{2,1,0:T(8,128)(2,1)S(1)}, bf16[1,1024,128]{2,1,0:T(8,128)(2,1)}, u32[]{:S(2)}) copy-start(bf16[1,1024,128]{2,1,0:T(8,128)(2,1)} %param.14) | copy-start | bytes 786436
  19.0 5.2 %copy-start.3 = (bf16[1,1024,128]{2,1,0:T(8,128)(2,1)S(1)}, bf16[1,1024,128]{2,1,0:T(8,128)(2,1)}, u32[]{:S(2)}) copy-start(bf16[1,1024,128]{2,1,0:T(8,128)(2,1)} %param.15) | copy-start | bytes 786436
  19.0 5.2 %copy-start.10 = (f32[1,1024,128]{2,1,0:T(8,128)S(1)}, f32[1,1024,128]{2,1,0:T(8,128)}, u32[]{:S(2)}) copy-start(f32[1,1024,128]{2,1,0:T(8,128)} %param.13) | copy-start | bytes 1572868
  19.0 18.4 %all-to-all-start = ((bf16[4,128,1024]{2,1,0:T(8,128)(2,1)}), bf16[4,128,1024]{2,1,0:T(8,128)(2,1)}, u32[]{:S(2)}, u32[]{:S(2)}) async-start(bf16[4,128,1024]{2,1,0:T(8,128)(2,1)} %broadcast_in_dim.35), calls=%async_computation | async-start | bytes 2097152 | tf_op jit(solution)/shard_map/all_to_all | solution.py:41
  24.2 10.4 %copy-start.11 = (s32[1,1024]{1,0:T(1,128)S(1)}, s32[1,1024]{1,0:T(1,128)}, u32[]{:S(2)}) copy-start(s32[1,1024]{1,0:T(1,128)} %param.21) | copy-start | bytes 12292
  24.7 21.6 %collective-permute-start = (bf16[64,128]{1,0:T(8,128)(2,1)S(1)}, bf16[64,128]{1,0:T(8,128)(2,1)S(1)}, u32[]{:S(2)}, u32[]{:S(2)}) collective-permute-start(bf16[64,128]{1,0:T(8,128)(2,1)S(1)} %get-tuple-element.53), channel_id=1, source_target_pairs={{0,504},{8,16},{16,8},{24,32},{32,24},{40,48},{48,40},{56,64},{64,... | collective-permute-start | bytes 49160 | tf_op jit(solution)/shard_map/ppermute | solution.py:24
  28.3 18.0 %collective-permute-start.1 = (bf16[64,128]{1,0:T(8,128)(2,1)S(1)}, bf16[64,128]{1,0:T(8,128)(2,1)S(1)}, u32[]{:S(2)}, u32[]{:S(2)}) collective-permute-start(bf16[64,128]{1,0:T(8,128)(2,1)S(1)} %get-tuple-element.53), channel_id=1, source_target_pairs={{0,8},{8,0},{16,24},{24,16},{32,40},{40,32},{48,56},{56,48},{64,72... | collective-permute-start | bytes 49160 | tf_op jit(solution)/shard_map/ppermute | solution.py:25
  37.4 27.1 %collective-permute-start.3 = (bf16[128,1024]{1,0:T(8,128)(2,1)S(1)}, bf16[128,1024]{1,0:T(8,128)(2,1)S(1)}, u32[]{:S(2)}, u32[]{:S(2)}) collective-permute-start(bf16[128,1024]{1,0:T(8,128)(2,1)S(1)} %collective-permute-done.2.other_0), channel_id=1, source_target_pairs={{0,1},{1,2},{2,3},{3,0},{4,5},{5,6},{6,7},{7,4},{8,9},{9,10},{10,1... | collective-permute-start | bytes 786440 | tf_op jit(solution)/shard_map/ppermute | solution.py:49
  39.7 24.8 %collective-permute-start.4 = (bf16[128,1024]{1,0:T(8,128)(2,1)S(1)}, bf16[128,1024]{1,0:T(8,128)(2,1)S(1)}, u32[]{:S(2)}, u32[]{:S(2)}) collective-permute-start(bf16[128,1024]{1,0:T(8,128)(2,1)S(1)} %collective-permute-done.2.other_0), channel_id=1, source_target_pairs={{0,2},{1,3},{2,0},{3,1},{4,6},{5,7},{6,4},{7,5},{8,10},{9,11},{10,... | collective-permute-start | bytes 786440 | tf_op jit(solution)/shard_map/ppermute | solution.py:49
  43.3 21.2 %collective-permute-start.5 = (bf16[128,1024]{1,0:T(8,128)(2,1)S(1)}, bf16[128,1024]{1,0:T(8,128)(2,1)S(1)}, u32[]{:S(2)}, u32[]{:S(2)}) collective-permute-start(bf16[128,1024]{1,0:T(8,128)(2,1)S(1)} %collective-permute-done.2.other_0), channel_id=1, source_target_pairs={{0,3},{1,0},{2,1},{3,2},{4,7},{5,4},{6,5},{7,6},{8,11},{9,8},{10,9... | collective-permute-start | bytes 786440 | tf_op jit(solution)/shard_map/ppermute | solution.py:49
  46.3 18.2 %copy-start.8 = (bf16[1024,128]{1,0:T(8,128)(2,1)S(1)}, bf16[1024,128]{1,0:T(8,128)(2,1)}, u32[]{:S(2)}) copy-start(bf16[1024,128]{1,0:T(8,128)(2,1)} %key_weight.1) | copy-start | bytes 786436
  46.3 18.2 %copy-start.9 = (bf16[1024,128]{1,0:T(8,128)(2,1)S(1)}, bf16[1024,128]{1,0:T(8,128)(2,1)}, u32[]{:S(2)}) copy-start(bf16[1024,128]{1,0:T(8,128)(2,1)} %value_weight.1) | copy-start | bytes 786436
  48.7 38.6 %all-to-all-start.1 = ((f32[16,1,128]{2,1,0:T(1,128)}), f32[16,1,128]{2,1,0:T(1,128)S(1)}, u32[]{:S(2)}, u32[]{:S(2)}) async-start(f32[16,1,128]{2,1,0:T(1,128)} %broadcast_in_dim.38), calls=%async_computation.1 | async-start | bytes 16384 | tf_op jit(solution)/shard_map/all_to_all | solution.py:31
  64.5 27.0 %copy-start.1 = (bf16[1,1024,128]{2,1,0:T(8,128)(2,1)S(1)}, bf16[1,1024,128]{2,1,0:T(8,128)(2,1)}, u32[]{:S(2)}) copy-start(bf16[1,1024,128]{2,1,0:T(8,128)(2,1)} %param.16) | copy-start | bytes 786436
  72.8 21.8 %collective-permute-start.6 = (f32[64,128]{1,0:T(8,128)S(1)}, f32[64,128]{1,0:T(8,128)S(1)}, u32[]{:S(2)}, u32[]{:S(2)}) collective-permute-start(f32[64,128]{1,0:T(8,128)S(1)} %get-tuple-element.32.kept), channel_id=1, source_target_pairs={{0,504},{8,16},{16,8},{24,32},{32,24},{40,48},{48,40},{56,64},{64,... | collective-permute-start | bytes 98312 | tf_op jit(solution)/shard_map/ppermute | solution.py:24
  78.8 15.8 %collective-permute-start.7 = (f32[64,128]{1,0:T(8,128)S(1)}, f32[64,128]{1,0:T(8,128)S(1)}, u32[]{:S(2)}, u32[]{:S(2)}) collective-permute-start(f32[64,128]{1,0:T(8,128)S(1)} %get-tuple-element.32.kept), channel_id=1, source_target_pairs={{0,8},{8,0},{16,24},{24,16},{32,40},{40,32},{48,56},{56,48},{64,72... | collective-permute-start | bytes 98312 | tf_op jit(solution)/shard_map/ppermute | solution.py:25
  87.9 10.5 %all-to-all-start.2 = ((f32[32,1,128]{2,1,0:T(1,128)}), f32[32,1,128]{2,1,0:T(1,128)S(1)}, u32[]{:S(2)}, u32[]{:S(2)}) async-start(f32[32,1,128]{2,1,0:T(1,128)} %broadcast_in_dim.39), calls=%async_computation.2 | async-start | bytes 32768 | tf_op jit(solution)/shard_map/all_to_all | solution.py:31
  91.5 1.0 copy-start.4
  91.5 1.0 %copy-start.5 = (bf16[1,1024,128]{2,1,0:T(8,128)(2,1)S(1)}, bf16[1,1024,128]{2,1,0:T(8,128)(2,1)}, u32[]{:S(2)}) copy-start(bf16[1,1024,128]{2,1,0:T(8,128)(2,1)} %param.17) | copy-start | bytes 786436
  91.5 1.2 %copy-start.6 = (bf16[1,1024,128]{2,1,0:T(8,128)(2,1)S(1)}, bf16[1,1024,128]{2,1,0:T(8,128)(2,1)}, u32[]{:S(2)}) copy-start(bf16[1,1024,128]{2,1,0:T(8,128)(2,1)} %param.19) | copy-start | bytes 786436
  91.5 1.4 %copy-start.7 = (bf16[1024,128]{1,0:T(8,128)(2,1)S(1)}, bf16[1024,128]{1,0:T(8,128)(2,1)}, u32[]{:S(2)}) copy-start(bf16[1024,128]{1,0:T(8,128)(2,1)} %get-tuple-element.33.gradient) | copy-start | bytes 786436

commit v9 on v8

--- a/solution.py
+++ b/solution.py
@@ -17,12 +17,15 @@
 step_rate = 0.5
 
 
-def swaps(value):
+def near_swap(value):
     count = lax.axis_size(BLK)
-    near = [(r, r ^ 1) for r in range(count)]
-    far = [(r, (r + 1) % count if r % 2 else (r - 1) % count) for r in range(count)]
-    from_far = lax.ppermute(value, BLK, far)
-    return lax.ppermute(value, BLK, near), from_far
+    return lax.ppermute(value, BLK, [(r, r ^ 1) for r in range(count)])
+
+
+def far_swap(value):
+    count = lax.axis_size(BLK)
+    pairs = [(r, (r + 1) % count if r % 2 else (r - 1) % count) for r in range(count)]
+    return lax.ppermute(value, BLK, pairs)
 
 
 def spread_rows(value, axes):
@@ -169,15 +172,14 @@
         fetch(source, joined.at[:, index * width : (index + 1) * width])
         for index, source in enumerate((query_weight, key_weight, value_weight))
     ]
-    parts = []
-    for part in range(own.shape[0] // WINDOW):
-        place = pl.multiple_of(spots[0] + part * WINDOW, WINDOW)
-        source = own.at[part * WINDOW : (part + 1) * WINDOW, :]
-        parts.append(fetch(source, tokens.at[pl.ds(place, WINDOW), :]))
+    half = own.shape[0]
+    other_parts = []
     for index, source in enumerate((other_0, other_1, other_2, other_3)):
         size = source.shape[0]
         place = pl.multiple_of(spots[1 + index], 128)
-        parts.append(fetch(source, tokens.at[pl.ds(place, size), :]))
+        other_parts.append(fetch(source, tokens.at[pl.ds(place, size), :]))
+    place = pl.multiple_of(spots[0], half)
+    own_parts = [fetch(own, tokens.at[pl.ds(place, half), :])]
     given_copy = fetch(out_grad_in, out_grad)
     late = [
         fetch(tracker_in, tracker),
@@ -187,8 +189,7 @@
     ]
     for copy in ready:
         copy.wait()
-    half = own.shape[0]
-    for place, group in ((spots[0], parts[:-4]), (half - spots[0], parts[-4:])):
+    for place, group in ((half - spots[0], other_parts), (spots[0], own_parts)):
         for copy in group:
             copy.wait()
         window = pl.ds(pl.multiple_of(place, half), half)
@@ -304,17 +305,17 @@
     blend = (mixed[...].astype(jnp.float32) + total[...] / 3.0).astype(jnp.bfloat16)
     mixed_new[...] = blend
     gap = blend.astype(jnp.float32) - fresh.astype(jnp.float32)
-    gaps[...] = jnp.sum(gap * gap, axis=0, keepdims=True)
-
-
-def param_step(own_picks, far_picks, near_picks, *arrays):
+    gaps[...] = jnp.broadcast_to(jnp.sum(gap * gap, axis=0, keepdims=True), gaps.shape)
+
+
+def param_step(count, own_picks, far_picks, near_picks, *arrays):
     scalars = [pl.BlockSpec(memory_space=pltpu.SMEM)] * 3
     whole = pl.BlockSpec(memory_space=pltpu.VMEM)
     rows, width = arrays[3].shape
     narrow = jax.ShapeDtypeStruct((rows, width), jnp.bfloat16)
     return pl.pallas_call(
         param_kernel,
-        out_shape=(narrow, narrow, jax.ShapeDtypeStruct((1, width), jnp.float32)),
+        out_shape=(narrow, narrow, jax.ShapeDtypeStruct((count, width), jnp.float32)),
         in_specs=scalars + [whole] * len(arrays),
         out_specs=(whole,) * 3,
         scratch_shapes=[pltpu.VMEM((rows, width), jnp.float32)],
@@ -377,12 +378,14 @@
         - step_rate * tracker[0].astype(jnp.float32)
     )
     param_values = select_rows(own_picks[0], weights_new - copy_value)
-    param_near, param_far = swaps(param_values.astype(jnp.bfloat16))
+    param_sent = param_values.astype(jnp.bfloat16)
+    param_far, param_near = far_swap(param_sent), near_swap(param_sent)
     param_picks = (picks[0][0], picks[2][0], picks[1][0])
     own_half, other, starts, later_picks = lax.optimization_barrier(
         (own_half, other, image_starts(image_ids[0]), [kept[1] for kept in picks])
     )
     copies_new, mixed_new, partial_sums = param_step(
+        lax.axis_size(("blk_1", "tp_0")),
         *param_picks,
         param_values,
         param_far,
@@ -392,7 +395,7 @@
     )
     blocks = pass_tokens(other)
     _, partial_sums = lax.optimization_barrier((other, partial_sums))
-    partial_sums = spread_rows(partial_sums, ("blk_1", "tp_0"))
+    partial_sums = lax.all_to_all(partial_sums, ("blk_1", "tp_0"), 0, 0, tiled=True)
     spots = [high * half] + [
         (1 - high) * half + ((place - shift) % len(blocks)) * height for shift in range(len(blocks))
     ]
@@ -412,7 +415,6 @@
         tracker_mixed[0],
         grad_prev[0],
     )
-    near, far = swaps(tracker_values)
     tracker_new, tracker_copy_new, update = tracker_step(
         later_picks[0],
         tracker_values,
@@ -422,10 +424,12 @@
         tracker_mixed[0],
         grad_prev[0],
     )
+    far = far_swap(tracker_values)
     _, partial_sums = lax.optimization_barrier((tracker_values, partial_sums))
-    partial_sums = spread_rows(
-        jnp.sum(partial_sums, axis=0, keepdims=True), ("blk_0", "blk_2", "tp_1")
-    )
+    partial_sums = jnp.sum(partial_sums, axis=0, keepdims=True)
+    tracker_values, partial_sums = lax.optimization_barrier((tracker_values, partial_sums))
+    near = near_swap(tracker_values)
+    partial_sums = spread_rows(partial_sums, ("blk_0", "blk_2", "tp_1"))
     tracker_mixed_new = mix_step(
         later_picks[2], later_picks[1], far, near, update, tracker_mixed[0]
     )

time: 101 us -> 100 us (0.990)
    all_to_all x0 -> x1, starting transfers between devices: none -> 15.8 us  [per_device(): lax.all_to_all(partial_sums, ('blk_1', 'tp_0'), 0, 0, tiled=True)]
    all_to_all x2 -> x1, starting transfers between devices: 19.4 us -> 3.63 us  [spread_rows(): return lax.all_to_all(rows, axes, 0, 0, tiled=True)]
    all_to_all x2 -> x1, waiting for transfers between devices: 2.16 us -> 2.17 us  [spread_rows(): return lax.all_to_all(rows, axes, 0, 0, tiled=True)]
  transfers between devices with their start and end apart: 11 -> 11, of which waited for: 2 -> 2; matrix products, arithmetic and copies ran while one was open for 6% -> 5% of each run, Pallas kernels for 13% -> 13%
where the time goes in v9:
time: 100 us; the launch traced here: 99.6 us
  starting transfers between devices  72.9 us (73%)
  Pallas kernels  12.8 us (13%)
  waiting for transfers between devices  4.84 us (5%)
  local copies, waits for them, and re-layouts  3.94 us (4%)
  between operations  2.79 us (3%)
  other arithmetic  1.85 us (2%)
    ppermute x1, starting transfers between devices, per_device(): other = lax.ppermute(tokens[0], 'tp_0', [(0, 1), (1, 0)])  16.3 us
    all_to_all x1, starting transfers between devices, per_device(): lax.all_to_all(partial_sums, ('blk_1', 'tp_0'), 0, 0, tiled=True)  15.8 us
    ppermute x2, starting transfers between devices, near_swap(): return lax.ppermute(value, BLK, [(r, r ^ 1) for r in range(count)])  14.6 us
    ppermute x2, starting transfers between devices, far_swap(): return lax.ppermute(value, BLK, pairs)  9.62 us
    ppermute x3, starting transfers between devices, pass_tokens(): blocks.append(lax.ppermute(value, 'tp_1', pairs))  8.56 us
    pallas_call x1, Pallas kernels, gradient_step(): pl.pallas_call(gradient_kernel, out_shape=(narrow, jax.ShapeDtypeStruct((...  7.69 us
    all_to_all x1, starting transfers between devices, spread_tokens(): lax.all_to_all(blocks, 'tp_1', 0, 0, tiled=True).reshape(-1, value.shape[1])  4.4 us
    all_to_all x1, starting transfers between devices, spread_rows(): return lax.all_to_all(rows, axes, 0, 0, tiled=True)  3.63 us
  transfers between devices with their start and end apart: 11, of which 2 were waited for; matrix products, arithmetic and copies ran while one was open for 5% of the time, Pallas kernels for 13%

profile of v9, /device:TPU:1, one launch (start us, length us, event | category | flops | bytes accessed | tf_op | source)
XLA Modules:
  0.0 99.6 jit_solution(17863630729002870803)
XLA Ops:
  0.6 16.3 %collective-permute-start.2 = (bf16[128,1024]{1,0:T(8,128)(2,1)}, bf16[128,1024]{1,0:T(8,128)(2,1)S(1)}, u32[]{:S(2)}, u32[]{:S(2)}) collective-permute-start(bf16[128,1024]{1,0:T(8,128)(2,1)} %bitcast.82), channel_id=1, source_target_pairs={{0,4},{4,0},{1,5},{5,1},{2,6},{6,2},{3,7},{7,3},{8,12},{12,8},{9,1... | collective-permute-start | bytes 786440 | tf_op jit(solution)/shard_map/ppermute | solution.py:369
  16.9 2.1 %broadcast_in_dim.32 = bf16[4,128,1024]{2,1,0:T(8,128)(2,1)} broadcast(bf16[128,1024]{1,0:T(8,128)(2,1)} %bitcast.83), dimensions={1,2} | broadcast | bytes 1310720 | tf_op jit(solution)/shard_map/broadcast_in_dim | solution.py:43
  19.0 4.4 %all-to-all-start = ((bf16[4,128,1024]{2,1,0:T(8,128)(2,1)}), bf16[4,128,1024]{2,1,0:T(8,128)(2,1)}, u32[]{:S(2)}, u32[]{:S(2)}) async-start(bf16[4,128,1024]{2,1,0:T(8,128)(2,1)} %broadcast_in_dim.32), calls=%async_computation | async-start | bytes 2097152 | tf_op jit(solution)/shard_map/all_to_all | solution.py:44
  23.4 0.7 constant_dynamic-slice_fusion
  24.2 0.0 copy-done.2
  24.2 0.0 copy-done.3
  24.2 0.0 copy-done.10
  24.2 0.0 copy-start.11
  24.2 0.5 fusion.11
  24.7 3.6 %collective-permute-start = (bf16[64,128]{1,0:T(8,128)(2,1)S(1)}, bf16[64,128]{1,0:T(8,128)(2,1)S(1)}, u32[]{:S(2)}, u32[]{:S(2)}) collective-permute-start(bf16[64,128]{1,0:T(8,128)(2,1)S(1)} %get-tuple-element.57), channel_id=1, source_target_pairs={{0,504},{8,16},{16,8},{24,32},{32,24},{40,48},{48,40},{56,64},{64,... | collective-permute-start | bytes 49160 | tf_op jit(solution)/shard_map/ppermute | solution.py:28
  28.3 6.2 %collective-permute-start.1 = (bf16[64,128]{1,0:T(8,128)(2,1)S(1)}, bf16[64,128]{1,0:T(8,128)(2,1)S(1)}, u32[]{:S(2)}, u32[]{:S(2)}) collective-permute-start(bf16[64,128]{1,0:T(8,128)(2,1)S(1)} %get-tuple-element.57), channel_id=1, source_target_pairs={{0,8},{8,0},{16,24},{24,16},{32,40},{40,32},{48,56},{56,48},{64,72... | collective-permute-start | bytes 49160 | tf_op jit(solution)/shard_map/ppermute | solution.py:22
  34.6 0.1 convert_reduce_fusion.starts
  34.7 0.0 collective-permute-done.2.other_0
  34.7 2.6 %all-to-all-done = bf16[4,128,1024]{2,1,0:T(8,128)(2,1)} async-done(((bf16[4,128,1024]{2,1,0:T(8,128)(2,1)}), bf16[4,128,1024]{2,1,0:T(8,128)(2,1)}, u32[]{:S(2)}, u32[]{:S(2)}) %all-to-all-start) | async-done | bytes 1048608 | tf_op jit(solution)/shard_map/all_to_all | solution.py:44
  37.4 2.3 %collective-permute-start.3 = (bf16[128,1024]{1,0:T(8,128)(2,1)S(1)}, bf16[128,1024]{1,0:T(8,128)(2,1)S(1)}, u32[]{:S(2)}, u32[]{:S(2)}) collective-permute-start(bf16[128,1024]{1,0:T(8,128)(2,1)S(1)} %collective-permute-done.2.other_0), channel_id=1, source_target_pairs={{0,1},{1,2},{2,3},{3,0},{4,5},{5,6},{6,7},{7,4},{8,9},{9,10},{10,1... | collective-permute-start | bytes 786440 | tf_op jit(solution)/shard_map/ppermute | solution.py:52
  39.7 3.5 %collective-permute-start.4 = (bf16[128,1024]{1,0:T(8,128)(2,1)S(1)}, bf16[128,1024]{1,0:T(8,128)(2,1)S(1)}, u32[]{:S(2)}, u32[]{:S(2)}) collective-permute-start(bf16[128,1024]{1,0:T(8,128)(2,1)S(1)} %collective-permute-done.2.other_0), channel_id=1, source_target_pairs={{0,2},{1,3},{2,0},{3,1},{4,6},{5,7},{6,4},{7,5},{8,10},{9,11},{10,... | collective-permute-start | bytes 786440 | tf_op jit(solution)/shard_map/ppermute | solution.py:52
  43.3 2.7 %collective-permute-start.5 = (bf16[128,1024]{1,0:T(8,128)(2,1)S(1)}, bf16[128,1024]{1,0:T(8,128)(2,1)S(1)}, u32[]{:S(2)}, u32[]{:S(2)}) collective-permute-start(bf16[128,1024]{1,0:T(8,128)(2,1)S(1)} %collective-permute-done.2.other_0), channel_id=1, source_target_pairs={{0,3},{1,0},{2,1},{3,2},{4,7},{5,4},{6,5},{7,6},{8,11},{9,8},{10,9... | collective-permute-start | bytes 786440 | tf_op jit(solution)/shard_map/ppermute | solution.py:52
  46.0 0.2 multiply_convert_fusion.query_weight
  46.2 0.1 stack.23.spots
  46.3 0.0 collective-permute-done.far
  46.3 0.0 collective-permute-done.1.near
  46.3 0.0 copy-start.9
  46.3 1.8 %shard_map.188 = (bf16[1024,128]{1,0:T(8,128)(2,1)}, bf16[1024,128]{1,0:T(8,128)(2,1)}, f32[16,128]{1,0:T(8,128)}) custom-call(s32[64]{0:T(128)S(1)} %get-tuple-element.56.own_picks, s32[64]{0:T(128)S(1)} %get-tuple-element.52.far_picks, s32[64]{0:T(128)S(1)} %get-tuple-element.59.near_picks, f32[64,128]{1,0:T(8,128)S(1)} %get-tuple-element.58.own, ...), custom_call_target="tpu_custom_call" | custom-call | flops 1000 | bytes 1000 | tf_op jit(solution)/shard_map/pallas_call | solution.py:316
  48.1 15.8 %all-to-all-start.1 = ((f32[16,1,128]{2,1,0:T(1,128)}), f32[16,1,128]{2,1,0:T(1,128)S(1)}, u32[]{:S(2)}, u32[]{:S(2)}) async-start(f32[16,1,128]{2,1,0:T(1,128)} %bitcast.27), calls=%async_computation.1 | async-start | bytes 16384 | tf_op jit(solution)/shard_map/all_to_all | solution.py:398
  63.9 0.0 collective-permute-done.3.other_1
  63.9 0.0 collective-permute-done.4.other_2
  63.9 0.0 collective-permute-done.5.other_3
  64.0 0.0 copy-start.1
  64.0 7.7 %shard_map.189 = (bf16[1024,128]{1,0:T(8,128)(2,1)}, f32[64,128]{1,0:T(8,128)S(1)}) custom-call(s32[5]{0:T(128)S(1)} %stack.23.spots, s32[8]{0:T(128)S(1)} %convert_reduce_fusion.starts, s32[64]{0:T(128)S(1)} %get-tuple-element.30.picks, bf16[512,1024]{1,0:T(8,128)(2,1)} %bitcast.10.own, bf16[128,1024]{1,0:T(8,128)(2,1)S(1)} %collective-permute-done.2.other_0, ...), custom_call_target="tpu_custom_call" | custom-call | flops 2000000000 | bytes 8000000 | tf_op jit(solution)/shard_map/pallas_call | solution.py:253
  71.7 6.0 %collective-permute-start.6 = (f32[64,128]{1,0:T(8,128)S(1)}, f32[64,128]{1,0:T(8,128)S(1)}, u32[]{:S(2)}, u32[]{:S(2)}) collective-permute-start(f32[64,128]{1,0:T(8,128)S(1)} %get-tuple-element.43.kept), channel_id=1, source_target_pairs={{0,504},{8,16},{16,8},{24,32},{32,24},{40,48},{48,40},{56,64},{64,... | collective-permute-start | bytes 98312 | tf_op jit(solution)/shard_map/ppermute | solution.py:28
  77.7 0.0 all-to-all-done.1
  77.7 8.4 %collective-permute-start.7 = (f32[64,128]{1,0:T(8,128)S(1)}, f32[64,128]{1,0:T(8,128)S(1)}, u32[]{:S(2)}, u32[]{:S(2)}) collective-permute-start(f32[64,128]{1,0:T(8,128)S(1)} %get-tuple-element.43.kept), channel_id=1, source_target_pairs={{0,8},{8,0},{16,24},{24,16},{32,40},{40,32},{48,56},{56,48},{64,72... | collective-permute-start | bytes 98312 | tf_op jit(solution)/shard_map/ppermute | solution.py:22
  86.1 0.6 broadcast_in_dim.36
  86.7 3.6 %all-to-all-start.2 = ((f32[32,1,128]{2,1,0:T(1,128)}), f32[32,1,128]{2,1,0:T(1,128)S(1)}, u32[]{:S(2)}, u32[]{:S(2)}) async-start(f32[32,1,128]{2,1,0:T(1,128)} %broadcast_in_dim.36), calls=%async_computation.2 | async-start | bytes 32768 | tf_op jit(solution)/shard_map/all_to_all | solution.py:34
  90.4 0.0 copy-start.4
  90.4 0.0 copy-start.5
  90.4 0.0 copy-start.6
  90.4 0.0 copy-start.7
  90.4 0.9 multiply_subtract_fusion
  91.3 0.0 copy-done.5
  91.4 0.2 copy-done.6
  91.5 0.2 copy-done.7
  91.7 1.7 %shard_map.190 = (bf16[1024,128]{1,0:T(8,128)(2,1)}, bf16[1024,128]{1,0:T(8,128)(2,1)}, f32[1024,128]{1,0:T(8,128)S(1)}) custom-call(s32[64]{0:T(128)S(1)} %get-tuple-element.30.picks, f32[64,128]{1,0:T(8,128)S(1)} %get-tuple-element.43.kept, bf16[1024,128]{1,0:T(8,128)(2,1)S(1)} %copy-done.7, bf16[1024,128]{1,0:T(8,128)(2,1)S(1)} %bitcast.71, ...), custom_call_target="tpu_custom_call" | custom-call | flops 1000000 | bytes 3000000 | tf_op jit(solution)/shard_map/pallas_call | solution.py:118
  93.5 0.0 collective-permute-done.7.near
  93.5 0.0 collective-permute-done.6.far
  93.5 1.5 %shard_map.191 = bf16[1024,128]{1,0:T(8,128)(2,1)} custom-call(s32[64]{0:T(128)S(1)} %get-tuple-element.38.far_picks, s32[64]{0:T(128)S(1)} %get-tuple-element.39.near_picks, f32[64,128]{1,0:T(8,128)S(1)} %collective-permute-done.6.far, f32[64,128]{1,0:T(8,128)S(1)} %collective-permute-done.7.near, f32[1024,128]{1,0:T(8,128)S(1)} %get-tuple-element.44.update, ...), custom_call_target="tpu_custom_call" | custom-call | flops 1000000 | bytes 1000000 | tf_op jit(solution)/shard_map/pallas_call | solution.py:338
  95.0 2.2 %all-to-all-done.2 = f32[32,1,128]{2,1,0:T(1,128)S(1)} async-done(((f32[32,1,128]{2,1,0:T(1,128)}), f32[32,1,128]{2,1,0:T(1,128)S(1)}, u32[]{:S(2)}, u32[]{:S(2)}) %all-to-all-start.2) | async-done | bytes 16416 | tf_op jit(solution)/shard_map/all_to_all | solution.py:34
  97.2 0.6 reduce_sum.29
  (14 shorter events, 0.0 us)
Async XLA Ops:
  0.6 34.1 %collective-permute-start.2 = (bf16[128,1024]{1,0:T(8,128)(2,1)}, bf16[128,1024]{1,0:T(8,128)(2,1)S(1)}, u32[]{:S(2)}, u32[]{:S(2)}) collective-permute-start(bf16[128,1024]{1,0:T(8,128)(2,1)} %bitcast.82), channel_id=1, source_target_pairs={{0,4},{4,0},{1,5},{5,1},{2,6},{6,2},{3,7},{7,3},{8,12},{12,8},{9,1... | collective-permute-start | bytes 786440 | tf_op jit(solution)/shard_map/ppermute | solution.py:369
  19.0 5.2 %copy-start = (bf16[1,1024,128]{2,1,0:T(8,128)(2,1)S(1)}, bf16[1,1024,128]{2,1,0:T(8,128)(2,1)}, u32[]{:S(2)}) copy-start(bf16[1,1024,128]{2,1,0:T(8,128)(2,1)} %param.16) | copy-start | bytes 786436
  19.0 5.2 %copy-start.2 = (bf16[1,1024,128]{2,1,0:T(8,128)(2,1)S(1)}, bf16[1,1024,128]{2,1,0:T(8,128)(2,1)}, u32[]{:S(2)}) copy-start(bf16[1,1024,128]{2,1,0:T(8,128)(2,1)} %param.14) | copy-start | bytes 786436
  19.0 5.2 %copy-start.3 = (bf16[1,1024,128]{2,1,0:T(8,128)(2,1)S(1)}, bf16[1,1024,128]{2,1,0:T(8,128)(2,1)}, u32[]{:S(2)}) copy-start(bf16[1,1024,128]{2,1,0:T(8,128)(2,1)} %param.15) | copy-start | bytes 786436
  19.0 5.2 %copy-start.10 = (f32[1,1024,128]{2,1,0:T(8,128)S(1)}, f32[1,1024,128]{2,1,0:T(8,128)}, u32[]{:S(2)}) copy-start(f32[1,1024,128]{2,1,0:T(8,128)} %param.13) | copy-start | bytes 1572868
  19.0 18.4 %all-to-all-start = ((bf16[4,128,1024]{2,1,0:T(8,128)(2,1)}), bf16[4,128,1024]{2,1,0:T(8,128)(2,1)}, u32[]{:S(2)}, u32[]{:S(2)}) async-start(bf16[4,128,1024]{2,1,0:T(8,128)(2,1)} %broadcast_in_dim.32), calls=%async_computation | async-start | bytes 2097152 | tf_op jit(solution)/shard_map/all_to_all | solution.py:44
  24.2 10.4 %copy-start.11 = (s32[1,1024]{1,0:T(1,128)S(1)}, s32[1,1024]{1,0:T(1,128)}, u32[]{:S(2)}) copy-start(s32[1,1024]{1,0:T(1,128)} %param.21) | copy-start | bytes 12292
  24.7 21.6 %collective-permute-start = (bf16[64,128]{1,0:T(8,128)(2,1)S(1)}, bf16[64,128]{1,0:T(8,128)(2,1)S(1)}, u32[]{:S(2)}, u32[]{:S(2)}) collective-permute-start(bf16[64,128]{1,0:T(8,128)(2,1)S(1)} %get-tuple-element.57), channel_id=1, source_target_pairs={{0,504},{8,16},{16,8},{24,32},{32,24},{40,48},{48,40},{56,64},{64,... | collective-permute-start | bytes 49160 | tf_op jit(solution)/shard_map/ppermute | solution.py:28
  28.3 18.0 %collective-permute-start.1 = (bf16[64,128]{1,0:T(8,128)(2,1)S(1)}, bf16[64,128]{1,0:T(8,128)(2,1)S(1)}, u32[]{:S(2)}, u32[]{:S(2)}) collective-permute-start(bf16[64,128]{1,0:T(8,128)(2,1)S(1)} %get-tuple-element.57), channel_id=1, source_target_pairs={{0,8},{8,0},{16,24},{24,16},{32,40},{40,32},{48,56},{56,48},{64,72... | collective-permute-start | bytes 49160 | tf_op jit(solution)/shard_map/ppermute | solution.py:22
  37.4 26.5 %collective-permute-start.3 = (bf16[128,1024]{1,0:T(8,128)(2,1)S(1)}, bf16[128,1024]{1,0:T(8,128)(2,1)S(1)}, u32[]{:S(2)}, u32[]{:S(2)}) collective-permute-start(bf16[128,1024]{1,0:T(8,128)(2,1)S(1)} %collective-permute-done.2.other_0), channel_id=1, source_target_pairs={{0,1},{1,2},{2,3},{3,0},{4,5},{5,6},{6,7},{7,4},{8,9},{9,10},{10,1... | collective-permute-start | bytes 786440 | tf_op jit(solution)/shard_map/ppermute | solution.py:52
  39.7 24.2 %collective-permute-start.4 = (bf16[128,1024]{1,0:T(8,128)(2,1)S(1)}, bf16[128,1024]{1,0:T(8,128)(2,1)S(1)}, u32[]{:S(2)}, u32[]{:S(2)}) collective-permute-start(bf16[128,1024]{1,0:T(8,128)(2,1)S(1)} %collective-permute-done.2.other_0), channel_id=1, source_target_pairs={{0,2},{1,3},{2,0},{3,1},{4,6},{5,7},{6,4},{7,5},{8,10},{9,11},{10,... | collective-permute-start | bytes 786440 | tf_op jit(solution)/shard_map/ppermute | solution.py:52
  43.3 20.7 %collective-permute-start.5 = (bf16[128,1024]{1,0:T(8,128)(2,1)S(1)}, bf16[128,1024]{1,0:T(8,128)(2,1)S(1)}, u32[]{:S(2)}, u32[]{:S(2)}) collective-permute-start(bf16[128,1024]{1,0:T(8,128)(2,1)S(1)} %collective-permute-done.2.other_0), channel_id=1, source_target_pairs={{0,3},{1,0},{2,1},{3,2},{4,7},{5,4},{6,5},{7,6},{8,11},{9,8},{10,9... | collective-permute-start | bytes 786440 | tf_op jit(solution)/shard_map/ppermute | solution.py:52
  46.3 17.7 %copy-start.8 = (bf16[1024,128]{1,0:T(8,128)(2,1)S(1)}, bf16[1024,128]{1,0:T(8,128)(2,1)}, u32[]{:S(2)}) copy-start(bf16[1024,128]{1,0:T(8,128)(2,1)} %key_weight.1) | copy-start | bytes 786436
  46.3 17.7 %copy-start.9 = (bf16[1024,128]{1,0:T(8,128)(2,1)S(1)}, bf16[1024,128]{1,0:T(8,128)(2,1)}, u32[]{:S(2)}) copy-start(bf16[1024,128]{1,0:T(8,128)(2,1)} %value_weight.1) | copy-start | bytes 786436
  48.1 29.5 %all-to-all-start.1 = ((f32[16,1,128]{2,1,0:T(1,128)}), f32[16,1,128]{2,1,0:T(1,128)S(1)}, u32[]{:S(2)}, u32[]{:S(2)}) async-start(f32[16,1,128]{2,1,0:T(1,128)} %bitcast.27), calls=%async_computation.1 | async-start | bytes 16384 | tf_op jit(solution)/shard_map/all_to_all | solution.py:398
  64.0 26.4 %copy-start.1 = (bf16[1,1024,128]{2,1,0:T(8,128)(2,1)S(1)}, bf16[1,1024,128]{2,1,0:T(8,128)(2,1)}, u32[]{:S(2)}) copy-start(bf16[1,1024,128]{2,1,0:T(8,128)(2,1)} %param.16) | copy-start | bytes 786436
  71.7 21.8 %collective-permute-start.6 = (f32[64,128]{1,0:T(8,128)S(1)}, f32[64,128]{1,0:T(8,128)S(1)}, u32[]{:S(2)}, u32[]{:S(2)}) collective-permute-start(f32[64,128]{1,0:T(8,128)S(1)} %get-tuple-element.43.kept), channel_id=1, source_target_pairs={{0,504},{8,16},{16,8},{24,32},{32,24},{40,48},{48,40},{56,64},{64,... | collective-permute-start | bytes 98312 | tf_op jit(solution)/shard_map/ppermute | solution.py:28
  77.7 15.8 %collective-permute-start.7 = (f32[64,128]{1,0:T(8,128)S(1)}, f32[64,128]{1,0:T(8,128)S(1)}, u32[]{:S(2)}, u32[]{:S(2)}) collective-permute-start(f32[64,128]{1,0:T(8,128)S(1)} %get-tuple-element.43.kept), channel_id=1, source_target_pairs={{0,8},{8,0},{16,24},{24,16},{32,40},{40,32},{48,56},{56,48},{64,72... | collective-permute-start | bytes 98312 | tf_op jit(solution)/shard_map/ppermute | solution.py:22
  86.7 10.5 %all-to-all-start.2 = ((f32[32,1,128]{2,1,0:T(1,128)}), f32[32,1,128]{2,1,0:T(1,128)S(1)}, u32[]{:S(2)}, u32[]{:S(2)}) async-start(f32[32,1,128]{2,1,0:T(1,128)} %broadcast_in_dim.36), calls=%async_computation.2 | async-start | bytes 32768 | tf_op jit(solution)/shard_map/all_to_all | solution.py:34
  90.4 1.0 copy-start.4
  90.4 1.0 %copy-start.5 = (bf16[1,1024,128]{2,1,0:T(8,128)(2,1)S(1)}, bf16[1,1024,128]{2,1,0:T(8,128)(2,1)}, u32[]{:S(2)}) copy-start(bf16[1,1024,128]{2,1,0:T(8,128)(2,1)} %param.17) | copy-start | bytes 786436
  90.4 1.2 %copy-start.6 = (bf16[1,1024,128]{2,1,0:T(8,128)(2,1)S(1)}, bf16[1,1024,128]{2,1,0:T(8,128)(2,1)}, u32[]{:S(2)}) copy-start(bf16[1,1024,128]{2,1,0:T(8,128)(2,1)} %param.19) | copy-start | bytes 786436
  90.4 1.4 %copy-start.7 = (bf16[1024,128]{1,0:T(8,128)(2,1)S(1)}, bf16[1024,128]{1,0:T(8,128)(2,1)}, u32[]{:S(2)}) copy-start(bf16[1024,128]{1,0:T(8,128)(2,1)} %get-tuple-element.35.gradient) | copy-start | bytes 786436

commit v10 on v9

--- a/solution.py
+++ b/solution.py
@@ -427,7 +427,7 @@
     far = far_swap(tracker_values)
     _, partial_sums = lax.optimization_barrier((tracker_values, partial_sums))
     partial_sums = jnp.sum(partial_sums, axis=0, keepdims=True)
-    tracker_values, partial_sums = lax.optimization_barrier((tracker_values, partial_sums))
+    tracker_values, update = lax.optimization_barrier((tracker_values, update))
     near = near_swap(tracker_values)
     partial_sums = spread_rows(partial_sums, ("blk_0", "blk_2", "tp_1"))
     tracker_mixed_new = mix_step(

time: 100 us -> 98.8 us (0.988)
  waiting for transfers between devices: 4.84 us -> 2.66 us
    all_to_all x1, starting transfers between devices: 3.63 us -> 10 us  [spread_rows(): return lax.all_to_all(rows, axes, 0, 0, tiled=True)]
    ppermute x2, starting transfers between devices: 14.6 us -> 8.44 us  [near_swap(): return lax.ppermute(value, BLK, [(r, r ^ 1) for r in range(count)])]
    all_to_all x1, waiting for transfers between devices: 2.17 us -> 0.01 us  [spread_rows(): return lax.all_to_all(rows, axes, 0, 0, tiled=True)]
  transfers between devices with their start and end apart: 11 -> 11, of which waited for: 2 -> 1; matrix products, arithmetic and copies ran while one was open for 5% -> 5% of each run, Pallas kernels for 13% -> 13%
where the time goes in v10:
time: 98.8 us; the launch traced here: 98.2 us
  starting transfers between devices  73.2 us (74%)
  Pallas kernels  12.7 us (13%)
  local copies, waits for them, and re-layouts  4.49 us (5%)
  between operations  2.82 us (3%)
  waiting for transfers between devices  2.66 us (3%)
  other arithmetic  1.85 us (2%)
    ppermute x1, starting transfers between devices, per_device(): other = lax.ppermute(tokens[0], 'tp_0', [(0, 1), (1, 0)])  16.3 us
    all_to_all x1, starting transfers between devices, per_device(): lax.all_to_all(partial_sums, ('blk_1', 'tp_0'), 0, 0, tiled=True)  15.8 us
    all_to_all x1, starting transfers between devices, spread_rows(): return lax.all_to_all(rows, axes, 0, 0, tiled=True)  10 us
    ppermute x2, starting transfers between devices, far_swap(): return lax.ppermute(value, BLK, pairs)  9.64 us
    ppermute x3, starting transfers between devices, pass_tokens(): blocks.append(lax.ppermute(value, 'tp_1', pairs))  8.57 us
    ppermute x2, starting transfers between devices, near_swap(): return lax.ppermute(value, BLK, [(r, r ^ 1) for r in range(count)])  8.44 us
    pallas_call x1, Pallas kernels, gradient_step(): pl.pallas_call(gradient_kernel, out_shape=(narrow, jax.ShapeDtypeStruct((...  7.64 us
    all_to_all x1, starting transfers between devices, spread_tokens(): lax.all_to_all(blocks, 'tp_1', 0, 0, tiled=True).reshape(-1, value.shape[1])  4.39 us
  transfers between devices with their start and end apart: 11, of which 1 were waited for; matrix products, arithmetic and copies ran while one was open for 5% of the time, Pallas kernels for 13%

profile of v10, /device:TPU:1, one launch (start us, length us, event | category | flops | bytes accessed | tf_op | source)
XLA Modules:
  0.0 98.2 jit_solution(16325221519497473093)
XLA Ops:
  0.6 16.3 %collective-permute-start.2 = (bf16[128,1024]{1,0:T(8,128)(2,1)}, bf16[128,1024]{1,0:T(8,128)(2,1)S(1)}, u32[]{:S(2)}, u32[]{:S(2)}) collective-permute-start(bf16[128,1024]{1,0:T(8,128)(2,1)} %bitcast.80), channel_id=1, source_target_pairs={{0,4},{4,0},{1,5},{5,1},{2,6},{6,2},{3,7},{7,3},{8,12},{12,8},{9,1... | collective-permute-start | bytes 786440 | tf_op jit(solution)/shard_map/ppermute | solution.py:369
  16.9 2.1 %broadcast_in_dim.30 = bf16[4,128,1024]{2,1,0:T(8,128)(2,1)} broadcast(bf16[128,1024]{1,0:T(8,128)(2,1)} %bitcast.81), dimensions={1,2} | broadcast | bytes 1310720 | tf_op jit(solution)/shard_map/broadcast_in_dim | solution.py:43
  19.0 4.4 %all-to-all-start = ((bf16[4,128,1024]{2,1,0:T(8,128)(2,1)}), bf16[4,128,1024]{2,1,0:T(8,128)(2,1)}, u32[]{:S(2)}, u32[]{:S(2)}) async-start(bf16[4,128,1024]{2,1,0:T(8,128)(2,1)} %broadcast_in_dim.30), calls=%async_computation | async-start | bytes 2097152 | tf_op jit(solution)/shard_map/all_to_all | solution.py:44
  23.4 0.7 constant_dynamic-slice_fusion
  24.1 0.0 copy-done
  24.1 0.0 copy-done.2
  24.1 0.0 copy-done.3
  24.2 0.0 copy-done.10
  24.2 0.0 copy-start.12
  24.2 0.5 fusion.11
  24.7 3.7 %collective-permute-start = (bf16[64,128]{1,0:T(8,128)(2,1)S(1)}, bf16[64,128]{1,0:T(8,128)(2,1)S(1)}, u32[]{:S(2)}, u32[]{:S(2)}) collective-permute-start(bf16[64,128]{1,0:T(8,128)(2,1)S(1)} %get-tuple-element.57), channel_id=1, source_target_pairs={{0,504},{8,16},{16,8},{24,32},{32,24},{40,48},{48,40},{56,64},{64,... | collective-permute-start | bytes 49160 | tf_op jit(solution)/shard_map/ppermute | solution.py:28
  28.3 6.2 %collective-permute-start.1 = (bf16[64,128]{1,0:T(8,128)(2,1)S(1)}, bf16[64,128]{1,0:T(8,128)(2,1)S(1)}, u32[]{:S(2)}, u32[]{:S(2)}) collective-permute-start(bf16[64,128]{1,0:T(8,128)(2,1)S(1)} %get-tuple-element.57), channel_id=1, source_target_pairs={{0,8},{8,0},{16,24},{24,16},{32,40},{40,32},{48,56},{56,48},{64,72... | collective-permute-start | bytes 49160 | tf_op jit(solution)/shard_map/ppermute | solution.py:22
  34.6 0.0 copy-done.12
  34.6 0.1 convert_reduce_fusion.starts
  34.7 0.0 collective-permute-done.2.other_0
  34.7 2.6 %all-to-all-done = bf16[4,128,1024]{2,1,0:T(8,128)(2,1)} async-done(((bf16[4,128,1024]{2,1,0:T(8,128)(2,1)}), bf16[4,128,1024]{2,1,0:T(8,128)(2,1)}, u32[]{:S(2)}, u32[]{:S(2)}) %all-to-all-start) | async-done | bytes 1048608 | tf_op jit(solution)/shard_map/all_to_all | solution.py:44
  37.3 2.4 %collective-permute-start.3 = (bf16[128,1024]{1,0:T(8,128)(2,1)S(1)}, bf16[128,1024]{1,0:T(8,128)(2,1)S(1)}, u32[]{:S(2)}, u32[]{:S(2)}) collective-permute-start(bf16[128,1024]{1,0:T(8,128)(2,1)S(1)} %collective-permute-done.2.other_0), channel_id=1, source_target_pairs={{0,1},{1,2},{2,3},{3,0},{4,5},{5,6},{6,7},{7,4},{8,9},{9,10},{10,1... | collective-permute-start | bytes 786440 | tf_op jit(solution)/shard_map/ppermute | solution.py:52
  39.7 3.5 %collective-permute-start.4 = (bf16[128,1024]{1,0:T(8,128)(2,1)S(1)}, bf16[128,1024]{1,0:T(8,128)(2,1)S(1)}, u32[]{:S(2)}, u32[]{:S(2)}) collective-permute-start(bf16[128,1024]{1,0:T(8,128)(2,1)S(1)} %collective-permute-done.2.other_0), channel_id=1, source_target_pairs={{0,2},{1,3},{2,0},{3,1},{4,6},{5,7},{6,4},{7,5},{8,10},{9,11},{10,... | collective-permute-start | bytes 786440 | tf_op jit(solution)/shard_map/ppermute | solution.py:52
  43.2 2.7 %collective-permute-start.5 = (bf16[128,1024]{1,0:T(8,128)(2,1)S(1)}, bf16[128,1024]{1,0:T(8,128)(2,1)S(1)}, u32[]{:S(2)}, u32[]{:S(2)}) collective-permute-start(bf16[128,1024]{1,0:T(8,128)(2,1)S(1)} %collective-permute-done.2.other_0), channel_id=1, source_target_pairs={{0,3},{1,0},{2,1},{3,2},{4,7},{5,4},{6,5},{7,6},{8,11},{9,8},{10,9... | collective-permute-start | bytes 786440 | tf_op jit(solution)/shard_map/ppermute | solution.py:52
  45.9 0.2 multiply_convert_fusion.query_weight
  46.2 0.1 stack.23.spots
  46.3 0.0 collective-permute-done.far
  46.3 0.0 collective-permute-done.1.near
  46.3 0.0 copy-start.9
  46.3 1.8 %shard_map.188 = (bf16[1024,128]{1,0:T(8,128)(2,1)}, bf16[1024,128]{1,0:T(8,128)(2,1)}, f32[16,128]{1,0:T(8,128)}) custom-call(s32[64]{0:T(128)S(1)} %get-tuple-element.56.own_picks, s32[64]{0:T(128)S(1)} %get-tuple-element.52.far_picks, s32[64]{0:T(128)S(1)} %get-tuple-element.59.near_picks, f32[64,128]{1,0:T(8,128)S(1)} %get-tuple-element.58.own, ...), custom_call_target="tpu_custom_call" | custom-call | flops 1000 | bytes 1000 | tf_op jit(solution)/shard_map/pallas_call | solution.py:316
  48.1 15.8 %all-to-all-start.1 = ((f32[16,1,128]{2,1,0:T(1,128)}), f32[16,1,128]{2,1,0:T(1,128)S(1)}, u32[]{:S(2)}, u32[]{:S(2)}) async-start(f32[16,1,128]{2,1,0:T(1,128)} %bitcast.27), calls=%async_computation.1 | async-start | bytes 16384 | tf_op jit(solution)/shard_map/all_to_all | solution.py:398
  63.9 0.0 collective-permute-done.3.other_1
  63.9 0.0 collective-permute-done.4.other_2
  63.9 0.0 collective-permute-done.5.other_3
  64.0 0.0 copy-start.1
  64.0 0.0 copy-start.4
  64.0 0.0 copy-start.5
  64.0 0.0 copy-start.6
  64.0 7.6 %shard_map.189 = (bf16[1024,128]{1,0:T(8,128)(2,1)}, f32[64,128]{1,0:T(8,128)S(1)}) custom-call(s32[5]{0:T(128)S(1)} %stack.23.spots, s32[8]{0:T(128)S(1)} %convert_reduce_fusion.starts, s32[64]{0:T(128)S(1)} %get-tuple-element.30.picks, bf16[512,1024]{1,0:T(8,128)(2,1)} %bitcast.10.own, bf16[128,1024]{1,0:T(8,128)(2,1)S(1)} %collective-permute-done.2.other_0, ...), custom_call_target="tpu_custom_call" | custom-call | flops 2000000000 | bytes 8000000 | tf_op jit(solution)/shard_map/pallas_call | solution.py:253
  71.7 6.0 %collective-permute-start.6 = (f32[64,128]{1,0:T(8,128)S(1)}, f32[64,128]{1,0:T(8,128)S(1)}, u32[]{:S(2)}, u32[]{:S(2)}) collective-permute-start(f32[64,128]{1,0:T(8,128)S(1)} %get-tuple-element.41.kept), channel_id=1, source_target_pairs={{0,504},{8,16},{16,8},{24,32},{32,24},{40,48},{48,40},{56,64},{64,... | collective-permute-start | bytes 98312 | tf_op jit(solution)/shard_map/ppermute | solution.py:28
  77.7 0.0 all-to-all-done.1
  77.7 0.6 broadcast_in_dim.33
  78.3 10.0 %all-to-all-start.2 = ((f32[32,1,128]{2,1,0:T(1,128)}), f32[32,1,128]{2,1,0:T(1,128)S(1)}, u32[]{:S(2)}, u32[]{:S(2)}) async-start(f32[32,1,128]{2,1,0:T(1,128)} %broadcast_in_dim.33), calls=%async_computation.2 | async-start | bytes 32768 | tf_op jit(solution)/shard_map/all_to_all | solution.py:34
  88.4 0.0 copy-start.7
  88.4 0.9 copy-done.7
  89.3 1.7 %shard_map.190 = (bf16[1024,128]{1,0:T(8,128)(2,1)}, bf16[1024,128]{1,0:T(8,128)(2,1)}, f32[1024,128]{1,0:T(8,128)S(1)}) custom-call(s32[64]{0:T(128)S(1)} %get-tuple-element.30.picks, f32[64,128]{1,0:T(8,128)S(1)} %get-tuple-element.41.kept, bf16[1024,128]{1,0:T(8,128)(2,1)S(1)} %copy-done.7, bf16[1024,128]{1,0:T(8,128)(2,1)S(1)} %bitcast.69, ...), custom_call_target="tpu_custom_call" | custom-call | flops 1000000 | bytes 3000000 | tf_op jit(solution)/shard_map/pallas_call | solution.py:118
  91.1 2.2 %collective-permute-start.7 = (f32[64,128]{1,0:T(8,128)S(1)}, f32[64,128]{1,0:T(8,128)S(1)}, u32[]{:S(2)}, u32[]{:S(2)}) collective-permute-start(f32[64,128]{1,0:T(8,128)S(1)} %get-tuple-element.41.kept), channel_id=1, source_target_pairs={{0,8},{8,0},{16,24},{24,16},{32,40},{40,32},{48,56},{56,48},{64,72... | collective-permute-start | bytes 98312 | tf_op jit(solution)/shard_map/ppermute | solution.py:22
  93.3 0.9 multiply_subtract_fusion
  94.3 0.0 collective-permute-done.7.near
  94.3 0.0 collective-permute-done.6.far
  94.3 1.5 %shard_map.191 = bf16[1024,128]{1,0:T(8,128)(2,1)} custom-call(s32[64]{0:T(128)S(1)} %get-tuple-element.38.far_picks, s32[64]{0:T(128)S(1)} %get-tuple-element.39.near_picks, f32[64,128]{1,0:T(8,128)S(1)} %collective-permute-done.6.far, f32[64,128]{1,0:T(8,128)S(1)} %collective-permute-done.7.near, f32[1024,128]{1,0:T(8,128)S(1)} %get-tuple-element.42.update, ...), custom_call_target="tpu_custom_call" | custom-call | flops 1000000 | bytes 1000000 | tf_op jit(solution)/shard_map/pallas_call | solution.py:338
  95.8 0.0 all-to-all-done.2
  95.8 0.6 reduce_sum.29
  (16 shorter events, 0.1 us)
Async XLA Ops:
  0.6 34.1 %collective-permute-start.2 = (bf16[128,1024]{1,0:T(8,128)(2,1)}, bf16[128,1024]{1,0:T(8,128)(2,1)S(1)}, u32[]{:S(2)}, u32[]{:S(2)}) collective-permute-start(bf16[128,1024]{1,0:T(8,128)(2,1)} %bitcast.80), channel_id=1, source_target_pairs={{0,4},{4,0},{1,5},{5,1},{2,6},{6,2},{3,7},{7,3},{8,12},{12,8},{9,1... | collective-permute-start | bytes 786440 | tf_op jit(solution)/shard_map/ppermute | solution.py:369
  19.0 5.2 %copy-start = (bf16[1,1024,128]{2,1,0:T(8,128)(2,1)S(1)}, bf16[1,1024,128]{2,1,0:T(8,128)(2,1)}, u32[]{:S(2)}) copy-start(bf16[1,1024,128]{2,1,0:T(8,128)(2,1)} %param.16) | copy-start | bytes 786436
  19.0 5.2 %copy-start.2 = (bf16[1,1024,128]{2,1,0:T(8,128)(2,1)S(1)}, bf16[1,1024,128]{2,1,0:T(8,128)(2,1)}, u32[]{:S(2)}) copy-start(bf16[1,1024,128]{2,1,0:T(8,128)(2,1)} %param.14) | copy-start | bytes 786436
  19.0 5.2 %copy-start.3 = (bf16[1,1024,128]{2,1,0:T(8,128)(2,1)S(1)}, bf16[1,1024,128]{2,1,0:T(8,128)(2,1)}, u32[]{:S(2)}) copy-start(bf16[1,1024,128]{2,1,0:T(8,128)(2,1)} %param.15) | copy-start | bytes 786436
  19.0 5.2 %copy-start.10 = (f32[1,1024,128]{2,1,0:T(8,128)S(1)}, f32[1,1024,128]{2,1,0:T(8,128)}, u32[]{:S(2)}) copy-start(f32[1,1024,128]{2,1,0:T(8,128)} %param.13) | copy-start | bytes 1572868
  19.0 18.4 %all-to-all-start = ((bf16[4,128,1024]{2,1,0:T(8,128)(2,1)}), bf16[4,128,1024]{2,1,0:T(8,128)(2,1)}, u32[]{:S(2)}, u32[]{:S(2)}) async-start(bf16[4,128,1024]{2,1,0:T(8,128)(2,1)} %broadcast_in_dim.30), calls=%async_computation | async-start | bytes 2097152 | tf_op jit(solution)/shard_map/all_to_all | solution.py:44
  24.2 10.4 %copy-start.12 = (s32[1,1024]{1,0:T(1,128)S(1)}, s32[1,1024]{1,0:T(1,128)}, u32[]{:S(2)}) copy-start(s32[1,1024]{1,0:T(1,128)} %param.21) | copy-start | bytes 12292
  24.7 21.6 %collective-permute-start = (bf16[64,128]{1,0:T(8,128)(2,1)S(1)}, bf16[64,128]{1,0:T(8,128)(2,1)S(1)}, u32[]{:S(2)}, u32[]{:S(2)}) collective-permute-start(bf16[64,128]{1,0:T(8,128)(2,1)S(1)} %get-tuple-element.57), channel_id=1, source_target_pairs={{0,504},{8,16},{16,8},{24,32},{32,24},{40,48},{48,40},{56,64},{64,... | collective-permute-start | bytes 49160 | tf_op jit(solution)/shard_map/ppermute | solution.py:28
  28.3 17.9 %collective-permute-start.1 = (bf16[64,128]{1,0:T(8,128)(2,1)S(1)}, bf16[64,128]{1,0:T(8,128)(2,1)S(1)}, u32[]{:S(2)}, u32[]{:S(2)}) collective-permute-start(bf16[64,128]{1,0:T(8,128)(2,1)S(1)} %get-tuple-element.57), channel_id=1, source_target_pairs={{0,8},{8,0},{16,24},{24,16},{32,40},{40,32},{48,56},{56,48},{64,72... | collective-permute-start | bytes 49160 | tf_op jit(solution)/shard_map/ppermute | solution.py:22
  37.3 26.6 %collective-permute-start.3 = (bf16[128,1024]{1,0:T(8,128)(2,1)S(1)}, bf16[128,1024]{1,0:T(8,128)(2,1)S(1)}, u32[]{:S(2)}, u32[]{:S(2)}) collective-permute-start(bf16[128,1024]{1,0:T(8,128)(2,1)S(1)} %collective-permute-done.2.other_0), channel_id=1, source_target_pairs={{0,1},{1,2},{2,3},{3,0},{4,5},{5,6},{6,7},{7,4},{8,9},{9,10},{10,1... | collective-permute-start | bytes 786440 | tf_op jit(solution)/shard_map/ppermute | solution.py:52
  39.7 24.2 %collective-permute-start.4 = (bf16[128,1024]{1,0:T(8,128)(2,1)S(1)}, bf16[128,1024]{1,0:T(8,128)(2,1)S(1)}, u32[]{:S(2)}, u32[]{:S(2)}) collective-permute-start(bf16[128,1024]{1,0:T(8,128)(2,1)S(1)} %collective-permute-done.2.other_0), channel_id=1, source_target_pairs={{0,2},{1,3},{2,0},{3,1},{4,6},{5,7},{6,4},{7,5},{8,10},{9,11},{10,... | collective-permute-start | bytes 786440 | tf_op jit(solution)/shard_map/ppermute | solution.py:52
  43.2 20.7 %collective-permute-start.5 = (bf16[128,1024]{1,0:T(8,128)(2,1)S(1)}, bf16[128,1024]{1,0:T(8,128)(2,1)S(1)}, u32[]{:S(2)}, u32[]{:S(2)}) collective-permute-start(bf16[128,1024]{1,0:T(8,128)(2,1)S(1)} %collective-permute-done.2.other_0), channel_id=1, source_target_pairs={{0,3},{1,0},{2,1},{3,2},{4,7},{5,4},{6,5},{7,6},{8,11},{9,8},{10,9... | collective-permute-start | bytes 786440 | tf_op jit(solution)/shard_map/ppermute | solution.py:52
  46.3 17.7 %copy-start.8 = (bf16[1024,128]{1,0:T(8,128)(2,1)S(1)}, bf16[1024,128]{1,0:T(8,128)(2,1)}, u32[]{:S(2)}) copy-start(bf16[1024,128]{1,0:T(8,128)(2,1)} %key_weight.1) | copy-start | bytes 786436
  46.3 17.7 %copy-start.9 = (bf16[1024,128]{1,0:T(8,128)(2,1)S(1)}, bf16[1024,128]{1,0:T(8,128)(2,1)}, u32[]{:S(2)}) copy-start(bf16[1024,128]{1,0:T(8,128)(2,1)} %value_weight.1) | copy-start | bytes 786436
  48.1 29.6 %all-to-all-start.1 = ((f32[16,1,128]{2,1,0:T(1,128)}), f32[16,1,128]{2,1,0:T(1,128)S(1)}, u32[]{:S(2)}, u32[]{:S(2)}) async-start(f32[16,1,128]{2,1,0:T(1,128)} %bitcast.27), calls=%async_computation.1 | async-start | bytes 16384 | tf_op jit(solution)/shard_map/all_to_all | solution.py:398
  64.0 24.4 %copy-start.1 = (bf16[1,1024,128]{2,1,0:T(8,128)(2,1)S(1)}, bf16[1,1024,128]{2,1,0:T(8,128)(2,1)}, u32[]{:S(2)}) copy-start(bf16[1,1024,128]{2,1,0:T(8,128)(2,1)} %param.16) | copy-start | bytes 786436
  64.0 24.4 %copy-start.4 = (bf16[1,1024,128]{2,1,0:T(8,128)(2,1)S(1)}, bf16[1,1024,128]{2,1,0:T(8,128)(2,1)}, u32[]{:S(2)}) copy-start(bf16[1,1024,128]{2,1,0:T(8,128)(2,1)} %param.18) | copy-start | bytes 786436
  64.0 24.4 %copy-start.5 = (bf16[1,1024,128]{2,1,0:T(8,128)(2,1)S(1)}, bf16[1,1024,128]{2,1,0:T(8,128)(2,1)}, u32[]{:S(2)}) copy-start(bf16[1,1024,128]{2,1,0:T(8,128)(2,1)} %param.17) | copy-start | bytes 786436
  64.0 24.4 %copy-start.6 = (bf16[1,1024,128]{2,1,0:T(8,128)(2,1)S(1)}, bf16[1,1024,128]{2,1,0:T(8,128)(2,1)}, u32[]{:S(2)}) copy-start(bf16[1,1024,128]{2,1,0:T(8,128)(2,1)} %param.19) | copy-start | bytes 786436
  71.7 22.6 %collective-permute-start.6 = (f32[64,128]{1,0:T(8,128)S(1)}, f32[64,128]{1,0:T(8,128)S(1)}, u32[]{:S(2)}, u32[]{:S(2)}) collective-permute-start(f32[64,128]{1,0:T(8,128)S(1)} %get-tuple-element.41.kept), channel_id=1, source_target_pairs={{0,504},{8,16},{16,8},{24,32},{32,24},{40,48},{48,40},{56,64},{64,... | collective-permute-start | bytes 98312 | tf_op jit(solution)/shard_map/ppermute | solution.py:28
  78.3 17.5 %all-to-all-start.2 = ((f32[32,1,128]{2,1,0:T(1,128)}), f32[32,1,128]{2,1,0:T(1,128)S(1)}, u32[]{:S(2)}, u32[]{:S(2)}) async-start(f32[32,1,128]{2,1,0:T(1,128)} %broadcast_in_dim.33), calls=%async_computation.2 | async-start | bytes 32768 | tf_op jit(solution)/shard_map/all_to_all | solution.py:34
  88.4 1.0 copy-start.7
  89.3 4.0 %copy-start.11 = (f32[1,1024,128]{2,1,0:T(8,128)S(1)}, f32[1,1024,128]{2,1,0:T(8,128)}, u32[]{:S(2)}) copy-start(f32[1,1024,128]{2,1,0:T(8,128)} %param.13) | copy-start | bytes 1572868
  91.1 3.2 %collective-permute-start.7 = (f32[64,128]{1,0:T(8,128)S(1)}, f32[64,128]{1,0:T(8,128)S(1)}, u32[]{:S(2)}, u32[]{:S(2)}) collective-permute-start(f32[64,128]{1,0:T(8,128)S(1)} %get-tuple-element.41.kept), channel_id=1, source_target_pairs={{0,8},{8,0},{16,24},{24,16},{32,40},{40,32},{48,56},{56,48},{64,72... | collective-permute-start | bytes 98312 | tf_op jit(solution)/shard_map/ppermute | solution.py:22
